TPU v7x, 32 devices: a whole 2x2x4 slice. The times are simulated.
32 devices in a mesh: ctx: 8 (over z, y), fsdp: 4 (over x, core).
Axes of the slice: x: 2, y: 2, z: 4, core: 2. Of those that a mesh axis runs over, the one named last changes fastest.
Arguments:
- hidden_in: float32 [4, 2048, 1024], P('fsdp', 'ctx'), may hold values from -6 to 6
- starts: int32 [4, 8], P('fsdp'), may hold values from 0 to 2047, as said below
- w_query: float32 [1024, 1024], P('fsdp'), may hold values from -0.1875 to 0.1875
- w_key: float32 [1024, 1024], P('fsdp'), may hold values from -0.1875 to 0.1875
- w_value: float32 [1024, 1024], P('fsdp'), may hold values from -0.1875 to 0.1875
- w_output: float32 [1024, 1024], P('fsdp'), may hold values from -2 to 2
- w_expand: float32 [1024, 4096], P('fsdp'), may hold values from -0.1875 to 0.1875
- w_reduce: float32 [4096, 1024], P('fsdp'), may hold values from -0.09375 to 0.09375
- bias_query: float32 [1024], replicated, may hold values from -3 to 3
- bias_value: float32 [1024], replicated, may hold values from -0.12 to 0.12
- bias_output: float32 [1024], replicated, may hold values from -1.8 to 1.8
- bias_expand: float32 [4096], replicated, may hold values from -3 to 3
- bias_reduce: float32 [1024], replicated, may hold values from -1.8 to 1.8
- attention_gain: float32 [1024], replicated, may hold values from 0.5 to 1.5
- attention_shift: float32 [1024], replicated, may hold values from -1.8 to 1.8
- feedforward_gain: float32 [1024], replicated, may hold values from 0.5 to 1.5
- feedforward_shift: float32 [1024], replicated, may hold values from -1.8 to 1.8
- cotangent: float32 [4, 2048, 1024], P('fsdp', 'ctx'), may hold values from -6 to 6
Outputs:
- layer_out: float32 [4, 2048, 1024], P('fsdp', 'ctx')
- input_grad: float32 [4, 2048, 1024], P('fsdp', 'ctx')
- grad_w_query: float32 [1024, 1024], P('fsdp')
- grad_w_key: float32 [1024, 1024], P('fsdp')
- grad_w_value: float32 [1024, 1024], P('fsdp')
- grad_w_output: float32 [1024, 1024], P('fsdp')
- grad_w_expand: float32 [1024, 4096], P('fsdp')
- grad_w_reduce: float32 [4096, 1024], P('fsdp')
- grad_bias_query: float32 [1024], P('fsdp')
- grad_bias_value: float32 [1024], P('fsdp')
- grad_bias_output: float32 [1024], P('fsdp')
- grad_bias_expand: float32 [4096], P('fsdp')
- grad_bias_reduce: float32 [1024], P('fsdp')
- grad_attention_gain: float32 [1024], P('fsdp')
- grad_attention_shift: float32 [1024], P('fsdp')
- grad_feedforward_gain: float32 [1024], P('fsdp')
- grad_feedforward_shift: float32 [1024], P('fsdp')
Inputs may be any that keep to these rules, and one draw needn't show every extreme that they name: Row s holds the first tokens of the documents of stream s, not decreasing, the first one 0; equal starts mark empty documents. One document of each stream has tokens among the first 256 and among the last 256 tokens of the stream.
All inputs are finite; a program needn't handle non-finite values.
Results may differ from a plain program's by a relative error of at most 0.023.
Values may be sent and summed in bfloat16 or wider, within the bound.
No kernel may reach another device: no remote copies, remote signals or barrier semaphores. Data moves between devices by JAX's collectives and lax.ppermute only.
A program may use at most 384 MiB of HBM per device.

v0:
```python
import math

import jax
import jax.numpy as jnp
from jax import lax
from jax.sharding import PartitionSpec as P

HEADS = 16


epsilon = 1e-05
masked_value = -1e30
query_scale = 0.125


def layer_norm(values, gain_vector, shift_vector):
    average = jnp.mean(values, axis=-1, keepdims=True)
    centered = values - average
    variance = jnp.mean(centered * centered, axis=-1, keepdims=True)
    return centered * lax.rsqrt(variance + epsilon) * gain_vector + shift_vector


def exact_gelu(values):
    return jax.nn.gelu(values, approximate=False)


def document_ids(starts_row, offset, row_count):
    positions = offset + lax.iota(jnp.int32, row_count)
    return jnp.sum((starts_row[None, :] <= positions[:, None]).astype(jnp.int32), axis=1) - 1


def matmul(left, right):
    return jnp.dot(left, right, preferred_element_type=jnp.float32)


def left_transposed(left, right):
    return lax.dot_general(
        left, right, (((0,), (0,)), ((), ())), preferred_element_type=jnp.float32
    )


def right_transposed(left, right):
    return lax.dot_general(
        left, right, (((1,), (1,)), ((), ())), preferred_element_type=jnp.float32
    )


def column_sum(rounded_rows):
    return jnp.sum(rounded_rows.astype(jnp.float32), axis=0)


def attend_block(carried, query_heads, query_docs, key_block, value_block, key_docs):
    accumulated, running_max, running_sum = carried
    scores = jnp.einsum("qhd,khd->qhk", query_heads, key_block, preferred_element_type=jnp.float32)
    allowed = (query_docs[:, None] == key_docs[None, :])[:, None, :]
    block_max = jnp.max(jnp.where(allowed, scores, masked_value), axis=-1)
    new_max = jnp.maximum(running_max, block_max)
    weights = jnp.exp(jnp.where(allowed, scores - new_max[..., None], masked_value))
    factor = jnp.exp(running_max - new_max)
    running_sum = running_sum * factor + jnp.sum(weights, axis=-1)
    accumulated = accumulated * factor[..., None] + jnp.einsum(
        "qhk,khd->qhd",
        weights.astype(jnp.bfloat16),
        value_block,
        preferred_element_type=jnp.float32,
    )
    return (accumulated, new_max, running_sum)


def pair_grads(
    query_heads, dout_heads, log_total, row_delta, query_docs, key_heads, value_heads, key_docs
):
    scores = jnp.einsum("qhd,khd->qhk", query_heads, key_heads, preferred_element_type=jnp.float32)
    allowed = (query_docs[:, None] == key_docs[None, :])[:, None, :]
    probabilities = jnp.exp(jnp.where(allowed, scores - log_total[..., None], masked_value))
    grad_probs = jnp.einsum(
        "qhd,khd->qhk", dout_heads, value_heads, preferred_element_type=jnp.float32
    )
    grad_scores = (probabilities * (grad_probs - row_delta[..., None])).astype(jnp.bfloat16)
    rounded_probs = probabilities.astype(jnp.bfloat16)
    grad_query_part = jnp.einsum(
        "qhk,khd->qhd", grad_scores, key_heads, preferred_element_type=jnp.float32
    )
    grad_key_part = jnp.einsum(
        "qhk,qhd->khd", grad_scores, query_heads, preferred_element_type=jnp.float32
    )
    grad_value_part = jnp.einsum(
        "qhk,qhd->khd", rounded_probs, dout_heads, preferred_element_type=jnp.float32
    )
    return (grad_query_part, grad_key_part, grad_value_part)


def per_device(
    hidden_in,
    starts,
    w_query,
    w_key,
    w_value,
    w_output,
    w_expand,
    w_reduce,
    bias_query,
    bias_value,
    bias_output,
    bias_expand,
    bias_reduce,
    attention_gain,
    attention_shift,
    feedforward_gain,
    feedforward_shift,
    cotangent,
):
    tokens = hidden_in.shape[1]
    model_width = hidden_in.shape[2]
    head_count = HEADS
    head_size = model_width // head_count
    stream_length = tokens * lax.axis_size("ctx")
    offset = lax.axis_index("ctx") * tokens
    starts_row = starts[0]
    query_docs = document_ids(starts_row, offset, tokens)
    query_matrix, key_matrix, value_matrix, output_matrix, expand_matrix, reduce_matrix = (
        lax.all_gather(w_query.astype(jnp.bfloat16), "fsdp", axis=0, tiled=True),
        lax.all_gather(w_key.astype(jnp.bfloat16), "fsdp", axis=0, tiled=True),
        lax.all_gather(w_value.astype(jnp.bfloat16), "fsdp", axis=0, tiled=True),
        lax.all_gather(w_output.astype(jnp.bfloat16), "fsdp", axis=0, tiled=True),
        lax.all_gather(w_expand.astype(jnp.bfloat16), "fsdp", axis=0, tiled=True),
        lax.all_gather(w_reduce.astype(jnp.bfloat16), "fsdp", axis=0, tiled=True),
    )
    inputs = hidden_in[0]
    inputs_r = inputs.astype(jnp.bfloat16)
    queries = ((matmul(inputs_r, query_matrix) + bias_query) * query_scale).astype(jnp.bfloat16)
    keys_r = matmul(inputs_r, key_matrix).astype(jnp.bfloat16)
    values_r = (matmul(inputs_r, value_matrix) + bias_value).astype(jnp.bfloat16)
    query_heads = queries.reshape(tokens, head_count, head_size)
    initial = (
        jnp.zeros((tokens, head_count, head_size), jnp.float32),
        jnp.full((tokens, head_count), masked_value, jnp.float32),
        jnp.zeros((tokens, head_count), jnp.float32),
    )
    key_piece = lax.all_gather(keys_r, "ctx", axis=0, tiled=True)
    value_piece = lax.all_gather(values_r, "ctx", axis=0, tiled=True)
    piece_rows = key_piece.shape[0]
    block_rows = math.gcd(piece_rows, 512)

    def forward_step(step_index, inner):
        row_start = step_index * block_rows
        key_block = lax.dynamic_slice_in_dim(key_piece, row_start, block_rows, 0).reshape(
            block_rows, head_count, head_size
        )
        value_block = lax.dynamic_slice_in_dim(value_piece, row_start, block_rows, 0).reshape(
            block_rows, head_count, head_size
        )
        key_docs = document_ids(starts_row, row_start, block_rows)
        return attend_block(inner, query_heads, query_docs, key_block, value_block, key_docs)

    accumulated, running_max, running_sum = lax.fori_loop(
        0, piece_rows // block_rows, forward_step, initial
    )
    attended = accumulated / running_sum[..., None]
    log_total = running_max + jnp.log(running_sum)
    attended_r = attended.reshape(tokens, model_width).astype(jnp.bfloat16)
    attention_out = matmul(attended_r, output_matrix) + bias_output
    normed, first_norm_back = jax.vjp(
        layer_norm, inputs + attention_out, attention_gain, attention_shift
    )
    normed_r = normed.astype(jnp.bfloat16)
    expanded = matmul(normed_r, expand_matrix) + bias_expand
    activated, gelu_back = jax.vjp(exact_gelu, expanded)
    activated_r = activated.astype(jnp.bfloat16)
    reduced = matmul(activated_r, reduce_matrix) + bias_reduce
    layer_out, second_norm_back = jax.vjp(
        layer_norm, normed + reduced, feedforward_gain, feedforward_shift
    )
    query_matrix, key_matrix, value_matrix, output_matrix, expand_matrix, reduce_matrix = (
        lax.all_gather(w_query.astype(jnp.bfloat16), "fsdp", axis=0, tiled=True),
        lax.all_gather(w_key.astype(jnp.bfloat16), "fsdp", axis=0, tiled=True),
        lax.all_gather(w_value.astype(jnp.bfloat16), "fsdp", axis=0, tiled=True),
        lax.all_gather(w_output.astype(jnp.bfloat16), "fsdp", axis=0, tiled=True),
        lax.all_gather(w_expand.astype(jnp.bfloat16), "fsdp", axis=0, tiled=True),
        lax.all_gather(w_reduce.astype(jnp.bfloat16), "fsdp", axis=0, tiled=True),
    )
    d_second, grad_ff_gain, grad_ff_shift = second_norm_back(cotangent[0])
    d_reduced_r = d_second.astype(jnp.bfloat16)
    grad_reduce = left_transposed(activated_r, d_reduced_r)
    grad_bias_reduce = column_sum(d_reduced_r)
    (d_expanded,) = gelu_back(right_transposed(d_reduced_r, reduce_matrix))
    d_expanded_r = d_expanded.astype(jnp.bfloat16)
    grad_expand = left_transposed(normed_r, d_expanded_r)
    grad_bias_expand = column_sum(d_expanded_r)
    d_normed = d_second + right_transposed(d_expanded_r, expand_matrix)
    d_first, grad_att_gain, grad_att_shift = first_norm_back(d_normed)
    d_attention_r = d_first.astype(jnp.bfloat16)
    grad_output = left_transposed(attended_r, d_attention_r)
    grad_bias_output = column_sum(d_attention_r)
    d_attended_r = right_transposed(d_attention_r, output_matrix).astype(jnp.bfloat16)
    dout_heads = d_attended_r.reshape(tokens, head_count, head_size)
    row_delta = jnp.sum(dout_heads.astype(jnp.float32) * attended, axis=-1)
    zero_heads = jnp.zeros((tokens, head_count, head_size), jnp.float32)
    start_state = (zero_heads, jnp.zeros((stream_length, 2 * model_width), jnp.float32))
    partial_key_piece = lax.all_gather(keys_r, "ctx", axis=0, tiled=True)
    partial_value_piece = lax.all_gather(values_r, "ctx", axis=0, tiled=True)
    piece_rows = partial_key_piece.shape[0]
    partial_block_rows = math.gcd(piece_rows, 512)

    def partial_step(step_index, inner):
        grad_queries, grad_rows = inner
        row_start = step_index * partial_block_rows
        key_block = lax.dynamic_slice_in_dim(
            partial_key_piece, row_start, partial_block_rows, 0
        ).reshape(partial_block_rows, head_count, head_size)
        value_block = lax.dynamic_slice_in_dim(
            partial_value_piece, row_start, partial_block_rows, 0
        ).reshape(partial_block_rows, head_count, head_size)
        key_docs = document_ids(starts_row, row_start, partial_block_rows)
        grad_query_part, grad_key_part, grad_value_part = pair_grads(
            query_heads,
            dout_heads,
            log_total,
            row_delta,
            query_docs,
            key_block,
            value_block,
            key_docs,
        )
        update = jnp.concatenate(
            (
                grad_key_part.reshape(partial_block_rows, model_width),
                grad_value_part.reshape(partial_block_rows, model_width),
            ),
            axis=1,
        )
        current = lax.dynamic_slice_in_dim(grad_rows, row_start, partial_block_rows, 0)
        grad_rows = lax.dynamic_update_slice_in_dim(grad_rows, current + update, row_start, 0)
        return (grad_queries + grad_query_part, grad_rows)

    grad_queries, grad_rows = lax.fori_loop(
        0, piece_rows // partial_block_rows, partial_step, start_state
    )
    own_rows = lax.psum_scatter(
        grad_rows.astype(jnp.bfloat16), "ctx", scatter_dimension=0, tiled=True
    ).astype(jnp.float32)
    d_keys_r = own_rows[:, :model_width].astype(jnp.bfloat16)
    d_values_r = own_rows[:, model_width:].astype(jnp.bfloat16)
    d_queries_r = grad_queries.reshape(tokens, model_width).astype(jnp.bfloat16)
    grad_query = query_scale * left_transposed(inputs_r, d_queries_r)
    grad_bias_query = query_scale * column_sum(d_queries_r)
    grad_key = left_transposed(inputs_r, d_keys_r)
    grad_value = left_transposed(inputs_r, d_values_r)
    grad_bias_value = column_sum(d_values_r)
    input_grad = (
        d_first
        + query_scale * right_transposed(d_queries_r, query_matrix)
        + right_transposed(d_keys_r, key_matrix)
        + right_transposed(d_values_r, value_matrix)
    )
    (
        shard_query,
        shard_key,
        shard_value,
        shard_output,
        shard_expand,
        shard_reduce,
        shard_bias_query,
        shard_bias_value,
        shard_bias_output,
        shard_bias_expand,
        shard_bias_reduce,
        shard_att_gain,
        shard_att_shift,
        shard_ff_gain,
        shard_ff_shift,
    ) = (
        lax.psum_scatter(
            grad_query.astype(jnp.bfloat16), "fsdp", scatter_dimension=0, tiled=True
        ).astype(jnp.float32),
        lax.psum_scatter(
            grad_key.astype(jnp.bfloat16), "fsdp", scatter_dimension=0, tiled=True
        ).astype(jnp.float32),
        lax.psum_scatter(
            grad_value.astype(jnp.bfloat16), "fsdp", scatter_dimension=0, tiled=True
        ).astype(jnp.float32),
        lax.psum_scatter(
            grad_output.astype(jnp.bfloat16), "fsdp", scatter_dimension=0, tiled=True
        ).astype(jnp.float32),
        lax.psum_scatter(
            grad_expand.astype(jnp.bfloat16), "fsdp", scatter_dimension=0, tiled=True
        ).astype(jnp.float32),
        lax.psum_scatter(
            grad_reduce.astype(jnp.bfloat16), "fsdp", scatter_dimension=0, tiled=True
        ).astype(jnp.float32),
        lax.psum_scatter(
            grad_bias_query.astype(jnp.bfloat16), "fsdp", scatter_dimension=0, tiled=True
        ).astype(jnp.float32),
        lax.psum_scatter(
            grad_bias_value.astype(jnp.bfloat16), "fsdp", scatter_dimension=0, tiled=True
        ).astype(jnp.float32),
        lax.psum_scatter(
            grad_bias_output.astype(jnp.bfloat16), "fsdp", scatter_dimension=0, tiled=True
        ).astype(jnp.float32),
        lax.psum_scatter(
            grad_bias_expand.astype(jnp.bfloat16), "fsdp", scatter_dimension=0, tiled=True
        ).astype(jnp.float32),
        lax.psum_scatter(
            grad_bias_reduce.astype(jnp.bfloat16), "fsdp", scatter_dimension=0, tiled=True
        ).astype(jnp.float32),
        lax.psum_scatter(
            grad_att_gain.astype(jnp.bfloat16), "fsdp", scatter_dimension=0, tiled=True
        ).astype(jnp.float32),
        lax.psum_scatter(
            grad_att_shift.astype(jnp.bfloat16), "fsdp", scatter_dimension=0, tiled=True
        ).astype(jnp.float32),
        lax.psum_scatter(
            grad_ff_gain.astype(jnp.bfloat16), "fsdp", scatter_dimension=0, tiled=True
        ).astype(jnp.float32),
        lax.psum_scatter(
            grad_ff_shift.astype(jnp.bfloat16), "fsdp", scatter_dimension=0, tiled=True
        ).astype(jnp.float32),
    )
    totals = (
        lax.psum(shard_query.astype(jnp.bfloat16), "ctx").astype(jnp.float32),
        lax.psum(shard_key.astype(jnp.bfloat16), "ctx").astype(jnp.float32),
        lax.psum(shard_value.astype(jnp.bfloat16), "ctx").astype(jnp.float32),
        lax.psum(shard_output.astype(jnp.bfloat16), "ctx").astype(jnp.float32),
        lax.psum(shard_expand.astype(jnp.bfloat16), "ctx").astype(jnp.float32),
        lax.psum(shard_reduce.astype(jnp.bfloat16), "ctx").astype(jnp.float32),
        lax.psum(shard_bias_query.astype(jnp.bfloat16), "ctx").astype(jnp.float32),
        lax.psum(shard_bias_value.astype(jnp.bfloat16), "ctx").astype(jnp.float32),
        lax.psum(shard_bias_output.astype(jnp.bfloat16), "ctx").astype(jnp.float32),
        lax.psum(shard_bias_expand.astype(jnp.bfloat16), "ctx").astype(jnp.float32),
        lax.psum(shard_bias_reduce.astype(jnp.bfloat16), "ctx").astype(jnp.float32),
        lax.psum(shard_att_gain.astype(jnp.bfloat16), "ctx").astype(jnp.float32),
        lax.psum(shard_att_shift.astype(jnp.bfloat16), "ctx").astype(jnp.float32),
        lax.psum(shard_ff_gain.astype(jnp.bfloat16), "ctx").astype(jnp.float32),
        lax.psum(shard_ff_shift.astype(jnp.bfloat16), "ctx").astype(jnp.float32),
    )
    return (
        layer_out[None],
        input_grad[None],
        totals[0],
        totals[1],
        totals[2],
        totals[3],
        totals[4],
        totals[5],
        totals[6],
        totals[7],
        totals[8],
        totals[9],
        totals[10],
        totals[11],
        totals[12],
        totals[13],
        totals[14],
    )


def solution(mesh):
    return jax.shard_map(
        per_device,
        mesh=mesh,
        in_specs=(
            P("fsdp", "ctx", None),
            P("fsdp", None),
            P("fsdp", None),
            P("fsdp", None),
            P("fsdp", None),
            P("fsdp", None),
            P("fsdp", None),
            P("fsdp", None),
            P(),
            P(),
            P(),
            P(),
            P(),
            P(),
            P(),
            P(),
            P(),
            P("fsdp", "ctx", None),
        ),
        out_specs=(
            P("fsdp", "ctx", None),
            P("fsdp", "ctx", None),
            P("fsdp", None),
            P("fsdp", None),
            P("fsdp", None),
            P("fsdp", None),
            P("fsdp", None),
            P("fsdp", None),
            P("fsdp"),
            P("fsdp"),
            P("fsdp"),
            P("fsdp"),
            P("fsdp"),
            P("fsdp"),
            P("fsdp"),
            P("fsdp"),
            P("fsdp"),
        ),
        check_vma=False,
    )
```

profile of v0, /device:TPU:0, one launch (start us, length us, event | category | flops | bytes accessed | tf_op | source)
XLA Modules:
  0.0 1164.1 jit_solution(17779362235741043624)
XLA Ops:
  12.8 22.7 %all-gather.9.cloned.1.call-done = bf16[1024,1024]{1,0:T(8,128)(2,1)} async-done(((bf16[256,1024]{1,0:T(8,128)(2,1)}), bf16[1024,1024]{1,0:T(8,128)(2,1)}) %all-gather.9.cloned.1.call-update) | async-done | bytes 2097168 | tf_op jit(solution)/shard_map/all_gather | solution.py:123
  35.5 3.1 convolution_convert_fusion.4
  38.7 21.6 %all-gather.15.cloned.1.call-done = bf16[1024,1024]{1,0:T(8,128)(2,1)} async-done(((bf16[256,1024]{1,0:T(8,128)(2,1)}), bf16[1024,1024]{1,0:T(8,128)(2,1)}) %all-gather.15.cloned.1.call-update) | async-done | bytes 2097168 | tf_op jit(solution)/shard_map/all_gather | solution.py:124
  60.3 3.1 fusion.44
  64.4 3.8 convert_element_type.279
  68.3 4.1 convert_element_type.281
  72.6 12.4 %all-gather.13.cloned.1.call-done = bf16[1024,1024]{1,0:T(8,128)(2,1)} async-done(((bf16[256,1024]{1,0:T(8,128)(2,1)}), bf16[1024,1024]{1,0:T(8,128)(2,1)}) %all-gather.13.cloned.1.call-update) | async-done | bytes 2097168 | tf_op jit(solution)/shard_map/all_gather | solution.py:122
  87.5 73.5 %all-gather.11.cloned.1.call-done = bf16[2048,1024]{1,0:T(8,128)(2,1)} async-done(((bf16[256,1024]{1,0:T(8,128)(2,1)}), bf16[2048,1024]{1,0:T(8,128)(2,1)}) %all-gather.11.cloned.1.call-update) | async-done | bytes 4194320 | tf_op jit(solution)/shard_map/all_gather | solution.py:140
  161.0 6.4 copy.81
  167.4 67.8 %all-gather.17.cloned.1.call-done = bf16[2048,1024]{1,0:T(8,128)(2,1)} async-done(((bf16[256,1024]{1,0:T(8,128)(2,1)}), bf16[2048,1024]{1,0:T(8,128)(2,1)}) %all-gather.17.cloned.1.call-update) | async-done | bytes 4194320 | tf_op jit(solution)/shard_map/all_gather | solution.py:141
  235.3 6.4 copy.82
  241.7 27.7 %while.38 = (s32[]{:T(128)}, f32[256,16,64]{0,2,1:T(8,128)S(1)}, f32[256,16]{0,1:T(8,128)S(1)}, f32[256,16]{0,1:T(8,128)S(1)}, s32[256]{0:T(256)S(1)}, /*index=5...) while((s32[]{:T(128)}, f32[256,16,64]{0,2,1:T(8,128)S(1)}, ...), condition=%wide.region_5.6_spmd.clone, body=%wide.region_1.5_spmd.clone.sunk | while | flops 554598912 | bytes 34878692 | solution.py:156
  269.6 3.7 fusion.64
  274.6 43.5 %all-gather.21.cloned.1.call-done = bf16[1024,4096]{1,0:T(8,128)(2,1)} async-done(((bf16[256,4096]{1,0:T(8,128)(2,1)}), bf16[1024,4096]{1,0:T(8,128)(2,1)}) %all-gather.21.cloned.1.call-update) | async-done | bytes 8388624 | tf_op jit(solution)/shard_map/all_gather | solution.py:126
  318.0 16.8 %multiply_convert_fusion.1 = (bf16[256,4096]{1,0:T(8,128)(2,1)}, f32[256,4096]{1,0:T(8,128)}, f32[256,4096]{1,0:T(8,128)}) fusion(f32[4096]{0:T(1024)S(1)} %copy-done.34, bf16[1024,4096]{1,0:T(8,128)(2,1)} %all-gather.21.cloned.1.call-done, f32[256,1024]{1,0:T(8,128)} %copy-done, f32[1024]{0:T(1024)S(1)} %copy-done.29, f32[1024]{0:T(1024)S(1)} %copy-done.28, ...), kind=kOutput, calls=%fused_computation.54 | convolution fusion | flops 2218000384 | bytes 19949568 | tf_op jit(solution)/shard_map/dot_general | solution.py:33
  334.8 43.1 %all-gather.23.cloned.1.call-done = bf16[4096,1024]{1,0:T(8,128)(2,1)} async-done(((bf16[1024,1024]{1,0:T(8,128)(2,1)}), bf16[4096,1024]{1,0:T(8,128)(2,1)}) %all-gather.23.cloned.1.call-update) | async-done | bytes 8388624 | tf_op jit(solution)/shard_map/all_gather | solution.py:127
  377.9 6.8 fusion.65
  387.5 11.1 fusion.59
  398.6 6.9 multiply_reduce_fusion
  410.6 7.9 broadcast_in_dim.151
  418.5 60.4 %while.39 = (s32[]{:T(128)}, f32[256,16,64]{0,2,1:T(8,128)S(1)}, f32[2048,2048]{0,1:T(8,128)}, bf16[2048,1024]{0,1:T(8,128)(2,1)}, s32[256]{0:T(256)S(1)}, /*ind...) while((s32[]{:T(128)}, f32[256,16,64]{0,2,1:T(8,128)S(1)}, ...), condition=%wide.region_17.18_spmd.clone, body=%wide.region_15.0_spmd.clone.sunk | while | flops 1361719808 | bytes 66516216 | solution.py:236
  423.7 2.5 fusion.152
  428.5 5.2 fusion.156
  438.7 2.5 fusion.152
  443.5 5.2 fusion.156
  453.8 2.5 fusion.152
  458.6 5.2 fusion.156
  468.9 2.5 fusion.152
  473.6 5.2 fusion.156
  478.8 9.1 convert_element_type.289
  494.4 7.9 convolution_convert_fusion.1
  504.1 5.6 convolution_convert_fusion
  509.8 127.7 %reduce-scatter.8.cloned.1.call-done = bf16[256,2048]{0,1:T(8,128)(2,1)} async-done(((bf16[2048,2048]{0,1:T(8,128)(2,1)}), bf16[256,2048]{0,1:T(8,128)(2,1)}) %reduce-scatter.8.cloned.1.call-update) | async-done | bytes 1048592 | tf_op jit(solution)/shard_map/reduce_scatter | solution.py:239
  637.5 3.2 convert_bitcast_fusion
  642.9 27.6 %reduce-scatter.16.cloned.1.call-done = bf16[256,1024]{1,0:T(8,128)(2,1)} async-done(((bf16[1024,1024]{1,0:T(8,128)(2,1)}), bf16[256,1024]{1,0:T(8,128)(2,1)}) %reduce-scatter.16.cloned.1.call-update) | async-done | bytes 524304 | tf_op jit(solution)/shard_map/reduce_scatter | solution.py:282
  670.5 34.6 %reduce-scatter.10.cloned.1.call-done = bf16[256,1024]{0,1:T(8,128)(2,1)} async-done(((bf16[1024,1024]{0,1:T(8,128)(2,1)}), bf16[256,1024]{0,1:T(8,128)(2,1)}) %reduce-scatter.10.cloned.1.call-update) | async-done | bytes 524304 | tf_op jit(solution)/shard_map/reduce_scatter | solution.py:273
  705.1 74.4 %reduce-scatter.18.cloned.1.call-done = bf16[256,4096]{1,0:T(8,128)(2,1)} async-done(((bf16[1024,4096]{1,0:T(8,128)(2,1)}), bf16[256,4096]{1,0:T(8,128)(2,1)}) %reduce-scatter.18.cloned.1.call-update) | async-done | bytes 2097168 | tf_op jit(solution)/shard_map/reduce_scatter | solution.py:285
  779.4 74.4 %reduce-scatter.20.cloned.1.call-done = bf16[1024,1024]{1,0:T(8,128)(2,1)} async-done(((bf16[4096,1024]{1,0:T(8,128)(2,1)}), bf16[1024,1024]{1,0:T(8,128)(2,1)}) %reduce-scatter.20.cloned.1.call-update) | async-done | bytes 2097168 | tf_op jit(solution)/shard_map/reduce_scatter | solution.py:288
  853.8 34.0 %reduce-scatter.14.cloned.1.call-done = bf16[256,1024]{0,1:T(8,128)(2,1)} async-done(((bf16[1024,1024]{0,1:T(8,128)(2,1)}), bf16[256,1024]{0,1:T(8,128)(2,1)}) %reduce-scatter.14.cloned.1.call-update) | async-done | bytes 524304 | tf_op jit(solution)/shard_map/reduce_scatter | solution.py:279
  887.8 34.4 %reduce-scatter.12.cloned.1.call-done = bf16[256,1024]{0,1:T(8,128)(2,1)} async-done(((bf16[1024,1024]{0,1:T(8,128)(2,1)}), bf16[256,1024]{0,1:T(8,128)(2,1)}) %reduce-scatter.12.cloned.1.call-update) | async-done | bytes 524304 | tf_op jit(solution)/shard_map/reduce_scatter | solution.py:276
  924.4 2.5 fusion.39
  927.1 10.3 all-reduce.11
  938.0 23.7 %all-reduce.9 = (bf16[256]{0:T(256)(128)(2,1)S(1)}, bf16[256]{0:T(256)(128)(2,1)S(1)}, bf16[256]{0:T(256)(128)(2,1)S(1)}, bf16[1024]{0:T(1024)(128)(2,1)S(1)}, b...) all-reduce(bf16[256]{0:T(256)(128)(2,1)S(1)} %dynamic-slice.1, ...), channel_id=1, replica_groups=mesh['ctx'=8,'fsdp'=4] {'ctx'}, use_global_device_ids=true, to_apply=%region_33.34 | all-reduce | flops 3072 | bytes 12288 | tf_op jit(solution)/shard_map/psum | solution.py:326
  966.9 2.5 convolution_add_fusion.2
  971.1 173.4 %all-reduce.14.cloned.1.call-done = (bf16[256,1024]{0,1:T(8,128)(2,1)}, bf16[256,1024]{0,1:T(8,128)(2,1)}, bf16[256,1024]{0,1:T(8,128)(2,1)}, bf16[256,1024]{1,0...) async-done(((bf16[256,1024]{0,1:T(8,128)(2,1)}, bf16[256,1024]{0,1:T(8,128)(2,1)}, bf16[256,1024]{0,1:T(8,128)(2,1)}, bf16[256,1024]{1,0:T(8,128)(2,1)}, ...) | async-done | bytes 6291472 | tf_op jit(solution)/shard_map/psum | solution.py:320
  1144.5 2.4 copy.86
  1152.4 2.5 convert_element_type.304
  1154.9 2.5 convert_element_type.306
  (258 shorter events, 99.3 us)
Async XLA Ops:
  7.2 4.5 copy-start.25
  7.2 5.5 copy-start.7
  7.2 28.3 %all-gather.9.cloned.1.call-start = ((), (), s32[]{:S(2)}) async-start(), calls=%async_computation.7 | async-start | bytes 2621440 | tf_op jit(solution)/shard_map/all_gather | solution.py:123
  9.5 50.7 %all-gather.15.cloned.1.call-start = ((), (), s32[]{:S(2)}) async-start(), calls=%async_computation.10 | async-start | bytes 2621440 | tf_op jit(solution)/shard_map/all_gather | solution.py:124
  11.7 48.6 %copy-start.35 = (f32[1024]{0:T(1024)S(1)}, f32[1024]{0:T(1024)}, u32[]{:S(2)}) copy-start(f32[1024]{0:T(1024)} %param.31) | copy-start | bytes 12292
  11.7 73.3 %all-gather.13.cloned.1.call-start = ((), (), s32[]{:S(2)}) async-start(), calls=%async_computation.9 | async-start | bytes 2621440 | tf_op jit(solution)/shard_map/all_gather | solution.py:122
  12.6 148.4 %all-gather.11.cloned.1.call-start = ((), (), s32[]{:S(2)}) async-start(), calls=%async_computation.8 | async-start | bytes 4718592 | tf_op jit(solution)/shard_map/all_gather | solution.py:140
  12.8 72.2 %copy-start.11 = (bf16[256,1024]{1,0:T(8,128)(2,1)}, bf16[256,1024]{1,0:T(8,128)(2,1)S(1)}, u32[]{:S(2)}) copy-start(bf16[256,1024]{1,0:T(8,128)(2,1)S(1)} %bitcast_convert_fusion) | copy-start | bytes 1572868
  12.8 50.6 %copy-start.26 = (f32[256,1024]{1,0:T(8,128)S(1)}, f32[256,1024]{1,0:T(8,128)}, u32[]{:S(2)}) copy-start(f32[256,1024]{1,0:T(8,128)} %param.27) | copy-start | bytes 3145732
  38.6 196.6 %all-gather.17.cloned.1.call-start = ((), (), s32[]{:S(2)}) async-start(), calls=%async_computation.11 | async-start | bytes 4718592 | tf_op jit(solution)/shard_map/all_gather | solution.py:141
  63.4 206.2 %all-gather.19.cloned.1.call-start = ((), (), s32[]{:S(2)}) async-start(), calls=%async_computation.12 | async-start | bytes 2621440 | tf_op jit(solution)/shard_map/all_gather | solution.py:125
  64.3 253.7 %all-gather.21.cloned.1.call-start = ((), (), s32[]{:S(2)}) async-start(), calls=%async_computation.13 | async-start | bytes 10485760 | tf_op jit(solution)/shard_map/all_gather | solution.py:126
  68.2 4.4 copy-start.30
  68.2 16.8 %copy-start.36 = (f32[1024]{0:T(1024)S(1)}, f32[1024]{0:T(1024)}, u32[]{:S(2)}) copy-start(f32[1024]{0:T(1024)} %param.30) | copy-start | bytes 12292
  68.2 309.7 %all-gather.23.cloned.1.call-start = ((), (), s32[]{:S(2)}) async-start(), calls=%async_computation.14 | async-start | bytes 10485760 | tf_op jit(solution)/shard_map/all_gather | solution.py:127
  72.4 565.1 %reduce-scatter.8.cloned.1.call-start = ((), (), s32[]{:S(2)}) async-start(), calls=%async_computation.15 | async-start | bytes 9437184 | tf_op jit(solution)/shard_map/reduce_scatter | solution.py:239
  241.7 27.9 %copy-start.32 = (f32[1024]{0:T(1024)S(1)}, f32[1024]{0:T(1024)}, u32[]{:S(2)}) copy-start(f32[1024]{0:T(1024)} %param.32) | copy-start | bytes 12292
  269.3 48.7 %copy-start.28 = (f32[1024]{0:T(1024)S(1)}, f32[1024]{0:T(1024)}, u32[]{:S(2)}) copy-start(f32[1024]{0:T(1024)} %param.35) | copy-start | bytes 12292
  269.4 48.7 %copy-start.29 = (f32[1024]{0:T(1024)S(1)}, f32[1024]{0:T(1024)}, u32[]{:S(2)}) copy-start(f32[1024]{0:T(1024)} %param.36) | copy-start | bytes 12292
  269.4 48.6 %copy-start.34 = (f32[4096]{0:T(1024)S(1)}, f32[4096]{0:T(1024)}, u32[]{:S(2)}) copy-start(f32[4096]{0:T(1024)} %param.33) | copy-start | bytes 49156
  269.5 65.3 %copy-start.13 = (bf16[256,16,64]{0,2,1:T(8,128)(2,1)}, bf16[256,16,64]{0,2,1:T(8,128)(2,1)S(1)}, u32[]{:S(2)}) copy-start(bf16[256,16,64]{0,2,1:T(8,128)(2,1)S(1)} %fusion.51) | copy-start | bytes 1572868
  274.5 103.3 %copy-start.37 = (f32[1024]{0:T(1024)S(1)}, f32[1024]{0:T(1024)}, u32[]{:S(2)}) copy-start(f32[1024]{0:T(1024)} %param.34) | copy-start | bytes 12292
  377.9 7.1 copy-start.5
  377.9 7.1 copy-start.31
  377.9 7.5 copy-start.33
  384.9 2.6 copy-start.39
  387.0 11.6 copy-start.16
  387.5 11.1 copy-start.1
  398.6 6.9 copy-start.18
  405.5 2.0 copy-start.22
  487.9 4.4 copy-start.8
  487.9 182.6 %reduce-scatter.16.cloned.1.call-start = ((), (), s32[]{:S(2)}) async-start(), calls=%async_computation.19 | async-start | bytes 2621440 | tf_op jit(solution)/shard_map/reduce_scatter | solution.py:282
  491.2 3.2 copy-start.2
  491.2 213.9 %reduce-scatter.10.cloned.1.call-start = ((), (), s32[]{:S(2)}) async-start(), calls=%async_computation.16 | async-start | bytes 2621440 | tf_op jit(solution)/shard_map/reduce_scatter | solution.py:273
  494.4 285.1 %reduce-scatter.18.cloned.1.call-start = ((), (), s32[]{:S(2)}) async-start(), calls=%async_computation.20 | async-start | bytes 10485760 | tf_op jit(solution)/shard_map/reduce_scatter | solution.py:285
  502.4 351.4 %reduce-scatter.20.cloned.1.call-start = ((), (), s32[]{:S(2)}) async-start(), calls=%async_computation.21 | async-start | bytes 10485760 | tf_op jit(solution)/shard_map/reduce_scatter | solution.py:288
  509.7 127.8 %copy-start.12 = (bf16[256,1024]{1,0:T(8,128)(2,1)S(1)}, bf16[256,1024]{1,0:T(8,128)(2,1)}, u32[]{:S(2)}) copy-start(bf16[256,1024]{1,0:T(8,128)(2,1)} %copy-done.11) | copy-start | bytes 1572868
  509.7 378.1 %reduce-scatter.14.cloned.1.call-start = ((), (), s32[]{:S(2)}) async-start(), calls=%async_computation.18 | async-start | bytes 2621440 | tf_op jit(solution)/shard_map/reduce_scatter | solution.py:279
  637.5 3.3 copy-start.9
  640.7 281.5 %reduce-scatter.12.cloned.1.call-start = ((), (), s32[]{:S(2)}) async-start(), calls=%async_computation.17 | async-start | bytes 2621440 | tf_op jit(solution)/shard_map/reduce_scatter | solution.py:276
  642.8 279.5 %copy-start.6 = (f32[1,256,1024]{2,1,0:T(8,128)S(1)}, f32[1,256,1024]{2,1,0:T(8,128)}, u32[]{:S(2)}) copy-start(f32[1,256,1024]{2,1,0:T(8,128)} %param.39) | copy-start | bytes 3145732
  642.8 279.5 %copy-start.38 = (u32[32]{0:T(128)S(1)}, u32[32]{0:T(128)}, u32[]{:S(2)}) copy-start(u32[32]{0:T(128)} %constant.235) | copy-start | bytes 388
  642.8 281.5 %copy-start.4 = (f32[256,1024]{1,0:T(8,128)S(1)}, f32[256,1024]{1,0:T(8,128)}, u32[]{:S(2)}) copy-start(f32[256,1024]{1,0:T(8,128)} %copy-done.3) | copy-start | bytes 3145732
  642.9 501.6 %all-reduce.14.cloned.1.call-start = ((), (), s32[]{:S(2)}) async-start(), calls=%async_computation.22 | async-start | bytes 12582912 | tf_op jit(solution)/shard_map/psum | solution.py:320
  961.7 7.6 copy-start.21
  1144.5 6.8 copy-start.27
  1144.5 7.9 copy-start.20
  1151.3 3.6 copy-start.19
  (8 other events, 9.3 us)
Sparse Core Ops, SparseCore 0:
  10.2 25.2 all-gather.8
  37.6 22.5 all-gather.14
  62.4 22.5 all-gather.12
  87.6 73.3 all-gather.10
  163.6 71.6 all-gather.16
  237.2 20.8 all-gather.18
  259.7 58.2 all-gather.20
  319.6 58.2 all-gather.22
  488.0 149.4 reduce-scatter.7
  640.0 30.4 reduce-scatter.15
  673.6 31.4 reduce-scatter.9
  707.7 71.6 reduce-scatter.17
  782.0 71.7 reduce-scatter.19
  856.3 31.4 reduce-scatter.13
  890.8 31.4 reduce-scatter.11
  927.9 216.5 all-reduce.13
where the time goes:
time: 1170 us; the launch traced here: 1160 us
  waiting for transfers between devices  865 us (74%)
  matrix products  130 us (11%)
  other arithmetic  66.8 us (6%)
  local copies, waits for them, and re-layouts  50.3 us (4%)
  blocking collectives  34 us (3%)
  between operations  16.1 us (1%)
    psum x1, waiting for transfers between devices, per_device(): lax.psum(shard_query.astype(jnp.bfloat16), 'ctx').astype(jnp.float32)  173 us
    reduce_scatter x1, waiting for transfers between devices, per_device(): lax.psum_scatter(grad_rows.astype(jnp.bfloat16), 'ctx', scatter_dimension...  128 us
    reduce_scatter x1, waiting for transfers between devices, per_device(): lax.psum_scatter(grad_reduce.astype(jnp.bfloat16), 'fsdp', scatter_dimens...  74.4 us
    reduce_scatter x1, waiting for transfers between devices, per_device(): lax.psum_scatter(grad_expand.astype(jnp.bfloat16), 'fsdp', scatter_dimens...  74.4 us
    all_gather x1, waiting for transfers between devices, per_device(): key_piece = lax.all_gather(keys_r, 'ctx', axis=0, tiled=True)  73.5 us
    all_gather x1, waiting for transfers between devices, per_device(): value_piece = lax.all_gather(values_r, 'ctx', axis=0, tiled=True)  67.8 us
    all_gather x1, waiting for transfers between devices, per_device(): lax.all_gather(w_expand.astype(jnp.bfloat16), 'fsdp', axis=0, tiled=True)  43.5 us
    all_gather x1, waiting for transfers between devices, per_device(): lax.all_gather(w_reduce.astype(jnp.bfloat16), 'fsdp', axis=0, tiled=True)  43.1 us
  transfers between devices with their start and end apart: 16, of which 15 were waited for; matrix products, arithmetic and copies ran while one was open for 10% of the time, Pallas kernels for 0%

commit v1 on v0

v1 whole, which is shorter than its diff:
```python
import functools

import jax
import jax.numpy as jnp
from jax import lax
from jax.experimental import pallas as pl
from jax.experimental.pallas import tpu as pltpu
from jax.sharding import PartitionSpec as P

HEADS = 16
LANES = 128
epsilon = 1e-05
masked_value = -1e30
query_scale = 0.125
bf16 = jnp.bfloat16
f32 = jnp.float32
vmem_limit = 56 * 1024 * 1024


def matmul(left, right):
    return jnp.dot(left, right, preferred_element_type=f32)


def left_transposed(left, right):
    return lax.dot_general(left, right, (((0,), (0,)), ((), ())), preferred_element_type=f32)


def right_transposed(left, right):
    return lax.dot_general(left, right, (((1,), (1,)), ((), ())), preferred_element_type=f32)


def swap(array, axis, mask):
    size = lax.axis_size(axis)
    return lax.ppermute(array, axis, [(i, i ^ mask) for i in range(size)])


def shape(*sizes, dtype=f32):
    return jax.ShapeDtypeStruct(sizes, dtype)


def call(body, name, out_shape, operands, scalars=None, scratch=(), aliases=None, **grid):
    count = 0 if scalars is None else 1
    if not grid:
        whole = pl.BlockSpec(memory_space=pltpu.VMEM)
        several = isinstance(out_shape, (list, tuple))
        grid = dict(
            grid=(), in_specs=[whole] * len(operands), out_specs=[whole] * len(out_shape) if several else whole
        )
    return pl.pallas_call(
        body,
        out_shape=out_shape,
        grid_spec=pltpu.PrefetchScalarGridSpec(
            num_scalar_prefetch=count, scratch_shapes=list(scratch), **grid
        ),
        input_output_aliases=aliases or {},
        compiler_params=pltpu.CompilerParams(vmem_limit_bytes=vmem_limit),
        cost_estimate=pl.CostEstimate(flops=1, bytes_accessed=1, transcendentals=0),
        name=name,
    )(*([] if scalars is None else [scalars]), *operands)


def aligned(index, size):
    return pl.ds(pl.multiple_of(index * size, size), size)


def gather_ctx(own):
    size = lax.axis_size("ctx")
    masks = [1 << i for i in range(size.bit_length() - 1)]
    blocks = {0: own}
    for mask in masks[1:]:
        for index in list(blocks):
            blocks[index | mask] = swap(blocks[index], "ctx", mask)
    for index in list(blocks):
        blocks[index | 1] = swap(blocks[index], "ctx", 1)
    return [blocks[i] for i in range(len(blocks))]


def ctx_groups():
    bits = lax.axis_size("ctx").bit_length() - 1
    groups = [(0, 2)]
    first = 1
    while first < bits:
        count = min(2, bits - first)
        groups.append((first, 1 << count))
        first += count
    return groups


def sum_split(arrays, members, place):
    rows, width = arrays[0].shape
    size = rows // members
    number = len(arrays)

    def body(place_ref, *refs):
        ins, outs, total = refs[:number], refs[number:-1], refs[-1]
        value = ins[0][...].astype(f32)
        for ref in ins[1:]:
            value = value + ref[...].astype(f32)
        total[...] = value.astype(bf16)
        for m in range(members):
            outs[m][...] = total[aligned(place_ref[0] ^ m, size), :]

    return call(
        body,
        "sum_split",
        [shape(size, width, dtype=bf16)] * members,
        arrays,
        scalars=place.reshape(1),
        scratch=[pltpu.VMEM((rows, width), bf16)],
    )


def sum_all(arrays):
    def body(*refs):
        value = refs[0][...].astype(f32)
        for ref in refs[1:-1]:
            value = value + ref[...].astype(f32)
        refs[-1][...] = value.astype(bf16)

    return call(body, "sum_all", shape(*arrays[0].shape, dtype=bf16), arrays)


def join(arrays, place):
    size, width = arrays[0].shape

    def body(place_ref, *refs):
        for m in range(len(arrays)):
            refs[-1][aligned(place_ref[0] ^ m, size), :] = refs[m][...]

    return call(
        body,
        "join",
        shape(size * len(arrays), width, dtype=bf16),
        arrays,
        scalars=place.reshape(1),
    )


def sum_ctx(arrays):
    index = lax.axis_index("ctx").astype(jnp.int32)
    groups = ctx_groups()
    for first, members in groups:
        place = (index >> first) & (members - 1)
        pieces = sum_split(arrays, members, place)
        arrays = [pieces[0]] + [swap(pieces[m], "ctx", m << first) for m in range(1, members)]
    piece = sum_all(arrays)
    for first, members in reversed(groups):
        place = (index >> first) & (members - 1)
        pieces = [piece] + [swap(piece, "ctx", m << first) for m in range(1, members)]
        if first:
            piece = join(pieces, place)
    return pieces, place


def place_rows(chunks):
    pairs = [chunk for chunk, _ in chunks]
    place = chunks[0][1]
    size, width = pairs[0][0].shape
    number = len(pairs)

    def body(place_ref, *refs):
        for k in range(number):

            @pl.when(pl.program_id(0) == k)
            def _():
                for m in range(2):
                    where = aligned(place_ref[0] ^ m, size)
                    refs[-1][where, :] = refs[2 * k + m][...].astype(f32)

    return call(
        body,
        "place_rows",
        shape(number * 2 * size, width),
        [piece for pair in pairs for piece in pair],
        scalars=place.reshape(1),
        grid=(number,),
        in_specs=[pl.BlockSpec((size, width), lambda k, s: (0, 0))] * (2 * number),
        out_specs=pl.BlockSpec((2 * size, width), lambda k, s: (k, 0)),
    )


def place_expand(first, second, place, own, shard, model):
    sizes = [first[0].shape[0], second[0].shape[0]]

    def body(scalars, a0, a1, b0, b1, expand_ref, output_ref, first_all, second_all):
        for m, ref in enumerate((a0, a1)):
            first_all[aligned(scalars[0] ^ m, sizes[0]), :] = ref[...]
        for m, ref in enumerate((b0, b1)):
            second_all[aligned(scalars[0] ^ m, sizes[1]), :] = ref[...]
        for k, (source, unit) in {
            0: (first_all, 0),
            2: (first_all, 1),
            1: (second_all, 0),
            3: (second_all, 1),
        }.items():
            expand_ref[:, aligned(scalars[1] ^ k, expand_ref.shape[1] // 4)] = source[
                unit * shard : (unit + 1) * shard, :
            ].astype(f32)
        output_ref[...] = first_all[2 * shard : 3 * shard, :].astype(f32)

    columns = first[0].shape[1]
    return call(
        body,
        "place_expand",
        [shape(shard, 4 * columns), shape(shard, model)],
        [*first, *second],
        scalars=jnp.stack((place, own)),
        scratch=[pltpu.VMEM((2 * size, columns), bf16) for size in sizes],
    )


def place_projections(pieces, scalar, rows, width):
    count = len(pieces)
    if width % LANES:
        ordered = jnp.take(jnp.stack(pieces)[:, :rows], jnp.arange(count) ^ scalar, axis=0)
        ordered = jnp.transpose(ordered, (1, 0, 2)).astype(f32)
        return tuple(
            ordered[:, :, k * width : (k + 1) * width].reshape(rows, count * width)
            for k in range(3)
        )

    def body(scalar_ref, *refs):
        for i in range(count):
            where = aligned(scalar_ref[0] ^ i, width)
            for k in range(3):
                refs[count + k][:, where] = refs[i][:rows, k * width : (k + 1) * width].astype(f32)

    return call(
        body,
        "place_projections",
        [shape(rows, count * width)] * 3,
        pieces,
        scalars=scalar.reshape(1),
    )


def project(blocks, first, weights, bias, query_docs, key_docs, own, heads, head_size, length, before):
    tokens, model = blocks[0].shape
    width = heads * head_size
    shard = weights[0].shape[0]
    number = len(blocks)
    rows = number * tokens
    tile = 256
    per_block = tokens // tile
    start = first * per_block

    def body(own_ref, *refs):
        x_refs, w_refs = refs[:number], refs[number : number + 4]
        b_ref, qd_ref, kd_ref = refs[number + 4 : number + 7]
        q_ref, k_ref, v_ref, kt_ref, x_out = refs[-5:]
        for k in range(number):

            @pl.when(pl.program_id(0) // per_block == k)
            def _():
                x_out[...] = x_refs[k][...]

        product = b_ref[...]
        for k in range(4):
            product = product + matmul(x_out[:, aligned(own_ref[0] ^ k, shard)], w_refs[k][...])
        lane = lax.broadcasted_iota(jnp.int32, (tile, LANES - head_size), 1)
        ones = jnp.where(lane < 3, 1.0, 0.0).astype(f32)
        keys = product[:, width : 2 * width]
        for h in range(heads):
            cut = slice(h * head_size, (h + 1) * head_size)
            q_ref[h] = jnp.concatenate((product[:, :width][:, cut], qd_ref[...]), 1).astype(bf16)
            k_ref[h] = jnp.concatenate((keys[:, cut], kd_ref[...]), 1).astype(bf16)
            v_ref[h] = jnp.concatenate((product[:, 2 * width :][:, cut], ones), 1).astype(bf16)
        kt_ref[...] = jnp.transpose(keys).astype(bf16)

    out = shape(heads, length, LANES, dtype=bf16)
    out_spec = pl.BlockSpec((heads, tile, LANES), lambda i, s: (0, i + start, 0))
    extra_spec = pl.BlockSpec((tile, LANES - head_size), lambda i, s: (i + start, 0))
    old = list(before) if before is not None else []

    def block_map(k, i, s):
        return (jnp.clip(i - k * per_block, 0, per_block - 1), 0)

    operands = [*blocks, *weights, bias, query_docs, key_docs, *old]
    return call(
        body,
        "project",
        [out, out, out, shape(width, length, dtype=bf16), shape(length, model, dtype=bf16)],
        operands,
        scalars=own.reshape(1),
        aliases={1 + len(operands) - 5 + k: k for k in range(5)} if old else None,
        grid=(rows // tile,),
        in_specs=[pl.BlockSpec((tile, model), functools.partial(block_map, k)) for k in range(number)]
        + [pl.BlockSpec((shard, 3 * width), lambda i, s: (0, 0))] * 4
        + [pl.BlockSpec((1, 3 * width), lambda i, s: (0, 0)), extra_spec, extra_spec]
        + [pl.BlockSpec(memory_space=pl.ANY)] * len(old),
        out_specs=[
            out_spec,
            out_spec,
            out_spec,
            pl.BlockSpec((width, tile), lambda i, s: (0, i + start)),
            pl.BlockSpec((tile, model), lambda i, s: (i + start, 0)),
        ],
    )


def three_parts(value):
    high = value.astype(bf16).astype(f32)
    rest = value - high
    middle = rest.astype(bf16).astype(f32)
    return high, middle, rest - middle


def attend(queries, keys, values, first, number, tokens, head_size, docs, after):
    heads, length, _ = keys.shape
    width = heads * head_size
    tile = 256 if length <= 4096 else 128
    per_block = tokens // tile
    start = first * per_block
    rows = number * tokens

    def body(q_ref, k_ref, v_ref, after_ref, *outs):
        wide_ref, back_ref = outs[number:]
        lane = lax.broadcasted_iota(jnp.int32, (tile, LANES), 1)
        for h in range(heads):
            query = q_ref[h]
            scores = right_transposed(query, k_ref[h])
            largest = jnp.max(scores, axis=1, keepdims=True)
            weights = jnp.exp(scores - largest).astype(bf16)
            summed = matmul(weights, v_ref[h])
            total = summed[:, head_size : head_size + 1]
            cut = slice(h * head_size, (h + 1) * head_size)
            wide_ref[:, cut] = summed[:, :head_size] / total
            parts = three_parts(-(largest + jnp.log(total)))
            back = query.astype(f32)
            for k in range(3):
                back = jnp.where(lane == head_size + docs + k, parts[k], back)
            back_ref[h] = back.astype(bf16)
        for k in range(number):

            @pl.when(pl.program_id(0) // per_block == k)
            def _():
                outs[k][...] = wide_ref[...].astype(bf16)

    def block_map(k, i):
        return (jnp.clip(i - k * per_block, 0, per_block - 1), 0)

    result = call(
        body,
        "attend",
        [shape(tokens, width, dtype=bf16)] * number
        + [shape(rows, width), shape(heads, rows, LANES, dtype=bf16)],
        [queries, keys, values, after],
        grid=(rows // tile,),
        in_specs=[
            pl.BlockSpec((heads, tile, LANES), lambda i: (0, i + start, 0)),
            pl.BlockSpec((heads, length, LANES), lambda i: (0, 0, 0)),
            pl.BlockSpec((heads, length, LANES), lambda i: (0, 0, 0)),
            pl.BlockSpec(memory_space=pl.ANY),
        ],
        out_specs=[pl.BlockSpec((tile, width), functools.partial(block_map, k)) for k in range(number)]
        + [
            pl.BlockSpec((tile, width), lambda i: (i, 0)),
            pl.BlockSpec((heads, tile, LANES), lambda i: (0, i, 0)),
        ],
    )
    return result[:number], result[number], result[number + 1]


def attend_back(queries, douts, attended, keys, values, keys_t, before, head_size, after):
    heads, length, _ = keys.shape
    rows = attended.shape[0]
    block = douts[0].shape[0]
    width = heads * head_size
    tile = 256 if length <= 4096 else 128
    number = len(douts)
    per_block = block // tile

    def body(*refs):
        q_ref, a_ref, k_ref, v_ref, kt_ref, after_ref = refs[:6]
        d_refs = refs[6 : 6 + number]
        rest = refs[6 + number :]
        if before is not None:
            old_k, old_v = rest[:2]
            rest = rest[2:]
        dq_ref, dk_ref, dv_ref, d_scratch = rest
        step = pl.program_id(0)

        @pl.when(step == 0)
        def _():
            if before is None:
                dk_ref[...] = jnp.zeros_like(dk_ref)
                dv_ref[...] = jnp.zeros_like(dv_ref)
            else:
                dk_ref[...] = old_k[...]
                dv_ref[...] = old_v[...]

        for k in range(number):

            @pl.when(step // per_block == k)
            def _():
                d_scratch[...] = d_refs[k][...].astype(f32)

        lane = lax.broadcasted_iota(jnp.int32, (tile, LANES - head_size), 1)
        for h in range(heads):
            cut = slice(h * head_size, (h + 1) * head_size)
            dout = d_scratch[:, cut]
            parts = three_parts(-jnp.sum(dout * a_ref[:, cut], axis=1, keepdims=True))
            extra = jnp.zeros((tile, LANES - head_size), f32)
            for k in range(3):
                extra = jnp.where(lane == k, parts[k], extra)
            dout = jnp.concatenate((dout, extra), axis=1).astype(bf16)
            query = q_ref[h]
            probabilities = jnp.exp(right_transposed(k_ref[h], query))
            grads = right_transposed(v_ref[h], dout)
            d_scores = (probabilities * grads).astype(bf16)
            dk_ref[:, cut] += matmul(d_scores, query)[:, :head_size]
            dv_ref[:, cut] += matmul(probabilities.astype(bf16), dout)[:, :head_size]
            dq_t = matmul(kt_ref[cut, :], d_scores)
            dq_ref[:, cut] = jnp.transpose(dq_t).astype(bf16)

    whole = pl.BlockSpec((length, width), lambda i: (0, 0))
    resident = pl.BlockSpec((heads, length, LANES), lambda i: (0, 0, 0))

    def dout_map(k, i):
        return (jnp.clip(i - k * per_block, 0, per_block - 1), 0)

    in_specs = [
        pl.BlockSpec((heads, tile, LANES), lambda i: (0, i, 0)),
        pl.BlockSpec((tile, width), lambda i: (i, 0)),
        resident,
        resident,
        pl.BlockSpec((width, length), lambda i: (0, 0)),
        pl.BlockSpec(memory_space=pl.ANY),
    ] + [pl.BlockSpec((tile, width), functools.partial(dout_map, k)) for k in range(number)]
    operands = [queries, attended, keys, values, keys_t, after, *douts]
    if before is not None:
        in_specs += [whole, whole]
        operands += list(before)
    return call(
        body,
        "attend_back",
        [shape(rows, width, dtype=bf16), shape(length, width), shape(length, width)],
        operands,
        scratch=[pltpu.VMEM((tile, width), f32)],
        grid=(rows // tile,),
        in_specs=in_specs,
        out_specs=[pl.BlockSpec((tile, width), lambda i: (i, 0)), whole, whole],
    )


def head_grads(d_queries, d_key, d_value, tokens, number):
    width = d_key.shape[1]
    count = len(d_queries)
    rows = number * tokens

    def body(*refs):
        dk_ref, dv_ref = refs[count : count + 2]
        all_ref = refs[count + 2]
        first = 0
        for ref in refs[:count]:
            all_ref[first : first + ref.shape[0], :width] = ref[...]
            first += ref.shape[0]
        all_ref[:, width : 2 * width] = dk_ref[:rows, :].astype(bf16)
        all_ref[:, 2 * width :] = dv_ref[:rows, :].astype(bf16)
        for k in range(number):
            refs[count + 3 + k][...] = all_ref[k * tokens : (k + 1) * tokens, :]

    result = call(
        body,
        "head_grads",
        [shape(rows, 3 * width, dtype=bf16)] + [shape(tokens, 3 * width, dtype=bf16)] * number,
        [*d_queries, d_key, d_value],
    )
    return result[0], result[1:]


def lane_copy(value):
    return jnp.broadcast_to(value, (value.shape[0], LANES))


def attention_norm(parts, weights, inputs, vectors, scalars, width):
    number = len(parts)
    tokens, model = inputs.shape
    shard = weights[0].shape[0]

    def body(s_ref, *refs):
        p_refs, w_refs = refs[:number], refs[number : number + 4]
        x_ref, v_ref = refs[number + 4 : number + 6]
        normed_ref, rounded_ref, unit_ref, inverse_ref, all_ref, matrix = refs[number + 6 :]
        for k in range(4):
            matrix[aligned(s_ref[1] ^ k, shard), :] = w_refs[k][...]
        value = x_ref[...] + v_ref[0:1, :]
        for i in range(number):
            all_ref[:, i * width : (i + 1) * width] = p_refs[i][...]
            value = value + matmul(p_refs[i][...], matrix[aligned(s_ref[0] ^ i, width), :])
        average = jnp.mean(value, axis=-1, keepdims=True)
        centered = value - average
        inverse = lax.rsqrt(jnp.mean(centered * centered, axis=-1, keepdims=True) + epsilon)
        unit = centered * inverse
        normed = unit * v_ref[1:2, :] + v_ref[2:3, :]
        normed_ref[...] = normed
        rounded_ref[...] = normed.astype(bf16)
        unit_ref[...] = unit
        inverse_ref[...] = lane_copy(inverse)

    return call(
        body,
        "attention_norm",
        [
            shape(tokens, model),
            shape(tokens, model, dtype=bf16),
            shape(tokens, model),
            shape(tokens, LANES),
            shape(tokens, model, dtype=bf16),
        ],
        [*parts, *weights, inputs, vectors],
        scalars=scalars,
        scratch=[pltpu.VMEM((model, model), bf16)],
    )


def feed_forward(own, sibling, expand_parts, reduce_parts, bias, f):
    tokens, model = own.shape
    shard = expand_parts[0].shape[0]
    half = reduce_parts[0].shape[0]
    tile = 256
    steps = 2 * half // tile

    def body(f_ref, a_ref, b_ref, *refs):
        w_refs, r_refs, bias_ref = refs[:4], refs[4:6], refs[6]
        act_ref, slope_ref, own_ref, other_ref, x_all = refs[7:]
        step = pl.program_id(0)

        @pl.when(step == 0)
        def _():
            for k in range(4):
                chunk = aligned(f_ref[0] ^ k, shard)
                x_all[:tokens, k * shard : (k + 1) * shard] = a_ref[:, chunk]
                x_all[tokens:, k * shard : (k + 1) * shard] = b_ref[:, chunk]
            own_ref[...] = jnp.zeros_like(own_ref)
            other_ref[...] = jnp.zeros_like(other_ref)

        value = bias_ref[...]
        for k in range(4):
            value = value + matmul(x_all[:, k * shard : (k + 1) * shard], w_refs[k][...])
        below = 0.5 + 0.5 * lax.erf(value * 0.7071067811865476)
        density = 0.3989422804014327 * jnp.exp(-0.5 * value * value)
        activated = (value * below).astype(bf16)
        act_ref[...] = activated
        slope_ref[...] = (below + value * density).astype(bf16)
        for k in range(2):

            @pl.when(step // (half // tile) == k)
            def _():
                own_ref[...] += matmul(activated[:tokens], r_refs[k][...])
                other_ref[...] += matmul(activated[tokens:], r_refs[k][...])

    per = half // tile
    wide = shape(2 * tokens, 2 * half, dtype=bf16)
    whole = pl.BlockSpec((tokens, model), lambda t, s: (0, 0))
    return call(
        body,
        "feed_forward",
        [wide, wide, shape(tokens, model), shape(tokens, model)],
        [own, sibling, *expand_parts, *reduce_parts, bias],
        scalars=f.reshape(1),
        scratch=[pltpu.VMEM((2 * tokens, model), bf16)],
        grid=(steps,),
        in_specs=[whole, whole]
        + [pl.BlockSpec((shard, tile), lambda t, s: (0, t))] * 4
        + [
            pl.BlockSpec((tile, model), lambda t, s: (jnp.minimum(t, per - 1), 0)),
            pl.BlockSpec((tile, model), lambda t, s: (jnp.maximum(t - per, 0), 0)),
            pl.BlockSpec((1, tile), lambda t, s: (0, t)),
        ],
        out_specs=[pl.BlockSpec((2 * tokens, tile), lambda t, s: (0, t))] * 2 + [whole, whole],
    )


def second_norm(normed, own, received, vectors, cotangent):
    tokens, model = normed.shape
    tile = 64

    def body(n_ref, p_ref, r_ref, v_ref, c_ref, out_ref, d_ref, rounded_ref, sums_ref):
        value = n_ref[...] + p_ref[...] + r_ref[...] + v_ref[0:1, :]
        average = jnp.mean(value, axis=-1, keepdims=True)
        centered = value - average
        inverse = lax.rsqrt(jnp.mean(centered * centered, axis=-1, keepdims=True) + epsilon)
        unit = centered * inverse
        out_ref[...] = unit * v_ref[1:2, :] + v_ref[2:3, :]
        dy = c_ref[...]
        dz = dy * v_ref[1:2, :]
        mean_dz = jnp.mean(dz, axis=-1, keepdims=True)
        mean_dzz = jnp.mean(dz * unit, axis=-1, keepdims=True)
        result = inverse * (dz - mean_dz - unit * mean_dzz)
        d_ref[...] = result
        rounded = result.astype(bf16)
        rounded_ref[...] = rounded

        @pl.when(pl.program_id(0) == 0)
        def _():
            sums_ref[...] = jnp.zeros_like(sums_ref)

        sums_ref[0:1, :] += jnp.sum(dy * unit, axis=0, keepdims=True)
        sums_ref[1:2, :] += jnp.sum(dy, axis=0, keepdims=True)
        sums_ref[2:3, :] += jnp.sum(rounded.astype(f32), axis=0, keepdims=True)

    rows = pl.BlockSpec((tile, model), lambda i: (i, 0))
    fixed = pl.BlockSpec((8, model), lambda i: (0, 0))
    return call(
        body,
        "second_norm",
        [shape(tokens, model), shape(tokens, model), shape(tokens, model, dtype=bf16), shape(8, model)],
        [normed, own, received, vectors, cotangent],
        grid=(tokens // tile,),
        in_specs=[rows, rows, rows, fixed, rows],
        out_specs=[rows, rows, rows, fixed],
    )


def feed_back(own, sibling, slope, expand_parts, reduce_parts, f):
    tokens, model = own.shape
    shard = expand_parts[0].shape[0]
    half = reduce_parts[0].shape[0]
    tile = 256
    per = half // tile
    steps = 2 * per

    def body(f_ref, a_ref, b_ref, slope_ref, *refs):
        w_refs, r_refs = refs[:4], refs[4:6]
        de_ref, sums_ref, own_ref, other_ref, d_all, dact, total = refs[6:]
        step = pl.program_id(0)

        @pl.when(step == 0)
        def _():
            d_all[:tokens, :] = a_ref[...]
            d_all[tokens:, :] = b_ref[...]
            total[...] = jnp.zeros_like(total)

        for k in range(2):

            @pl.when(step // per == k)
            def _():
                dact[...] = right_transposed(d_all[...], r_refs[k][...])

        rounded = (dact[...] * slope_ref[...].astype(f32)).astype(bf16)
        de_ref[...] = rounded
        sums_ref[...] = jnp.sum(rounded.astype(f32), axis=0, keepdims=True)
        for k in range(4):
            total[:, k * shard : (k + 1) * shard] += right_transposed(rounded, w_refs[k][...])

        @pl.when(step == steps - 1)
        def _():
            for k in range(4):
                chunk = aligned(f_ref[0] ^ k, shard)
                own_ref[:, chunk] = total[:tokens, k * shard : (k + 1) * shard]
                other_ref[:, chunk] = total[tokens:, k * shard : (k + 1) * shard]

    whole = pl.BlockSpec((tokens, model), lambda t, s: (0, 0))
    wide = pl.BlockSpec((2 * tokens, tile), lambda t, s: (0, t))
    return call(
        body,
        "feed_back",
        [
            shape(2 * tokens, 2 * half, dtype=bf16),
            shape(1, 2 * half),
            shape(tokens, model),
            shape(tokens, model),
        ],
        [own, sibling, slope, *expand_parts, *reduce_parts],
        scalars=f.reshape(1),
        scratch=[
            pltpu.VMEM((2 * tokens, model), bf16),
            pltpu.VMEM((2 * tokens, tile), f32),
            pltpu.VMEM((2 * tokens, model), f32),
        ],
        grid=(steps,),
        in_specs=[whole, whole, wide]
        + [pl.BlockSpec((shard, tile), lambda t, s: (0, t))] * 4
        + [
            pl.BlockSpec((tile, model), lambda t, s: (jnp.minimum(t, per - 1), 0)),
            pl.BlockSpec((tile, model), lambda t, s: (jnp.maximum(t - per, 0), 0)),
        ],
        out_specs=[wide, pl.BlockSpec((1, tile), lambda t, s: (0, t)), whole, whole],
    )


def first_norm_back(d_second, own, received, unit, inverse, vectors, weights, scalars, width, number):
    tokens, model = d_second.shape
    shard = weights[0].shape[0]

    def body(s_ref, d_ref, p_ref, r_ref, u_ref, i_ref, v_ref, *refs):
        w_refs = refs[:4]
        first_ref, rounded_ref, sums_ref = refs[4:7]
        outs, matrix = refs[7:-1], refs[-1]
        for k in range(4):
            matrix[aligned(s_ref[1] ^ k, shard), :] = w_refs[k][...]
        dy = d_ref[...] + p_ref[...] + r_ref[...]
        unit_value = u_ref[...]
        dz = dy * v_ref[1:2, :]
        mean_dz = jnp.mean(dz, axis=-1, keepdims=True)
        mean_dzz = jnp.mean(dz * unit_value, axis=-1, keepdims=True)
        result = i_ref[:, 0:1] * (dz - mean_dz - unit_value * mean_dzz)
        first_ref[...] = result
        rounded = result.astype(bf16)
        rounded_ref[...] = rounded
        sums_ref[...] = jnp.zeros_like(sums_ref)
        sums_ref[0:1, :] = jnp.sum(dy * unit_value, axis=0, keepdims=True)
        sums_ref[1:2, :] = jnp.sum(dy, axis=0, keepdims=True)
        sums_ref[2:3, :] = jnp.sum(rounded.astype(f32), axis=0, keepdims=True)
        for i in range(number):
            rows = matrix[aligned(s_ref[0] ^ i, width), :]
            outs[i][...] = right_transposed(rounded, rows).astype(bf16)

    result = call(
        body,
        "first_norm_back",
        [shape(tokens, model), shape(tokens, model, dtype=bf16), shape(8, model)]
        + [shape(tokens, width, dtype=bf16)] * number,
        [d_second, own, received, unit, inverse, vectors, *weights],
        scalars=scalars,
        scratch=[pltpu.VMEM((model, model), bf16)],
    )
    return result[:3], result[3:]


def input_gradient(d_first, blocks, matrix, scalar, width):
    number = len(blocks)
    tokens, model = d_first.shape
    if width % LANES:
        columns = [
            lax.dynamic_slice_in_dim(matrix, k * model + (scalar ^ i) * width, width, 1)
            for i in range(number)
            for k in range(3)
        ]
        return d_first + right_transposed(
            jnp.concatenate(blocks, axis=1), jnp.concatenate(columns, axis=1)
        )

    def body(s_ref, d_ref, m_ref, *refs):
        value = d_ref[...]
        for i in range(number):
            for k in range(3):
                where = pl.ds(pl.multiple_of(k * model + (s_ref[0] ^ i) * width, width), width)
                value = value + right_transposed(
                    refs[i][:, k * width : (k + 1) * width], m_ref[:, where]
                )
        refs[-1][...] = value

    return call(
        body,
        "input_gradient",
        shape(tokens, model),
        [d_first, matrix, *blocks],
        scalars=scalar.reshape(1),
    )


def cast_projections(matrices, after):
    rows, model = matrices[0].shape

    def body(q_ref, k_ref, v_ref, after_ref, out_ref):
        out_ref[:, :model] = (q_ref[...] * query_scale).astype(bf16)
        out_ref[:, model : 2 * model] = k_ref[...].astype(bf16)
        out_ref[:, 2 * model :] = v_ref[...].astype(bf16)

    whole = pl.BlockSpec((rows, model), lambda: (0, 0))
    return call(
        body,
        "cast_projections",
        shape(rows, 3 * model, dtype=bf16),
        [*matrices, after],
        grid=(),
        in_specs=[whole] * 3 + [pl.BlockSpec(memory_space=pl.ANY)],
        out_specs=pl.BlockSpec((rows, 3 * model), lambda: (0, 0)),
    )


def padded(vectors):
    return jnp.concatenate((jnp.stack(vectors), jnp.zeros((8 - len(vectors), vectors[0].shape[0]), f32)))


def per_device(
    hidden_in,
    starts,
    w_query,
    w_key,
    w_value,
    w_output,
    w_expand,
    w_reduce,
    bias_query,
    bias_value,
    bias_output,
    bias_expand,
    bias_reduce,
    attention_gain,
    attention_shift,
    feedforward_gain,
    feedforward_shift,
    cotangent,
):
    tokens, model = hidden_in.shape[1:]
    head_size = model // HEADS
    ctx_size = lax.axis_size("ctx")
    length = tokens * ctx_size
    near = min(ctx_size, HEADS)
    copies = ctx_size // near
    heads = HEADS // near
    width = heads * head_size
    shard = w_query.shape[0]
    ff_block = w_reduce.shape[0]
    documents = starts.shape[1]
    c = lax.axis_index("ctx").astype(jnp.int32)
    f = lax.axis_index("fsdp").astype(jnp.int32)
    group = c & (near - 1)
    both = jnp.stack((group, f))

    inputs = hidden_in[0]
    blocks = gather_ctx(inputs.astype(bf16))

    own_columns = jnp.concatenate(
        [
            lax.dynamic_slice_in_dim(m, group * width, width, 1) * scale
            for m, scale in ((w_query, query_scale), (w_key, 1.0), (w_value, 1.0))
        ],
        axis=1,
    ).astype(bf16)

    def gather_rows(own):
        rows = own.shape[0]
        across = swap(own, "fsdp", 2)
        others = swap(jnp.concatenate((own, across), axis=0), "fsdp", 1)
        return [own, others[:rows], across, others[rows:]]

    projection_parts = gather_rows(own_columns)
    output_parts = gather_rows(w_output.astype(bf16))

    def expand_columns(order):
        return jnp.concatenate(
            [lax.dynamic_slice_in_dim(w_expand, (f ^ k) * ff_block, ff_block, 1) for k in order],
            axis=1,
        ).astype(bf16)

    expand_own = expand_columns((0, 2))
    expand_flipped = expand_columns((2, 0))
    sibling_flipped = swap(expand_columns((3, 1)), "fsdp", 1)
    expand_sibling = jnp.concatenate(
        (sibling_flipped[:, ff_block:], sibling_flipped[:, :ff_block]), axis=1
    )
    expand_parts = [
        expand_own,
        expand_sibling,
        swap(expand_flipped, "fsdp", 2),
        swap(sibling_flipped, "fsdp", 2),
    ]
    reduce_r = w_reduce.astype(bf16)
    reduce_parts = [reduce_r, swap(reduce_r, "fsdp", 2)]
    expand_bias = jnp.concatenate(
        [lax.dynamic_slice_in_dim(bias_expand, (f ^ k) * ff_block, ff_block, 0) for k in (0, 2)]
    ).reshape(1, -1)

    order = c ^ lax.iota(jnp.int32, ctx_size)
    positions = (order[:, None] * tokens + lax.iota(jnp.int32, tokens)[None, :]).reshape(-1)
    docs = jnp.sum((starts[0][None, :] <= positions[:, None]).astype(jnp.int32), axis=1) - 1
    lane = lax.iota(jnp.int32, LANES - head_size)[None, :]
    same = docs[:, None] == lane
    query_docs = jnp.where((lane < documents) & ~same, masked_value, 0.0).astype(f32)
    key_docs = jnp.where(same | ((lane >= documents) & (lane < documents + 3)), 1.0, 0.0).astype(f32)
    own_bias = jnp.concatenate(
        (
            lax.dynamic_slice_in_dim(bias_query * query_scale, group * width, width, 0),
            jnp.zeros((width,), f32),
            lax.dynamic_slice_in_dim(bias_value, group * width, width, 0),
        )
    ).reshape(1, -1)
    attention_vectors = padded((bias_output, attention_gain, attention_shift))
    feed_vectors = padded((bias_reduce, feedforward_gain, feedforward_shift))

    state = None
    for first in range(0, ctx_size, 2):
        state = project(
            blocks[first : first + 2],
            first,
            projection_parts,
            own_bias,
            query_docs,
            key_docs,
            f,
            heads,
            head_size,
            length,
            state,
        )
    queries, keys, values, keys_t, stream = state
    all_projection = lax.all_gather(
        cast_projections((w_query, w_key, w_value), queries), "fsdp", axis=0, tiled=True
    )

    half = near // 2
    parts = [None] * near
    kept = [None, None]
    after = queries
    for part in (1, 0):
        outs, wide, back = attend(
            queries, keys, values, part * half, half, tokens, head_size, documents, after
        )
        after = wide
        kept[part] = (wide, back)
        for k in range(half):
            index = part * half + k
            parts[index] = outs[k] if index == 0 else swap(outs[k], "ctx", index)
    normed, normed_r, first_unit, first_inverse, attended_r = attention_norm(
        parts, output_parts, inputs, attention_vectors, both, width
    )

    sibling_normed = swap(normed_r, "fsdp", 1)
    activated_r, slope, partial, other = feed_forward(
        normed_r, sibling_normed, expand_parts, reduce_parts, expand_bias, f
    )
    layer_out, d_second, d_reduced_r, second_sums = second_norm(
        normed, partial, swap(other, "fsdp", 1), feed_vectors, cotangent[0]
    )
    sibling_reduced = swap(d_reduced_r, "fsdp", 1)
    pair_reduced = jnp.concatenate((d_reduced_r, sibling_reduced), axis=0)
    pair_normed = jnp.concatenate((normed_r, sibling_normed), axis=0)

    cut = ff_block // 2

    def reduce_rows(first):
        return left_transposed(activated_r[:, first : first + cut], pair_reduced).astype(bf16)

    reduce_received = [swap(reduce_rows(ff_block + k * cut), "fsdp", 2) for k in range(2)]
    d_expanded_r, bias_expand_sum, partial, other = feed_back(
        d_reduced_r, sibling_reduced, slope, expand_parts, reduce_parts, f
    )
    (d_first, d_attention_r, first_sums), d_attended = first_norm_back(
        d_second,
        partial,
        swap(other, "fsdp", 1),
        first_unit,
        first_inverse,
        attention_vectors,
        output_parts,
        both,
        width,
        near,
    )
    douts = [d_attended[0]] + [swap(d_attended[i], "ctx", i) for i in range(1, near)]

    def expand_unit(row_block, column_block):
        rows = lax.dynamic_slice_in_dim(pair_normed, (f ^ row_block) * shard, shard, 1)
        columns = d_expanded_r[:, column_block * ff_block : (column_block + 1) * ff_block]
        return left_transposed(rows, columns).astype(bf16)

    def expand_units(row_block, flip):
        return jnp.concatenate([expand_unit(row_block, k ^ flip) for k in range(2)], axis=0)

    expand_received = [swap(expand_units(k, 1), "fsdp", 2) for k in (2, 3)]
    expand_other = sum_all([expand_units(1, 0), expand_received[1]])
    expand_mine = expand_units(0, 0)

    grad_output = left_transposed(attended_r, d_attention_r).astype(bf16)
    per_shard = shard // width

    def output_rows(index):
        return [
            lax.dynamic_slice_in_dim(
                grad_output, ((index * per_shard + e) ^ group) * width, width, 0
            )
            for e in range(per_shard)
        ]

    received = swap(jnp.concatenate(output_rows(f ^ 1) + output_rows(f ^ 3), axis=0), "fsdp", 1)
    output_sum = sum_all([jnp.concatenate(output_rows(f) + output_rows(f ^ 2), axis=0), received])
    output_received = swap(output_sum[shard:], "fsdp", 2)

    unit = 16 * ctx_size

    def pad_rows(arrays):
        rows = sum(a.shape[0] for a in arrays)
        missing = -rows % unit
        if missing:
            arrays = [*arrays, jnp.zeros((missing, arrays[0].shape[1]), bf16)]
        return jnp.concatenate(arrays, axis=0) if len(arrays) > 1 else arrays[0]

    chunk_terms = [
        [reduce_rows(0), reduce_received[0]],
        [reduce_rows(cut), reduce_received[1]],
        [pad_rows([expand_mine, output_sum[:shard]]), pad_rows([expand_received[0], output_received])],
        [swap(expand_other, "fsdp", 1)],
    ]
    chunks = [sum_ctx(terms) for terms in chunk_terms]
    grad_w_reduce = place_rows(chunks[:2])
    grad_w_expand, grad_w_output = place_expand(
        chunks[2][0], chunks[3][0], chunks[3][1], f, shard, model
    )

    bias_expand_all = jnp.zeros((4 * ff_block,), f32)
    for k in range(2):
        bias_expand_all = lax.dynamic_update_slice_in_dim(
            bias_expand_all,
            bias_expand_sum[0, k * ff_block : (k + 1) * ff_block],
            (f ^ (2 * k)) * ff_block,
            0,
        )
    vectors = jnp.concatenate(
        (first_sums[:3].reshape(-1), second_sums[:3].reshape(-1), bias_expand_all)
    ).reshape(-1, LANES)
    masks = [1 << i for i in range(ctx_size.bit_length() - 1)]
    for axis, mask in [("fsdp", 1), ("fsdp", 2)] + [("ctx", mask) for mask in masks]:
        vectors = vectors + swap(vectors, axis, mask)
    vectors = vectors.reshape(-1)
    grad_att_gain, grad_att_shift, grad_bias_output, grad_ff_gain, grad_ff_shift, grad_bias_reduce = [
        lax.dynamic_slice_in_dim(vectors[k * model : (k + 1) * model], f * shard, shard, 0)
        for k in range(6)
    ]
    grad_bias_expand = lax.dynamic_slice_in_dim(vectors[6 * model :], f * ff_block, ff_block, 0)

    before = None
    d_queries = []
    after = d_attended[0]
    for part in (0, 1):
        wide, back = kept[part]
        d_query, d_key, d_value = attend_back(
            back,
            douts[part * half : (part + 1) * half],
            wide,
            keys,
            values,
            keys_t,
            before,
            head_size,
            after,
        )
        before = (d_key, d_value)
        after = d_query
        d_queries.append(d_query)
    count = ctx_size
    while count > near:
        count //= 2
        received = [
            swap(d[count * tokens :].astype(bf16), "ctx", count).astype(f32) for d in (d_key, d_value)
        ]
        d_key = d_key[: count * tokens] + received[0]
        d_value = d_value[: count * tokens] + received[1]
    d_all, d_blocks = head_grads(d_queries, d_key, d_value, tokens, near)

    scales = jnp.concatenate((jnp.full((width,), query_scale, f32), jnp.ones((2 * width,), f32)))
    grad_projection = (left_transposed(stream[: near * tokens], d_all) * scales).astype(bf16)
    bias_rows = jnp.broadcast_to(jnp.sum(d_all.astype(f32), axis=0) * scales, (16, 3 * width)).astype(
        bf16
    )

    def projection_rows(index):
        return lax.dynamic_slice_in_dim(grad_projection, index * shard, shard, 0)

    received = swap(
        jnp.concatenate((projection_rows(f ^ 3), projection_rows(f ^ 1), bias_rows), axis=0),
        "fsdp",
        1,
    )
    mine = jnp.concatenate((projection_rows(f ^ 2), projection_rows(f), bias_rows), axis=0)
    mine = sum_all([mine, received])
    received = swap(jnp.concatenate((mine[:shard], mine[2 * shard :]), axis=0), "fsdp", 2)
    mine = sum_all([mine[shard:], received])
    count = ctx_size
    while count > near:
        count //= 2
        mine = sum_all([mine, swap(mine, "ctx", count)])
    pieces = gather_ctx(mine)[:near]
    grad_query, grad_key, grad_value = place_projections(pieces, group, shard, width)
    bias_all = jnp.stack([piece[shard] for piece in pieces]).astype(f32)
    bias_all = jnp.take(bias_all, group ^ lax.iota(jnp.int32, near), axis=0)
    grad_bias_query = lax.dynamic_slice_in_dim(bias_all[:, :width].reshape(-1), f * shard, shard, 0)
    grad_bias_value = lax.dynamic_slice_in_dim(
        bias_all[:, 2 * width :].reshape(-1), f * shard, shard, 0
    )

    mine = [d_blocks[0]] + [swap(d_blocks[i], "ctx", i) for i in range(1, near)]
    input_grad = input_gradient(d_first, mine, all_projection, group, width)

    return (
        layer_out[None],
        input_grad[None],
        grad_query,
        grad_key,
        grad_value,
        grad_w_output,
        grad_w_expand,
        grad_w_reduce,
        grad_bias_query,
        grad_bias_value,
        grad_bias_output,
        grad_bias_expand,
        grad_bias_reduce,
        grad_att_gain,
        grad_att_shift,
        grad_ff_gain,
        grad_ff_shift,
    )


def solution(mesh):
    rows = P("fsdp", None)
    activations = P("fsdp", "ctx", None)
    return jax.shard_map(
        per_device,
        mesh=mesh,
        in_specs=(activations,) + (rows,) * 7 + (P(),) * 9 + (activations,),
        out_specs=(activations, activations) + (rows,) * 6 + (P("fsdp"),) * 9,
        check_vma=False,
    )
```

time: 1170 us -> 633 us (0.54)
  waiting for transfers between devices: 865 us -> 233 us
  Pallas kernels: 0 us -> 185 us
  starting transfers between devices: 0.88 us -> 115 us
  matrix products: 130 us -> 19.1 us
  other arithmetic: 66.8 us -> 20.7 us
  blocking collectives: 34 us -> 0 us
  local copies, waits for them, and re-layouts: 50.3 us -> 36.4 us
    reduce_scatter x7 -> x0, waiting for transfers between devices: 407 us -> none  [the longest x1 128 us: per_device(): lax.psum_scatter(grad_rows.astype(jnp.bfloat16), 'ctx', scatter_dimension...]
    all_gather x8 -> x1, waiting for transfers between devices: 284 us -> 0.02 us  [per_device(): lax.all_gather(cast_projections((w_query, w_key, w_value), queries), 'fsd...]
    ppermute x0 -> x93, waiting for transfers between devices: none -> 233 us  [swap(): return lax.ppermute(array, axis, [(i, i ^ mask) for i in range(size)])]
    pallas_call x0 -> x39, Pallas kernels: none -> 185 us  [call(): pl.pallas_call(body, out_shape=out_shape, grid_spec=pltpu.PrefetchScalarG...]
    psum x1 -> x0, waiting for transfers between devices: 173 us -> none  [per_device(): lax.psum(shard_query.astype(jnp.bfloat16), 'ctx').astype(jnp.float32)]
    ppermute x0 -> x93, starting transfers between devices: none -> 115 us  [swap(): return lax.ppermute(array, axis, [(i, i ^ mask) for i in range(size)])]
    dot_general x40 -> x0, matrix products: 107 us -> none  [the longest x6 35.8 us: matmul(): return jnp.dot(left, right, preferred_element_type=jnp.float32)]
    convert_element_type x22 -> x5, other arithmetic: 34.4 us -> 1.78 us  [the longest x1 1.37 us: per_device(): blocks = gather_ctx(inputs.astype(bf16))]
  transfers between devices with their start and end apart: 16 -> 94, of which waited for: 15 -> 30; matrix products, arithmetic and copies ran while one was open for 10% -> 10% of each run, Pallas kernels for 0% -> 25%
where the time goes in v1:
time: 633 us; the launch traced here: 625 us
  waiting for transfers between devices  233 us (37%)
  Pallas kernels  185 us (29%)
  starting transfers between devices  115 us (18%)
  local copies, waits for them, and re-layouts  36.4 us (6%)
  other arithmetic  20.7 us (3%)
  matrix products  19.1 us (3%)
  between operations  15.6 us (2%)
    ppermute x93, waiting for transfers between devices, swap(): return lax.ppermute(array, axis, [(i, i ^ mask) for i in range(size)])  233 us
    pallas_call x39, Pallas kernels, call(): pl.pallas_call(body, out_shape=out_shape, grid_spec=pltpu.PrefetchScalarG...  185 us
    ppermute x93, starting transfers between devices, swap(): return lax.ppermute(array, axis, [(i, i ^ mask) for i in range(size)])  115 us
    dot_general x14, matrix products, left_transposed(): lax.dot_general(left, right, (((0,), (0,)), ((), ())), preferred_element_...  19.1 us
  transfers between devices with their start and end apart: 94, of which 30 were waited for; matrix products, arithmetic and copies ran while one was open for 10% of the time, Pallas kernels for 25%

profile of v1, /device:TPU:0, one launch (start us, length us, event | category | flops | bytes accessed | tf_op | source)
XLA Modules:
  0.0 624.7 jit_solution(3664918836645891680)
XLA Ops:
  22.0 3.8 collective-permute-done.3.refs_4_
  29.6 6.7 %collective-permute-done.refs_0_ = bf16[256,1024]{1,0:T(8,128)(2,1)} collective-permute-done((bf16[256,1024]{1,0:T(8,128)(2,1)S(1)}, bf16[256,1024]{1,0:T(8,128)(2,1)}, u32[]{:S(2)}, u32[]{:S(2)}) %collective-permute-start) | collective-permute-done | bytes 524320 | tf_op jit(solution)/shard_map/ppermute | solution.py:34
  42.0 7.0 %collective-permute-done.7.refs_1_ = bf16[256,1024]{1,0:T(8,128)(2,1)S(1)} collective-permute-done((bf16[256,1024]{1,0:T(8,128)(2,1)}, bf16[256,1024]{1,0:T(8,128)(2,1)S(1)}, u32[]{:S(2)}, u32[]{:S(2)}) %collective-permute-start.7) | collective-permute-done | bytes 524320 | tf_op jit(solution)/shard_map/ppermute | solution.py:34
  49.7 11.9 %collective-permute-done.1.refs_0_ = bf16[256,1024]{1,0:T(8,128)(2,1)} collective-permute-done((bf16[256,1024]{1,0:T(8,128)(2,1)}, bf16[256,1024]{1,0:T(8,128)(2,1)}, u32[]{:S(2)}, u32[]{:S(2)}) %collective-permute-start.1) | collective-permute-done | bytes 524320 | tf_op jit(solution)/shard_map/ppermute | solution.py:34
  65.6 4.0 project.4
  69.6 3.8 project.5
  75.0 3.8 project.6
  79.5 3.8 project.7
  83.3 9.8 %attend.2 = (bf16[256,128]{1,0:T(8,128)(2,1)}, bf16[256,128]{1,0:T(8,128)(2,1)}, bf16[256,128]{1,0:T(8,128)(2,1)}, bf16[256,128]{1,0:T(8,128)(2,1)}, f32[1024,128]{1,0:T(8,128)}, /*index=5*/bf16[2,1024,128]{2,1,0:T(8,128)(2,1)}) custom-call(bf16[2,2048,128]{2,1,0:T(8,128)(2,1)} %get-tuple-element.136.q_ref.after_ref, ...), custom_call_target="tpu_custom_call" | custom-call | flops 1 | bytes 1 | tf_op jit(solution)/shard_map/attend/pallas_call | solution.py:49
  93.3 9.9 %attend.3 = (bf16[256,128]{1,0:T(8,128)(2,1)}, bf16[256,128]{1,0:T(8,128)(2,1)}, bf16[256,128]{1,0:T(8,128)(2,1)}, bf16[256,128]{1,0:T(8,128)(2,1)}, f32[1024,128]{1,0:T(8,128)}, /*index=5*/bf16[2,1024,128]{2,1,0:T(8,128)(2,1)}) custom-call(bf16[2,2048,128]{2,1,0:T(8,128)(2,1)} %get-tuple-element.136.q_ref.after_ref, ...), custom_call_target="tpu_custom_call" | custom-call | flops 1 | bytes 1 | tf_op jit(solution)/shard_map/attend/pallas_call | solution.py:49
  127.7 6.3 %attention_norm.1 = (f32[256,1024]{1,0:T(8,128)}, bf16[256,1024]{1,0:T(8,128)(2,1)}, f32[256,1024]{1,0:T(8,128)}, f32[256,128]{1,0:T(8,128)}, bf16[256,1024]{1,0:T(8,128)(2,1)}) custom-call(s32[2]{0:T(128)} %pad_add_fusion.s_ref, bf16[256,128]{1,0:T(8,128)(2,1)} %get-tuple-element.140.refs_0_, bf16[256,128]{1,0:T(8,128)(2,1)} %copy-done.88, ...), custom_call_target="tpu_custom_call" | custom-call | flops 1 | bytes 1 | tf_op jit(solution)/shard_map/attention_norm/pallas_call | solution.py:49
  139.1 13.2 %feed_forward.1 = (bf16[512,2048]{1,0:T(8,128)(2,1)}, bf16[512,2048]{1,0:T(8,128)(2,1)}, f32[256,1024]{1,0:T(8,128)}, f32[256,1024]{1,0:T(8,128)}) custom-call(s32[1]{0:T(128)} %bitcast.1.own_ref.f_ref, bf16[256,1024]{1,0:T(8,128)(2,1)} %get-tuple-element.149.a_ref, bf16[256,1024]{1,0:T(8,128)(2,1)} %copy-done.12, ...), custom_call_target="tpu_custom_call" | custom-call | flops 1 | bytes 1 | tf_op jit(solution)/shard_map/feed_forward/pallas_call | solution.py:49
  156.4 4.8 second_norm.1
  161.7 3.2 cast_projections.1
  167.9 14.2 %feed_back.1 = (bf16[512,2048]{1,0:T(8,128)(2,1)}, f32[1,2048]{1,0:T(1,128)}, f32[256,1024]{1,0:T(8,128)}, f32[256,1024]{1,0:T(8,128)}) custom-call(s32[1]{0:T(128)} %bitcast.1.own_ref.f_ref, bf16[256,1024]{1,0:T(8,128)(2,1)} %get-tuple-element.154.a_ref, bf16[256,1024]{1,0:T(8,128)(2,1)} %copy-done.15, bf16[512,2048]{1,0:T(8,128)(2,1)} %get-tuple-element.155.slope_ref, ...), custom_call_target="tpu_custom_call" | custom-call | flops 1 | bytes 1 | tf_op jit(solution)/shard_map/feed_back/pallas_call | solution.py:49
  204.5 6.2 first_norm_back.1
  215.4 15.9 %collective-permute-done.79.refs_1_ = bf16[512,1024]{1,0:T(8,128)(2,1)S(1)} collective-permute-done((bf16[512,1024]{1,0:T(8,128)(2,1)}, bf16[512,1024]{1,0:T(8,128)(2,1)S(1)}, u32[]{:S(2)}, u32[]{:S(2)}) %collective-permute-start.79) | collective-permute-done | bytes 1048608 | tf_op jit(solution)/shard_map/ppermute | solution.py:34
  231.4 22.5 %collective-permute-done.70.refs_1_ = bf16[512,1024]{1,0:T(8,128)(2,1)S(1)} collective-permute-done((bf16[512,1024]{1,0:T(8,128)(2,1)}, bf16[512,1024]{1,0:T(8,128)(2,1)S(1)}, u32[]{:S(2)}, u32[]{:S(2)}) %collective-permute-start.70) | collective-permute-done | bytes 1048608 | tf_op jit(solution)/shard_map/ppermute | solution.py:34
  256.3 19.8 %collective-permute-done.60.refs_1_ = bf16[512,1024]{1,0:T(8,128)(2,1)S(1)} collective-permute-done((bf16[512,1024]{1,0:T(8,128)(2,1)}, bf16[512,1024]{1,0:T(8,128)(2,1)S(1)}, u32[]{:S(2)}, u32[]{:S(2)}) %collective-permute-start.60) | collective-permute-done | bytes 1048608 | tf_op jit(solution)/shard_map/ppermute | solution.py:34
  280.4 3.1 sum_split.12
  290.3 3.4 collective-permute-start.31
  294.3 15.3 %attend_back.2 = (bf16[1024,128]{1,0:T(8,128)(2,1)}, f32[2048,128]{1,0:T(8,128)}, f32[2048,128]{1,0:T(8,128)}) custom-call(bf16[2,1024,128]{2,1,0:T(8,128)(2,1)} %get-tuple-element.161.refs_0_, f32[1024,128]{1,0:T(8,128)} %get-tuple-element.162.refs_1_, bf16[2,2048,128]{2,1,0:T(8,128)(2,1)} %get-tuple-element.137.k_ref.refs_2_, ...), custom_call_target="tpu_custom_call" | custom-call | flops 1 | bytes 1 | tf_op jit(solution)/shard_map/attend_back/pallas_call | solution.py:49
  312.9 16.4 %attend_back.3 = (bf16[1024,128]{1,0:T(8,128)(2,1)}, f32[2048,128]{1,0:T(8,128)}, f32[2048,128]{1,0:T(8,128)}) custom-call(bf16[2,1024,128]{2,1,0:T(8,128)(2,1)} %get-tuple-element.169.refs_0_, f32[1024,128]{1,0:T(8,128)} %get-tuple-element.139.after_ref.refs_1_, bf16[2,2048,128]{2,1,0:T(8,128)(2,1)} %get-tuple-element.137.k_ref.refs_2_, ...), custom_call_target="tpu_custom_call" | custom-call | flops 1 | bytes 1 | tf_op jit(solution)/shard_map/attend_back/pallas_call | solution.py:49
  329.3 3.4 head_grads.1
  332.8 4.8 multiply_convert_fusion
  347.2 10.0 %collective-permute-done.51 = bf16[256,1024]{1,0:T(8,128)(2,1)S(1)} collective-permute-done((bf16[256,1024]{1,0:T(8,128)(2,1)S(1)}, bf16[256,1024]{1,0:T(8,128)(2,1)S(1)}, u32[]{:S(2)}, u32[]{:S(2)}) %collective-permute-start.51) | collective-permute-done | bytes 524320 | tf_op jit(solution)/shard_map/ppermute | solution.py:34
  358.5 3.9 sum_split.8
  366.9 16.6 %collective-permute-done.90 = f32[80,128]{1,0:T(8,128)S(1)} collective-permute-done((f32[80,128]{1,0:T(8,128)S(1)}, f32[80,128]{1,0:T(8,128)S(1)}, u32[]{:S(2)}, u32[]{:S(2)}) %collective-permute-start.90) | collective-permute-done | bytes 40992 | tf_op jit(solution)/shard_map/ppermute | solution.py:34
  389.4 3.6 collective-permute-start.92
  411.4 5.1 collective-permute-done.73.refs_2_
  416.5 3.6 collective-permute-start.85
  436.5 3.8 collective-permute-start.55
  442.9 8.1 %collective-permute-start.45 = (bf16[272,384]{1,0:T(8,128)(2,1)}, bf16[272,384]{1,0:T(8,128)(2,1)S(1)}, u32[]{:S(2)}, u32[]{:S(2)}) collective-permute-start(bf16[272,384]{1,0:T(8,128)(2,1)} %sum_all.9.refs_0_), channel_id=1, source_target_pairs={{0,16},{4,20},{8,24},{12,28},{16,0},{20,4},{24,8},{28,12},{1,17},{... | collective-permute-start | bytes 626696 | tf_op jit(solution)/shard_map/ppermute | solution.py:34
  451.1 13.7 %collective-permute-done.54.refs_2_ = bf16[96,1024]{1,0:T(8,128)(2,1)S(1)} collective-permute-done((bf16[96,1024]{1,0:T(8,128)(2,1)}, bf16[96,1024]{1,0:T(8,128)(2,1)S(1)}, u32[]{:S(2)}, u32[]{:S(2)}) %collective-permute-start.54) | collective-permute-done | bytes 196640 | tf_op jit(solution)/shard_map/ppermute | solution.py:34
  471.6 7.6 %collective-permute-done.76.refs_2_ = bf16[64,1024]{1,0:T(8,128)(2,1)S(1)} collective-permute-done((bf16[64,1024]{1,0:T(8,128)(2,1)S(1)}, bf16[64,1024]{1,0:T(8,128)(2,1)S(1)}, u32[]{:S(2)}, u32[]{:S(2)}) %collective-permute-start.76) | collective-permute-done | bytes 131104 | tf_op jit(solution)/shard_map/ppermute | solution.py:34
  479.1 4.4 collective-permute-start.56
  487.6 12.5 %collective-permute-done.67.refs_2_ = bf16[64,1024]{1,0:T(8,128)(2,1)S(1)} collective-permute-done((bf16[64,1024]{1,0:T(8,128)(2,1)}, bf16[64,1024]{1,0:T(8,128)(2,1)S(1)}, u32[]{:S(2)}, u32[]{:S(2)}) %collective-permute-start.67) | collective-permute-done | bytes 131104 | tf_op jit(solution)/shard_map/ppermute | solution.py:34
  500.2 6.3 %collective-permute-done.57.refs_2_ = bf16[96,1024]{1,0:T(8,128)(2,1)S(1)} collective-permute-done((bf16[96,1024]{1,0:T(8,128)(2,1)}, bf16[96,1024]{1,0:T(8,128)(2,1)S(1)}, u32[]{:S(2)}, u32[]{:S(2)}) %collective-permute-start.57) | collective-permute-done | bytes 196640 | tf_op jit(solution)/shard_map/ppermute | solution.py:34
  525.4 37.6 %collective-permute-done.48.refs_7_ = bf16[272,384]{1,0:T(8,128)(2,1)S(1)} collective-permute-done((bf16[272,384]{1,0:T(8,128)(2,1)S(1)}, bf16[272,384]{1,0:T(8,128)(2,1)S(1)}, u32[]{:S(2)}, u32[]{:S(2)}) %collective-permute-start.48) | collective-permute-done | bytes 208928 | tf_op jit(solution)/shard_map/ppermute | solution.py:34
  565.1 3.5 place_projections.1
  569.9 4.3 collective-permute-done.33.refs_1_
  575.5 5.0 collective-permute-done.34.refs_2_
  587.0 3.5 collective-permute-start.39
  591.7 3.7 place_rows.1
  595.4 5.1 place_expand.1
  600.6 4.4 collective-permute-done.36.refs_4_
  605.0 4.0 collective-permute-done.37.refs_5_
  609.7 8.0 %input_gradient.1 = f32[256,1024]{1,0:T(8,128)} custom-call(s32[1]{0:T(128)} %bitcast.s_ref.scalar_ref, f32[256,1024]{1,0:T(8,128)} %get-tuple-element.160.d_ref, bf16[1024,3072]{1,0:T(8,128)(2,1)} %all-gather.2.cloned.1.call-done.m_ref, bf16[256,384]{1,0:T(8,128)(2,1)} %get-tuple-element.179.refs_0_, bf16[256,384]{1,0:T(8,128)(2,1)} %copy-done.57, ...), custom_call_target="tpu_custom_call" | custom-call | flops 1 | bytes 1 | tf_op jit(solution)/shard_map/input_gradient/pallas_call | solution.py:49
  (534 shorter events, 213.8 us)
Async XLA Ops:
  7.2 601.9 %all-gather.2.cloned.1.call-start = ((), (), s32[]{:S(2)}) async-start(), calls=%async_computation | async-start | bytes 7864320 | tf_op jit(solution)/shard_map/all_gather | solution.py:891
  8.6 30.7 %collective-permute-start.8 = (bf16[256,1024]{1,0:T(8,128)(2,1)S(1)}, bf16[256,1024]{1,0:T(8,128)(2,1)}, u32[]{:S(2)}, u32[]{:S(2)}) collective-permute-start(bf16[256,1024]{1,0:T(8,128)(2,1)S(1)} %bitcast_convert_fusion.refs_0_), channel_id=1, source_target_pairs={{0,4},{4,0},{8,12},{12,8},{16,20},{20,16},{24,28},{28,24},{1,5},{5... | collective-permute-start | bytes 1572872 | tf_op jit(solution)/shard_map/ppermute | solution.py:34
  11.7 24.6 %collective-permute-start = (bf16[256,1024]{1,0:T(8,128)(2,1)S(1)}, bf16[256,1024]{1,0:T(8,128)(2,1)}, u32[]{:S(2)}, u32[]{:S(2)}) collective-permute-start(bf16[256,1024]{1,0:T(8,128)(2,1)S(1)} %bitcast_convert_fusion.refs_0_), channel_id=1, source_target_pairs={{0,8},{4,12},{8,0},{12,4},{16,24},{20,28},{24,16},{28,20},{1,9},{5... | collective-permute-start | bytes 1572872 | tf_op jit(solution)/shard_map/ppermute | solution.py:34
  13.3 26.1 %collective-permute-start.5 = (bf16[256,1024]{1,0:T(8,128)(2,1)S(1)}, bf16[256,1024]{1,0:T(8,128)(2,1)}, u32[]{:S(2)}, u32[]{:S(2)}) collective-permute-start(bf16[256,1024]{1,0:T(8,128)(2,1)S(1)} %bitcast_convert_fusion.refs_0_), channel_id=1, source_target_pairs={{0,16},{4,20},{8,24},{12,28},{16,0},{20,4},{24,8},{28,12},{1,17},{... | collective-permute-start | bytes 1572872 | tf_op jit(solution)/shard_map/ppermute | solution.py:34
  36.7 24.9 %collective-permute-start.1 = (bf16[256,1024]{1,0:T(8,128)(2,1)}, bf16[256,1024]{1,0:T(8,128)(2,1)}, u32[]{:S(2)}, u32[]{:S(2)}) collective-permute-start(bf16[256,1024]{1,0:T(8,128)(2,1)} %collective-permute-done.refs_0_), channel_id=1, source_target_pairs={{0,16},{4,20},{8,24},{12,28},{16,0},{20,4},{24,8},{28,12},{1,17},{... | collective-permute-start | bytes 1572872 | tf_op jit(solution)/shard_map/ppermute | solution.py:34
  39.4 64.6 %collective-permute-start.19 = (bf16[256,2048]{1,0:T(8,128)(2,1)}, bf16[256,2048]{1,0:T(8,128)(2,1)}, u32[]{:S(2)}, u32[]{:S(2)}) collective-permute-start(bf16[256,2048]{1,0:T(8,128)(2,1)} %pad_maximum_fusion.4), channel_id=1, source_target_pairs={{0,1},{1,0},{2,3},{3,2},{4,5},{5,4},{6,7},{7,6},{8,9},{9,8},{10,11... | collective-permute-start | bytes 3145736 | tf_op jit(solution)/shard_map/ppermute | solution.py:34
  39.4 97.6 %collective-permute-start.22 = (bf16[1024,1024]{1,0:T(8,128)(2,1)S(1)}, bf16[1024,1024]{1,0:T(8,128)(2,1)S(1)}, u32[]{:S(2)}, u32[]{:S(2)}) collective-permute-start(bf16[1024,1024]{1,0:T(8,128)(2,1)S(1)} %convert_element_type.71.refs_4_), channel_id=1, source_target_pairs={{0,2},{1,3},{2,0},{3,1},{4,6},{5,7},{6,4},{7,5},{8,10},{9,11},{10,... | collective-permute-start | bytes 6291464 | tf_op jit(solution)/shard_map/ppermute | solution.py:34
  41.0 63.7 %collective-permute-start.17 = (bf16[512,1024]{1,0:T(8,128)(2,1)}, bf16[512,1024]{1,0:T(8,128)(2,1)}, u32[]{:S(2)}, u32[]{:S(2)}) collective-permute-start(bf16[512,1024]{1,0:T(8,128)(2,1)} %pad_maximum_fusion.2), channel_id=1, source_target_pairs={{0,1},{1,0},{2,3},{3,2},{4,5},{5,4},{6,7},{7,6},{8,9},{9,8},{10,11... | collective-permute-start | bytes 3145736 | tf_op jit(solution)/shard_map/ppermute | solution.py:34
  49.0 24.4 %collective-permute-start.6 = (bf16[256,1024]{1,0:T(8,128)(2,1)}, bf16[256,1024]{1,0:T(8,128)(2,1)S(1)}, u32[]{:S(2)}, u32[]{:S(2)}) collective-permute-start(bf16[256,1024]{1,0:T(8,128)(2,1)} %collective-permute-done.5.refs_0_), channel_id=1, source_target_pairs={{0,4},{4,0},{8,12},{12,8},{16,20},{20,16},{24,28},{28,24},{1,5},{5... | collective-permute-start | bytes 1572872 | tf_op jit(solution)/shard_map/ppermute | solution.py:34
  73.4 63.6 %collective-permute-start.20 = (bf16[256,2048]{1,0:T(8,128)(2,1)S(1)}, bf16[256,2048]{1,0:T(8,128)(2,1)S(1)}, u32[]{:S(2)}, u32[]{:S(2)}) collective-permute-start(bf16[256,2048]{1,0:T(8,128)(2,1)S(1)} %get-tuple-element.239), channel_id=1, source_target_pairs={{0,2},{1,3},{2,0},{3,1},{4,6},{5,7},{6,4},{7,5},{8,10},{9,11},{10,... | collective-permute-start | bytes 3145736 | tf_op jit(solution)/shard_map/ppermute | solution.py:34
  104.0 33.0 %collective-permute-start.21 = (bf16[256,2048]{1,0:T(8,128)(2,1)}, bf16[256,2048]{1,0:T(8,128)(2,1)S(1)}, u32[]{:S(2)}, u32[]{:S(2)}) collective-permute-start(bf16[256,2048]{1,0:T(8,128)(2,1)} %collective-permute-done.19), channel_id=1, source_target_pairs={{0,2},{1,3},{2,0},{3,1},{4,6},{5,7},{6,4},{7,5},{8,10},{9,11},{10,... | collective-permute-start | bytes 3145736 | tf_op jit(solution)/shard_map/ppermute | solution.py:34
  182.2 21.4 %collective-permute-start.25 = (f32[256,1024]{1,0:T(8,128)}, f32[256,1024]{1,0:T(8,128)S(1)}, u32[]{:S(2)}, u32[]{:S(2)}) collective-permute-start(f32[256,1024]{1,0:T(8,128)} %get-tuple-element.157), channel_id=1, source_target_pairs={{0,1},{1,0},{2,3},{3,2},{4,5},{5,4},{6,7},{7,6},{8,9},{9,8},{10,11... | collective-permute-start | bytes 3145736 | tf_op jit(solution)/shard_map/ppermute | solution.py:34
  185.1 46.3 %collective-permute-start.79 = (bf16[512,1024]{1,0:T(8,128)(2,1)}, bf16[512,1024]{1,0:T(8,128)(2,1)S(1)}, u32[]{:S(2)}, u32[]{:S(2)}) collective-permute-start(bf16[512,1024]{1,0:T(8,128)(2,1)} %convolution_convert_fusion.1), channel_id=1, source_target_pairs={{0,2},{1,3},{2,0},{3,1},{4,6},{5,7},{6,4},{7,5},{8,10},{9,11},{10,... | collective-permute-start | bytes 3145736 | tf_op jit(solution)/shard_map/ppermute | solution.py:34
  188.4 65.4 %collective-permute-start.70 = (bf16[512,1024]{1,0:T(8,128)(2,1)}, bf16[512,1024]{1,0:T(8,128)(2,1)S(1)}, u32[]{:S(2)}, u32[]{:S(2)}) collective-permute-start(bf16[512,1024]{1,0:T(8,128)(2,1)} %convolution_convert_fusion.3), channel_id=1, source_target_pairs={{0,2},{1,3},{2,0},{3,1},{4,6},{5,7},{6,4},{7,5},{8,10},{9,11},{10,... | collective-permute-start | bytes 3145736 | tf_op jit(solution)/shard_map/ppermute | solution.py:34
  190.9 85.3 %collective-permute-start.60 = (bf16[512,1024]{1,0:T(8,128)(2,1)}, bf16[512,1024]{1,0:T(8,128)(2,1)S(1)}, u32[]{:S(2)}, u32[]{:S(2)}) collective-permute-start(bf16[512,1024]{1,0:T(8,128)(2,1)} %pad_maximum_fusion.11), channel_id=1, source_target_pairs={{0,2},{1,3},{2,0},{3,1},{4,6},{5,7},{6,4},{7,5},{8,10},{9,11},{10,... | collective-permute-start | bytes 3145736 | tf_op jit(solution)/shard_map/ppermute | solution.py:34
  211.5 74.9 %collective-permute-start.88 = (f32[80,128]{1,0:T(8,128)S(1)}, f32[80,128]{1,0:T(8,128)S(1)}, u32[]{:S(2)}, u32[]{:S(2)}) collective-permute-start(f32[80,128]{1,0:T(8,128)S(1)} %maximum_bitcast_fusion), channel_id=1, source_target_pairs={{0,1},{1,0},{2,3},{3,2},{4,5},{5,4},{6,7},{7,6},{8,9},{9,8},{10,11... | collective-permute-start | bytes 122888 | tf_op jit(solution)/shard_map/ppermute | solution.py:34
  211.5 77.3 %collective-permute-start.26 = (bf16[256,128]{1,0:T(8,128)(2,1)}, bf16[256,128]{1,0:T(8,128)(2,1)S(1)}, u32[]{:S(2)}, u32[]{:S(2)}) collective-permute-start(bf16[256,128]{1,0:T(8,128)(2,1)} %get-tuple-element.165), channel_id=1, source_target_pairs={{0,4},{4,0},{8,12},{12,8},{16,20},{20,16},{24,28},{28,24},{1,5},{5... | collective-permute-start | bytes 196616 | tf_op jit(solution)/shard_map/ppermute | solution.py:34
  231.4 59.0 %collective-permute-start.27 = (bf16[256,128]{1,0:T(8,128)(2,1)S(1)}, bf16[256,128]{1,0:T(8,128)(2,1)S(1)}, u32[]{:S(2)}, u32[]{:S(2)}) collective-permute-start(bf16[256,128]{1,0:T(8,128)(2,1)S(1)} %copy-done.116), channel_id=1, source_target_pairs={{0,8},{4,12},{8,0},{12,4},{16,24},{20,28},{24,16},{28,20},{1,9},{5... | collective-permute-start | bytes 196616 | tf_op jit(solution)/shard_map/ppermute | solution.py:34
  253.8 39.9 %collective-permute-start.28 = (bf16[256,128]{1,0:T(8,128)(2,1)S(1)}, bf16[256,128]{1,0:T(8,128)(2,1)S(1)}, u32[]{:S(2)}, u32[]{:S(2)}) collective-permute-start(bf16[256,128]{1,0:T(8,128)(2,1)S(1)} %copy-done.115), channel_id=1, source_target_pairs={{0,12},{4,8},{8,4},{12,0},{16,28},{20,24},{24,20},{28,16},{1,13},{... | collective-permute-start | bytes 196616 | tf_op jit(solution)/shard_map/ppermute | solution.py:34
  276.1 61.7 %collective-permute-start.49 = (bf16[512,1024]{1,0:T(8,128)(2,1)}, bf16[512,1024]{1,0:T(8,128)(2,1)S(1)}, u32[]{:S(2)}, u32[]{:S(2)}) collective-permute-start(bf16[512,1024]{1,0:T(8,128)(2,1)} %pad_maximum_fusion.8), channel_id=1, source_target_pairs={{0,1},{1,0},{2,3},{3,2},{4,5},{5,4},{6,7},{7,6},{8,9},{9,8},{10,11... | collective-permute-start | bytes 3145736 | tf_op jit(solution)/shard_map/ppermute | solution.py:34
  286.3 23.3 %collective-permute-start.29 = (bf16[256,128]{1,0:T(8,128)(2,1)S(1)}, bf16[256,128]{1,0:T(8,128)(2,1)S(1)}, u32[]{:S(2)}, u32[]{:S(2)}) collective-permute-start(bf16[256,128]{1,0:T(8,128)(2,1)S(1)} %copy-done.114), channel_id=1, source_target_pairs={{0,16},{4,20},{8,24},{12,28},{16,0},{20,4},{24,8},{28,12},{1,17},{... | collective-permute-start | bytes 196616 | tf_op jit(solution)/shard_map/ppermute | solution.py:34
  288.8 21.5 %collective-permute-start.30 = (bf16[256,128]{1,0:T(8,128)(2,1)S(1)}, bf16[256,128]{1,0:T(8,128)(2,1)S(1)}, u32[]{:S(2)}, u32[]{:S(2)}) collective-permute-start(bf16[256,128]{1,0:T(8,128)(2,1)S(1)} %copy-done.113), channel_id=1, source_target_pairs={{0,20},{4,16},{8,28},{12,24},{16,4},{20,0},{24,12},{28,8},{1,21},{... | collective-permute-start | bytes 196616 | tf_op jit(solution)/shard_map/ppermute | solution.py:34
  290.3 21.4 %collective-permute-start.31 = (bf16[256,128]{1,0:T(8,128)(2,1)S(1)}, bf16[256,128]{1,0:T(8,128)(2,1)S(1)}, u32[]{:S(2)}, u32[]{:S(2)}) collective-permute-start(bf16[256,128]{1,0:T(8,128)(2,1)S(1)} %copy-done.112), channel_id=1, source_target_pairs={{0,24},{4,28},{8,16},{12,20},{16,8},{20,12},{24,0},{28,4},{1,25},{... | collective-permute-start | bytes 196616 | tf_op jit(solution)/shard_map/ppermute | solution.py:34
  309.7 37.0 %collective-permute-start.50 = (bf16[512,1024]{1,0:T(8,128)(2,1)}, bf16[512,1024]{1,0:T(8,128)(2,1)S(1)}, u32[]{:S(2)}, u32[]{:S(2)}) collective-permute-start(bf16[512,1024]{1,0:T(8,128)(2,1)} %pad_maximum_fusion.9), channel_id=1, source_target_pairs={{0,2},{1,3},{2,0},{3,1},{4,6},{5,7},{6,4},{7,5},{8,10},{9,11},{10,... | collective-permute-start | bytes 3145736 | tf_op jit(solution)/shard_map/ppermute | solution.py:34
  310.3 74.6 %collective-permute-start.80 = (bf16[256,1024]{1,0:T(8,128)(2,1)}, bf16[256,1024]{1,0:T(8,128)(2,1)}, u32[]{:S(2)}, u32[]{:S(2)}) collective-permute-start(bf16[256,1024]{1,0:T(8,128)(2,1)} %get-tuple-element.217), channel_id=1, source_target_pairs={{0,4},{4,0},{8,12},{12,8},{16,20},{20,16},{24,28},{28,24},{1,5},{5... | collective-permute-start | bytes 1572872 | tf_op jit(solution)/shard_map/ppermute | solution.py:34
  311.7 81.2 %collective-permute-start.71 = (bf16[256,1024]{1,0:T(8,128)(2,1)}, bf16[256,1024]{1,0:T(8,128)(2,1)}, u32[]{:S(2)}, u32[]{:S(2)}) collective-permute-start(bf16[256,1024]{1,0:T(8,128)(2,1)} %get-tuple-element.211), channel_id=1, source_target_pairs={{0,4},{4,0},{8,12},{12,8},{16,20},{20,16},{24,28},{28,24},{1,5},{5... | collective-permute-start | bytes 1572872 | tf_op jit(solution)/shard_map/ppermute | solution.py:34
  312.3 51.6 %collective-permute-start.61 = (bf16[512,1024]{1,0:T(8,128)(2,1)S(1)}, bf16[512,1024]{1,0:T(8,128)(2,1)}, u32[]{:S(2)}, u32[]{:S(2)}) collective-permute-start(bf16[512,1024]{1,0:T(8,128)(2,1)S(1)} %copy-done.19), channel_id=1, source_target_pairs={{0,1},{1,0},{2,3},{3,2},{4,5},{5,4},{6,7},{7,6},{8,9},{9,8},{10,11... | collective-permute-start | bytes 3145736 | tf_op jit(solution)/shard_map/ppermute | solution.py:34
  358.5 30.9 %collective-permute-start.40 = (bf16[528,384]{1,0:T(8,128)(2,1)S(1)}, bf16[528,384]{1,0:T(8,128)(2,1)S(1)}, u32[]{:S(2)}, u32[]{:S(2)}) collective-permute-start(bf16[528,384]{1,0:T(8,128)(2,1)S(1)} %get-tuple-element.261), channel_id=1, source_target_pairs={{0,1},{1,0},{2,3},{3,2},{4,5},{5,4},{6,7},{7,6},{8,9},{9,8},{10,11... | collective-permute-start | bytes 1216520 | tf_op jit(solution)/shard_map/ppermute | solution.py:34
  362.4 67.0 %collective-permute-start.52 = (bf16[384,1024]{1,0:T(8,128)(2,1)}, bf16[384,1024]{1,0:T(8,128)(2,1)S(1)}, u32[]{:S(2)}, u32[]{:S(2)}) collective-permute-start(bf16[384,1024]{1,0:T(8,128)(2,1)} %get-tuple-element.196), channel_id=1, source_target_pairs={{0,4},{4,0},{8,12},{12,8},{16,20},{20,16},{24,28},{28,24},{1,5},{5... | collective-permute-start | bytes 2359304 | tf_op jit(solution)/shard_map/ppermute | solution.py:34
  383.5 39.3 %collective-permute-start.62 = (bf16[256,1024]{1,0:T(8,128)(2,1)}, bf16[256,1024]{1,0:T(8,128)(2,1)S(1)}, u32[]{:S(2)}, u32[]{:S(2)}) collective-permute-start(bf16[256,1024]{1,0:T(8,128)(2,1)} %get-tuple-element.202), channel_id=1, source_target_pairs={{0,4},{4,0},{8,12},{12,8},{16,20},{20,16},{24,28},{28,24},{1,5},{5... | collective-permute-start | bytes 1572872 | tf_op jit(solution)/shard_map/ppermute | solution.py:34
  435.2 29.6 %collective-permute-start.54 = (bf16[96,1024]{1,0:T(8,128)(2,1)}, bf16[96,1024]{1,0:T(8,128)(2,1)S(1)}, u32[]{:S(2)}, u32[]{:S(2)}) collective-permute-start(bf16[96,1024]{1,0:T(8,128)(2,1)} %get-tuple-element.199), channel_id=1, source_target_pairs={{0,16},{4,20},{8,24},{12,28},{16,0},{20,4},{24,8},{28,12},{1,17},{... | collective-permute-start | bytes 589832 | tf_op jit(solution)/shard_map/ppermute | solution.py:34
  436.5 31.8 %collective-permute-start.55 = (bf16[96,1024]{1,0:T(8,128)(2,1)}, bf16[96,1024]{1,0:T(8,128)(2,1)S(1)}, u32[]{:S(2)}, u32[]{:S(2)}) collective-permute-start(bf16[96,1024]{1,0:T(8,128)(2,1)} %get-tuple-element.200), channel_id=1, source_target_pairs={{0,24},{4,28},{8,16},{12,20},{16,8},{20,12},{24,0},{28,4},{1,25},{... | collective-permute-start | bytes 589832 | tf_op jit(solution)/shard_map/ppermute | solution.py:34
  442.8 40.8 %collective-permute-start.43 = (bf16[272,384]{1,0:T(8,128)(2,1)}, bf16[272,384]{1,0:T(8,128)(2,1)S(1)}, u32[]{:S(2)}, u32[]{:S(2)}) collective-permute-start(bf16[272,384]{1,0:T(8,128)(2,1)} %sum_all.9.refs_0_), channel_id=1, source_target_pairs={{0,8},{4,12},{8,0},{12,4},{16,24},{20,28},{24,16},{28,20},{1,9},{5... | collective-permute-start | bytes 626696 | tf_op jit(solution)/shard_map/ppermute | solution.py:34
  442.9 40.7 %collective-permute-start.45 = (bf16[272,384]{1,0:T(8,128)(2,1)}, bf16[272,384]{1,0:T(8,128)(2,1)S(1)}, u32[]{:S(2)}, u32[]{:S(2)}) collective-permute-start(bf16[272,384]{1,0:T(8,128)(2,1)} %sum_all.9.refs_0_), channel_id=1, source_target_pairs={{0,16},{4,20},{8,24},{12,28},{16,0},{20,4},{24,8},{28,12},{1,17},{... | collective-permute-start | bytes 626696 | tf_op jit(solution)/shard_map/ppermute | solution.py:34
  451.0 28.1 %collective-permute-start.76 = (bf16[64,1024]{1,0:T(8,128)(2,1)S(1)}, bf16[64,1024]{1,0:T(8,128)(2,1)S(1)}, u32[]{:S(2)}, u32[]{:S(2)}) collective-permute-start(bf16[64,1024]{1,0:T(8,128)(2,1)S(1)} %copy-done.39), channel_id=1, source_target_pairs={{0,16},{4,20},{8,24},{12,28},{16,0},{20,4},{24,8},{28,12},{1,17},{... | collective-permute-start | bytes 393224 | tf_op jit(solution)/shard_map/ppermute | solution.py:34
  479.1 21.0 %collective-permute-start.67 = (bf16[64,1024]{1,0:T(8,128)(2,1)}, bf16[64,1024]{1,0:T(8,128)(2,1)S(1)}, u32[]{:S(2)}, u32[]{:S(2)}) collective-permute-start(bf16[64,1024]{1,0:T(8,128)(2,1)} %sum_all.13.refs_0_), channel_id=1, source_target_pairs={{0,16},{4,20},{8,24},{12,28},{16,0},{20,4},{24,8},{28,12},{1,17},{... | collective-permute-start | bytes 393224 | tf_op jit(solution)/shard_map/ppermute | solution.py:34
  483.6 23.0 %collective-permute-start.57 = (bf16[96,1024]{1,0:T(8,128)(2,1)}, bf16[96,1024]{1,0:T(8,128)(2,1)S(1)}, u32[]{:S(2)}, u32[]{:S(2)}) collective-permute-start(bf16[96,1024]{1,0:T(8,128)(2,1)} %sum_all.11.refs_0_), channel_id=1, source_target_pairs={{0,16},{4,20},{8,24},{12,28},{16,0},{20,4},{24,8},{28,12},{1,17},{... | collective-permute-start | bytes 589832 | tf_op jit(solution)/shard_map/ppermute | solution.py:34
  483.6 23.0 %collective-permute-start.58 = (bf16[96,1024]{1,0:T(8,128)(2,1)}, bf16[96,1024]{1,0:T(8,128)(2,1)S(1)}, u32[]{:S(2)}, u32[]{:S(2)}) collective-permute-start(bf16[96,1024]{1,0:T(8,128)(2,1)} %sum_all.11.refs_0_), channel_id=1, source_target_pairs={{0,24},{4,28},{8,16},{12,20},{16,8},{20,12},{24,0},{28,4},{1,25},{... | collective-permute-start | bytes 589832 | tf_op jit(solution)/shard_map/ppermute | solution.py:34
  486.1 24.7 %collective-permute-start.68 = (bf16[64,1024]{1,0:T(8,128)(2,1)}, bf16[64,1024]{1,0:T(8,128)(2,1)S(1)}, u32[]{:S(2)}, u32[]{:S(2)}) collective-permute-start(bf16[64,1024]{1,0:T(8,128)(2,1)} %sum_all.13.refs_0_), channel_id=1, source_target_pairs={{0,24},{4,28},{8,16},{12,20},{16,8},{20,12},{24,0},{28,4},{1,25},{... | collective-permute-start | bytes 393224 | tf_op jit(solution)/shard_map/ppermute | solution.py:34
  510.8 76.2 %collective-permute-start.59 = (bf16[384,1024]{1,0:T(8,128)(2,1)}, bf16[384,1024]{1,0:T(8,128)(2,1)S(1)}, u32[]{:S(2)}, u32[]{:S(2)}) collective-permute-start(bf16[384,1024]{1,0:T(8,128)(2,1)} %join.4.a0), channel_id=1, source_target_pairs={{0,4},{4,0},{8,12},{12,8},{16,20},{20,16},{24,28},{28,24},{1,5},{5... | collective-permute-start | bytes 2359304 | tf_op jit(solution)/shard_map/ppermute | solution.py:34
  518.1 64.5 %collective-permute-start.87 = (bf16[256,1024]{1,0:T(8,128)(2,1)S(1)}, bf16[256,1024]{1,0:T(8,128)(2,1)S(1)}, u32[]{:S(2)}, u32[]{:S(2)}) collective-permute-start(bf16[256,1024]{1,0:T(8,128)(2,1)S(1)} %copy-done.16), channel_id=1, source_target_pairs={{0,4},{4,0},{8,12},{12,8},{16,20},{20,16},{24,28},{28,24},{1,5},{5... | collective-permute-start | bytes 1572872 | tf_op jit(solution)/shard_map/ppermute | solution.py:34
  519.5 63.1 %collective-permute-start.78 = (bf16[256,1024]{1,0:T(8,128)(2,1)}, bf16[256,1024]{1,0:T(8,128)(2,1)S(1)}, u32[]{:S(2)}, u32[]{:S(2)}) collective-permute-start(bf16[256,1024]{1,0:T(8,128)(2,1)} %join.6.refs_0_), channel_id=1, source_target_pairs={{0,4},{4,0},{8,12},{12,8},{16,20},{20,16},{24,28},{28,24},{1,5},{5... | collective-permute-start | bytes 1572872 | tf_op jit(solution)/shard_map/ppermute | solution.py:34
  520.2 42.8 %collective-permute-start.48 = (bf16[272,384]{1,0:T(8,128)(2,1)S(1)}, bf16[272,384]{1,0:T(8,128)(2,1)S(1)}, u32[]{:S(2)}, u32[]{:S(2)}) collective-permute-start(bf16[272,384]{1,0:T(8,128)(2,1)S(1)} %collective-permute-done.47.refs_6_), channel_id=1, source_target_pairs={{0,4},{4,0},{8,12},{12,8},{16,20},{20,16},{24,28},{28,24},{1,5},{5... | collective-permute-start | bytes 626696 | tf_op jit(solution)/shard_map/ppermute | solution.py:34
  521.6 63.4 %collective-permute-start.69 = (bf16[256,1024]{1,0:T(8,128)(2,1)}, bf16[256,1024]{1,0:T(8,128)(2,1)S(1)}, u32[]{:S(2)}, u32[]{:S(2)}) collective-permute-start(bf16[256,1024]{1,0:T(8,128)(2,1)} %join.5.b0), channel_id=1, source_target_pairs={{0,4},{4,0},{8,12},{12,8},{16,20},{20,16},{24,28},{28,24},{1,5},{5... | collective-permute-start | bytes 1572872 | tf_op jit(solution)/shard_map/ppermute | solution.py:34
  582.6 22.4 %collective-permute-start.36 = (bf16[256,384]{1,0:T(8,128)(2,1)}, bf16[256,384]{1,0:T(8,128)(2,1)S(1)}, u32[]{:S(2)}, u32[]{:S(2)}) collective-permute-start(bf16[256,384]{1,0:T(8,128)(2,1)} %get-tuple-element.183), channel_id=1, source_target_pairs={{0,16},{4,20},{8,24},{12,28},{16,0},{20,4},{24,8},{28,12},{1,17},{... | collective-permute-start | bytes 589832 | tf_op jit(solution)/shard_map/ppermute | solution.py:34
  582.6 26.4 %collective-permute-start.37 = (bf16[256,384]{1,0:T(8,128)(2,1)}, bf16[256,384]{1,0:T(8,128)(2,1)S(1)}, u32[]{:S(2)}, u32[]{:S(2)}) collective-permute-start(bf16[256,384]{1,0:T(8,128)(2,1)} %get-tuple-element.184), channel_id=1, source_target_pairs={{0,20},{4,16},{8,28},{12,24},{16,4},{20,0},{24,12},{28,8},{1,21},{... | collective-permute-start | bytes 589832 | tf_op jit(solution)/shard_map/ppermute | solution.py:34
  585.0 24.1 %collective-permute-start.38 = (bf16[256,384]{1,0:T(8,128)(2,1)}, bf16[256,384]{1,0:T(8,128)(2,1)}, u32[]{:S(2)}, u32[]{:S(2)}) collective-permute-start(bf16[256,384]{1,0:T(8,128)(2,1)} %get-tuple-element.185), channel_id=1, source_target_pairs={{0,24},{4,28},{8,16},{12,20},{16,8},{20,12},{24,0},{28,4},{1,25},{... | collective-permute-start | bytes 589832 | tf_op jit(solution)/shard_map/ppermute | solution.py:34
  587.0 22.0 %collective-permute-start.39 = (bf16[256,384]{1,0:T(8,128)(2,1)}, bf16[256,384]{1,0:T(8,128)(2,1)}, u32[]{:S(2)}, u32[]{:S(2)}) collective-permute-start(bf16[256,384]{1,0:T(8,128)(2,1)} %get-tuple-element.186), channel_id=1, source_target_pairs={{0,28},{4,24},{8,20},{12,16},{16,12},{20,8},{24,4},{28,0},{1,29},{... | collective-permute-start | bytes 589832 | tf_op jit(solution)/shard_map/ppermute | solution.py:34
  (167 other events, 2371.4 us)
Sparse Core Ops, SparseCore 0:
  165.0 65.7 all-gather.1

commit v2 on v1

v2 whole, which is shorter than its diff:
```python
import functools

import jax
import jax.numpy as jnp
from jax import lax
from jax.experimental import pallas as pl
from jax.experimental.pallas import tpu as pltpu
from jax.sharding import PartitionSpec as P

HEADS = 16
LANES = 128
epsilon = 1e-05
masked_value = -1e30
query_scale = 0.125
bf16 = jnp.bfloat16
f32 = jnp.float32
vmem_limit = 28 * 1024 * 1024


def matmul(left, right):
    return jnp.dot(left, right, preferred_element_type=f32)


def left_transposed(left, right):
    return lax.dot_general(left, right, (((0,), (0,)), ((), ())), preferred_element_type=f32)


def right_transposed(left, right):
    return lax.dot_general(left, right, (((1,), (1,)), ((), ())), preferred_element_type=f32)


def swap(array, axis, mask):
    size = lax.axis_size(axis)
    return lax.ppermute(array, axis, [(i, i ^ mask) for i in range(size)])


def shape(*sizes, dtype=f32):
    return jax.ShapeDtypeStruct(sizes, dtype)


class Order:
    last = ()


def call(
    body, name, out_shape, operands, scalars=None, scratch=(), aliases=None, deps=(), limit=vmem_limit, **grid
):
    count = 0 if scalars is None else 1
    several = isinstance(out_shape, (list, tuple))
    if not grid:
        whole = pl.BlockSpec(memory_space=pltpu.VMEM)
        grid = dict(
            grid=(),
            in_specs=[whole] * len(operands),
            out_specs=[whole] * len(out_shape) if several else whole,
        )
    extra = [*Order.last, *deps]
    first = count + len(operands)
    grid["in_specs"] = list(grid["in_specs"]) + [pl.BlockSpec(memory_space=pl.ANY)] * len(extra)

    def ordered(*refs):
        body(*refs[:first], *refs[first + len(extra) :])

    result = pl.pallas_call(
        ordered,
        out_shape=out_shape,
        grid_spec=pltpu.PrefetchScalarGridSpec(
            num_scalar_prefetch=count, scratch_shapes=list(scratch), **grid
        ),
        input_output_aliases=aliases or {},
        compiler_params=pltpu.CompilerParams(vmem_limit_bytes=limit),
        cost_estimate=pl.CostEstimate(flops=1, bytes_accessed=1, transcendentals=0),
        name=name,
    )(*([] if scalars is None else [scalars]), *operands, *extra)
    Order.last = (result[0] if several else result,)
    return result


def aligned(index, size):
    return pl.ds(pl.multiple_of(index * size, size), size)


def gather_ctx(own):
    size = lax.axis_size("ctx")
    masks = [1 << i for i in range(size.bit_length() - 1)]
    blocks = {0: own}
    for mask in reversed(masks[1:]):
        for index in list(blocks):
            blocks[index | mask] = swap(blocks[index], "ctx", mask)
    for index in list(blocks):
        if index != 2:
            blocks[index | 1] = swap(blocks[index], "ctx", 1)
    blocks[3] = swap(blocks[1], "ctx", 2)
    return [blocks[i] for i in range(len(blocks))]


def exchange(array, number):
    size = lax.axis_size("ctx")
    if number == size:
        return lax.all_to_all(array, "ctx", 0, 0, tiled=True)
    rows = array.shape[0] // number
    own = lax.axis_index("ctx").astype(jnp.int32) & (number - 1)
    result = jnp.zeros_like(array)
    for i in range(number):
        block = lax.dynamic_slice_in_dim(array, (own ^ i) * rows, rows, 0)
        block = block if i == 0 else swap(block, "ctx", i)
        result = lax.dynamic_update_slice_in_dim(result, block, (own ^ i) * rows, 0)
    return result


def ctx_groups():
    return [(bit, 2) for bit in range(lax.axis_size("ctx").bit_length() - 1)]


def piece_of(index, size):
    bits = size.bit_length() - 1
    piece = 0
    for bit in range(bits):
        piece = piece | (((index >> bit) & 1) << (bits - 1 - bit))
    return piece


def sum_split(segments, members, place, rows, deps):
    width = segments[0][0][0].shape[1]
    size = rows // members
    number = sum(len(arrays) for arrays, _, _ in segments)

    def body(place_ref, *refs):
        ins, outs, total = refs[:number], refs[number:-1], refs[-1]
        first = at = 0
        for arrays, begin, end in segments:
            value = ins[at][begin:end, :].astype(f32)
            for ref in ins[at + 1 : at + len(arrays)]:
                value = value + ref[begin:end, :].astype(f32)
            total[first : first + end - begin, :] = value.astype(bf16)
            first += end - begin
            at += len(arrays)
        if first < rows:
            total[first:, :] = jnp.zeros((rows - first, width), bf16)
        for m in range(members):
            outs[m][...] = total[aligned(place_ref[0] ^ m, size), :]

    return call(
        body,
        "sum_split",
        [shape(size, width, dtype=bf16)] * members,
        [array for arrays, _, _ in segments for array in arrays],
        deps=deps,
        scalars=place.reshape(1),
        scratch=[pltpu.VMEM((rows, width), bf16)],
    )


def sum_all(arrays, dtype=bf16):
    def body(*refs):
        value = refs[0][...].astype(f32)
        for ref in refs[1:-1]:
            value = value + ref[...].astype(f32)
        refs[-1][...] = value.astype(dtype)

    return call(body, "sum_all", shape(*arrays[0].shape, dtype=dtype), arrays)


class CtxSum:
    def __init__(self, groups, *segments):
        self.index = lax.axis_index("ctx").astype(jnp.int32)
        self.groups = list(groups)
        self.segments = segments
        unit = 16
        for _, members in groups:
            unit *= members
        self.rows = -(-sum(end - begin for _, begin, end in segments) // unit) * unit

    def step(self, deps=()):
        if not self.groups:
            return
        first, members = self.groups.pop(0)
        place = (self.index >> first) & (members - 1)
        pieces = sum_split(self.segments, members, place, self.rows, deps)
        self.rows //= members
        arrays = [pieces[0]] + [swap(pieces[m], "ctx", m << first) for m in range(1, members)]
        self.segments = [(arrays, 0, self.rows)]

    def finish(self):
        while self.groups:
            self.step()
        return self.segments[0][0]


def place_rows(gathered, size):
    rows, width = gathered.shape

    def body(in_ref, out_ref):
        out_ref[...] = in_ref[...].astype(f32)

    return call(
        body,
        "place_rows",
        shape(rows, width),
        [gathered],
        grid=(size,),
        in_specs=[pl.BlockSpec((rows // size, width), lambda p: (piece_of(p, size), 0))],
        out_specs=pl.BlockSpec((rows // size, width), lambda p: (p, 0)),
    )


def place_expand(gathered, f, shard, size):
    rows, columns = gathered.shape
    piece = rows // size

    def body(f_ref, in_ref, expand_ref, output_ref, *refs):
        outs, ordered, small = refs[:-2], refs[-2], refs[-1]
        for j in range(size):
            at = piece_of(j, size) * piece
            ordered[at : at + piece, :] = in_ref[j * piece : (j + 1) * piece, :]
        for unit, k in enumerate((0, 2, 1, 3)):
            expand_ref[:, aligned(f_ref[0] ^ k, columns)] = ordered[
                unit * shard : (unit + 1) * shard, :
            ].astype(f32)
        output_ref[...] = ordered[4 * shard : 5 * shard, :].astype(f32)
        small[...] = ordered[5 * shard : 5 * shard + 16, :].astype(f32)
        for k in range(6):
            outs[k][...] = small[k : k + 1, aligned(f_ref[0], shard)]
        outs[6][...] = small[pl.ds(8 + f_ref[0], 1), :]

    return call(
        body,
        "place_expand",
        [shape(shard, 4 * columns), shape(shard, columns)]
        + [shape(1, shard)] * 6
        + [shape(1, columns)],
        [gathered],
        scalars=f.reshape(1),
        scratch=[pltpu.VMEM((rows, columns), bf16), pltpu.VMEM((16, columns), f32)],
    )


def cast_feed(expand, reduce):
    shard, columns = expand.shape
    block = columns // 4

    def body(e_ref, r_ref, out_ref):
        at = pl.program_id(0)

        @pl.when(at < 4)
        def _():
            out_ref[...] = e_ref[...].astype(bf16)

        @pl.when(at >= 4)
        def _():
            out_ref[...] = r_ref[...].astype(bf16)

    return call(
        body,
        "cast_feed",
        shape(4 * shard + reduce.shape[0], block, dtype=bf16),
        [expand, reduce],
        grid=(8,),
        in_specs=[
            pl.BlockSpec((shard, block), lambda i: (0, jnp.minimum(i, 3))),
            pl.BlockSpec((reduce.shape[0] // 4, block), lambda i: (jnp.maximum(i - 4, 0), 0)),
        ],
        out_specs=pl.BlockSpec((shard, block), lambda i: (i, 0)),
    )


def cast_all(matrix, deps=()):
    rows, columns = matrix.shape
    tile = min(rows, 256)

    def body(in_ref, out_ref):
        out_ref[...] = in_ref[...].astype(bf16)

    spec = pl.BlockSpec((tile, columns), lambda i: (i, 0))
    return call(
        body,
        "cast_all",
        shape(rows, columns, dtype=bf16),
        [matrix],
        deps=deps,
        grid=(rows // tile,),
        in_specs=[spec],
        out_specs=spec,
    )


def reduce_gradient(activated, own, sibling, half, deps=()):
    rows, columns = activated.shape
    tokens, model = own.shape
    tile = columns // 4

    def body(h_ref, a_ref, d_ref, s_ref, out_ref):
        value = left_transposed(a_ref[:tokens, :], d_ref[...])
        out_ref[...] = (value + left_transposed(a_ref[tokens:, :], s_ref[...])).astype(bf16)

    whole = pl.BlockSpec((tokens, model), lambda i, s: (0, 0))
    return call(
        body,
        "reduce_gradient",
        shape(columns // 2, model, dtype=bf16),
        [activated, own, sibling],
        deps=deps,
        scalars=half.reshape(1),
        grid=(2,),
        in_specs=[pl.BlockSpec((rows, tile), lambda i, s: (0, 2 * i + s[0])), whole, whole],
        out_specs=pl.BlockSpec((tile, model), lambda i, s: (i, 0)),
    )


def expand_gradients(own, sibling, d_expanded, f, row_blocks, flip, shard):
    tokens, model = own.shape
    columns = d_expanded.shape[1] // 2

    def body(f_ref, a_ref, b_ref, d_ref, out_ref):
        value = left_transposed(a_ref[...], d_ref[:tokens, :])
        out_ref[...] = (value + left_transposed(b_ref[...], d_ref[tokens:, :])).astype(bf16)

    def rows_map(i, s):
        return (0, s[0] ^ jnp.where(i < 2, row_blocks[0], row_blocks[1]))

    left = pl.BlockSpec((tokens, shard), rows_map)
    return call(
        body,
        "expand_gradients",
        shape(4 * shard, columns, dtype=bf16),
        [own, sibling, d_expanded],
        scalars=f.reshape(1),
        grid=(4,),
        in_specs=[left, left, pl.BlockSpec((2 * tokens, columns), lambda i, s: (0, (i % 2) ^ flip))],
        out_specs=pl.BlockSpec((shard, columns), lambda i, s: (i, 0)),
    )


def output_gradient(attended, d_attention, first_sums, second_sums, bias_sums, f, shard):
    model = d_attention.shape[1]
    tile = 256
    steps = model // tile

    def body(s_ref, a_ref, d_ref, first_ref, second_ref, bias_ref, keep_ref, send_ref, rows, small):
        step = pl.program_id(0)
        rows[aligned(step, tile), :] = left_transposed(a_ref[...], d_ref[...]).astype(bf16)

        @pl.when(step == steps - 1)
        def _():
            small[...] = jnp.zeros_like(small)
            small[0:3, :] = first_ref[0:3, :]
            small[3:6, :] = second_ref[0:3, :]
            for k in range(2):
                small[pl.ds(8 + (s_ref[0] ^ (2 * k)), 1), :] = bias_ref[
                    :, k * model : (k + 1) * model
                ]
            for out_ref, blocks in ((keep_ref, (0, 2)), (send_ref, (1, 3))):
                for k, block in enumerate(blocks):
                    out_ref[k * shard : (k + 1) * shard, :] = rows[
                        aligned(s_ref[0] ^ block, shard), :
                    ]
                out_ref[2 * shard :, :] = small[...].astype(bf16)

    total = 2 * shard + 16
    whole = pl.BlockSpec((total, model), lambda i, s: (0, 0))
    return call(
        body,
        "output_gradient",
        [shape(total, model, dtype=bf16)] * 2,
        [attended, d_attention, first_sums, second_sums, bias_sums],
        scalars=f.reshape(1),
        scratch=[pltpu.VMEM((model, model), bf16), pltpu.VMEM((16, model), f32)],
        grid=(steps,),
        in_specs=[pl.BlockSpec((attended.shape[0], tile), lambda i, s: (0, i))]
        + [
            pl.BlockSpec(array.shape, lambda i, s: (0, 0))
            for array in (d_attention, first_sums, second_sums, bias_sums)
        ],
        out_specs=[whole, whole],
    )


def add_parts(first, second, parts):
    width = first.shape[1]

    def body(a_ref, b_ref, *outs):
        for out_ref, ranges in zip(outs, parts):
            at = 0
            for begin, end in ranges:
                value = a_ref[begin:end, :].astype(f32) + b_ref[begin:end, :].astype(f32)
                out_ref[at : at + end - begin, :] = value.astype(bf16)
                at += end - begin

    return call(
        body,
        "add_parts",
        [shape(sum(e - b for b, e in ranges), width, dtype=bf16) for ranges in parts],
        [first, second],
    )


def projection_gradients(stream, d_all, f, shard):
    rows, width = d_all.shape
    model = stream.shape[1]
    tile = 512
    steps = rows // tile

    def body(f_ref, x_ref, d_ref, send_ref, keep_ref, total, sums, rounded):
        step = pl.program_id(0)

        @pl.when(step == 0)
        def _():
            total[...] = jnp.zeros_like(total)
            sums[...] = jnp.zeros_like(sums)

        d_value = d_ref[...]
        total[...] += left_transposed(x_ref[...], d_value)
        sums[...] += jnp.sum(d_value.astype(f32), axis=0, keepdims=True)

        @pl.when(step == steps - 1)
        def _():
            lane = lax.broadcasted_iota(jnp.int32, (1, width), 1)
            scale = jnp.where(lane < width // 3, query_scale, 1.0)
            rounded[...] = (total[...] * scale).astype(bf16)
            bias = jnp.broadcast_to(sums[...] * scale, (16, width)).astype(bf16)
            for out_ref, blocks in ((send_ref, (3, 1)), (keep_ref, (2, 0))):
                for k, block in enumerate(blocks):
                    out_ref[k * shard : (k + 1) * shard, :] = rounded[
                        aligned(f_ref[0] ^ block, shard), :
                    ]
                out_ref[2 * shard :, :] = bias

    out = shape(2 * shard + 16, width, dtype=bf16)
    whole = pl.BlockSpec((2 * shard + 16, width), lambda i, s: (0, 0))
    return call(
        body,
        "projection_gradients",
        [out, out],
        [stream, d_all],
        scalars=f.reshape(1),
        scratch=[
            pltpu.VMEM((model, width), f32),
            pltpu.VMEM((1, width), f32),
            pltpu.VMEM((model, width), bf16),
        ],
        grid=(steps,),
        in_specs=[
            pl.BlockSpec((tile, model), lambda i, s: (i, 0)),
            pl.BlockSpec((tile, width), lambda i, s: (i, 0)),
        ],
        out_specs=[whole, whole],
    )


def place_projections(gathered, f, count, width, shard):
    rows = gathered.shape[0] // count

    def body(f_ref, in_ref, *refs):
        outs, sums = refs[:-1], refs[-1]
        for j in range(count):
            where = slice(j * width, (j + 1) * width)
            for k in range(3):
                cut = slice(k * width, (k + 1) * width)
                outs[k][:, where] = in_ref[j * rows : j * rows + shard, cut].astype(f32)
                sums[k : k + 1, where] = in_ref[j * rows + shard : (j + 1) * rows, cut].astype(f32)[
                    0:1, :
                ]
        for k, row in ((3, 0), (4, 2)):
            outs[k][...] = sums[row : row + 1, aligned(f_ref[0], shard)]

    return call(
        body,
        "place_projections",
        [shape(shard, count * width)] * 3 + [shape(1, shard)] * 2,
        [gathered],
        scalars=f.reshape(1),
        scratch=[pltpu.VMEM((8, count * width), f32)],
    )


def project(blocks, first, weights, bias, query_docs, key_docs, own, heads, head_size, length, before, deps):
    tokens, model = blocks[0].shape
    width = heads * head_size
    shard = weights[0].shape[0]
    number = len(blocks)
    rows = number * tokens
    tile = 256
    per_block = tokens // tile
    start = first * per_block

    def body(own_ref, *refs):
        x_refs, w_refs = refs[:number], refs[number : number + 4]
        b_ref, qd_ref, kd_ref = refs[number + 4 : number + 7]
        q_ref, k_ref, v_ref, kt_ref, x_out = refs[-5:]
        for k in range(number):

            @pl.when(pl.program_id(0) // per_block == k)
            def _():
                x_out[...] = x_refs[k][...]

        product = b_ref[...]
        for k in range(4):
            product = product + matmul(x_out[:, aligned(own_ref[0] ^ k, shard)], w_refs[k][...])
        lane = lax.broadcasted_iota(jnp.int32, (tile, LANES - head_size), 1)
        ones = jnp.where(lane < 3, 1.0, 0.0).astype(f32)
        keys = product[:, width : 2 * width]
        for h in range(heads):
            cut = slice(h * head_size, (h + 1) * head_size)
            q_ref[h] = jnp.concatenate((product[:, :width][:, cut], qd_ref[...]), 1).astype(bf16)
            k_ref[h] = jnp.concatenate((keys[:, cut], kd_ref[...]), 1).astype(bf16)
            v_ref[h] = jnp.concatenate((product[:, 2 * width :][:, cut], ones), 1).astype(bf16)
        kt_ref[...] = jnp.transpose(keys).astype(bf16)

    out = shape(heads, length, LANES, dtype=bf16)
    out_spec = pl.BlockSpec((heads, tile, LANES), lambda i, s: (0, i + start, 0))
    extra_spec = pl.BlockSpec((tile, LANES - head_size), lambda i, s: (i + start, 0))
    old = list(before) if before is not None else []

    def block_map(k, i, s):
        return (jnp.clip(i - k * per_block, 0, per_block - 1), 0)

    operands = [*blocks, *weights, bias, query_docs, key_docs, *old]
    return call(
        body,
        "project",
        [out, out, out, shape(width, length, dtype=bf16), shape(length, model, dtype=bf16)],
        operands,
        scalars=own.reshape(1),
        deps=deps,
        aliases={1 + len(operands) - 5 + k: k for k in range(5)} if old else None,
        grid=(rows // tile,),
        in_specs=[pl.BlockSpec((tile, model), functools.partial(block_map, k)) for k in range(number)]
        + [pl.BlockSpec((shard, 3 * width), lambda i, s: (0, 0))] * 4
        + [pl.BlockSpec((1, 3 * width), lambda i, s: (0, 0)), extra_spec, extra_spec]
        + [pl.BlockSpec(memory_space=pl.ANY)] * len(old),
        out_specs=[
            out_spec,
            out_spec,
            out_spec,
            pl.BlockSpec((width, tile), lambda i, s: (0, i + start)),
            pl.BlockSpec((tile, model), lambda i, s: (i + start, 0)),
        ],
    )


def three_parts(value):
    high = value.astype(bf16).astype(f32)
    rest = value - high
    middle = rest.astype(bf16).astype(f32)
    return high, middle, rest - middle


def attend(queries, keys, values, group, number, tokens, head_size, docs, deps):
    heads, length, _ = keys.shape
    width = heads * head_size
    tile = 256 if length <= 4096 else 128
    per = tokens // tile
    rows = number * tokens

    def body(s_ref, q_ref, k_ref, v_ref, out_ref, wide_ref, back_ref):
        lane = lax.broadcasted_iota(jnp.int32, (tile, LANES), 1)
        for h in range(heads):
            query = q_ref[h]
            scores = right_transposed(query, k_ref[h])
            largest = jnp.max(scores, axis=1, keepdims=True)
            weights = jnp.exp(scores - largest).astype(bf16)
            summed = matmul(weights, v_ref[h])
            total = summed[:, head_size : head_size + 1]
            cut = slice(h * head_size, (h + 1) * head_size)
            attended = summed[:, :head_size] / total
            wide_ref[:, cut] = attended
            out_ref[:, cut] = attended.astype(bf16)
            parts = three_parts(-(largest + jnp.log(total)))
            back = query.astype(f32)
            for k in range(3):
                back = jnp.where(lane == head_size + docs + k, parts[k], back)
            back_ref[h] = back.astype(bf16)

    return call(
        body,
        "attend",
        [
            shape(rows, width, dtype=bf16),
            shape(rows, width),
            shape(heads, rows, LANES, dtype=bf16),
        ],
        [queries, keys, values],
        deps=deps,
        scalars=group.reshape(1),
        grid=(rows // tile,),
        in_specs=[
            pl.BlockSpec((heads, tile, LANES), lambda i, s: (0, i, 0)),
            pl.BlockSpec((heads, length, LANES), lambda i, s: (0, 0, 0)),
            pl.BlockSpec((heads, length, LANES), lambda i, s: (0, 0, 0)),
        ],
        out_specs=[
            pl.BlockSpec((tile, width), lambda i, s: (((i // per) ^ s[0]) * per + i % per, 0)),
            pl.BlockSpec((tile, width), lambda i, s: (i, 0)),
            pl.BlockSpec((heads, tile, LANES), lambda i, s: (0, i, 0)),
        ],
    )


def attend_back(queries, douts, attended, keys, values, keys_t, head_size, tokens, group):
    heads, length, _ = keys.shape
    rows = attended.shape[0]
    width = heads * head_size
    tile = 256 if length <= 4096 else 128
    per = tokens // tile

    def body(s_ref, q_ref, d_ref, a_ref, k_ref, v_ref, kt_ref, dq_ref, dk_ref, dv_ref):
        @pl.when(pl.program_id(0) == 0)
        def _():
            dk_ref[...] = jnp.zeros_like(dk_ref)
            dv_ref[...] = jnp.zeros_like(dv_ref)

        lane = lax.broadcasted_iota(jnp.int32, (tile, LANES - head_size), 1)
        for h in range(heads):
            cut = slice(h * head_size, (h + 1) * head_size)
            dout = d_ref[:, cut].astype(f32)
            parts = three_parts(-jnp.sum(dout * a_ref[:, cut], axis=1, keepdims=True))
            extra = jnp.zeros((tile, LANES - head_size), f32)
            for k in range(3):
                extra = jnp.where(lane == k, parts[k], extra)
            dout = jnp.concatenate((dout, extra), axis=1).astype(bf16)
            query = q_ref[h]
            probabilities = jnp.exp(right_transposed(k_ref[h], query))
            grads = right_transposed(v_ref[h], dout)
            d_scores = (probabilities * grads).astype(bf16)
            dk_ref[:, cut] += matmul(d_scores, query)[:, :head_size]
            dv_ref[:, cut] += matmul(probabilities.astype(bf16), dout)[:, :head_size]
            dq_t = matmul(kt_ref[cut, :], d_scores)
            dq_ref[:, cut] = jnp.transpose(dq_t).astype(bf16)

    whole = pl.BlockSpec((length, width), lambda i, s: (0, 0))
    resident = pl.BlockSpec((heads, length, LANES), lambda i, s: (0, 0, 0))

    def dout_map(i, s):
        return (((i // per) ^ s[0]) * per + i % per, 0)

    in_specs = [
        pl.BlockSpec((heads, tile, LANES), lambda i, s: (0, i, 0)),
        pl.BlockSpec((tile, width), dout_map),
        pl.BlockSpec((tile, width), lambda i, s: (i, 0)),
        resident,
        resident,
        pl.BlockSpec((width, length), lambda i, s: (0, 0)),
    ]
    operands = [queries, douts, attended, keys, values, keys_t]
    return call(
        body,
        "attend_back",
        [shape(rows, width, dtype=bf16), shape(length, width), shape(length, width)],
        operands,
        scalars=group.reshape(1),
        limit=vmem_limit if length <= 4096 else 2 * vmem_limit,
        grid=(rows // tile,),
        in_specs=in_specs,
        out_specs=[pl.BlockSpec((tile, width), lambda i, s: (i, 0)), whole, whole],
    )


def head_grads(d_queries, d_key, d_value, tokens, number, group):
    width = d_key.shape[1]
    count = len(d_queries)
    rows = number * tokens

    def body(s_ref, *refs):
        dk_ref, dv_ref, all_ref, send_ref = refs[count:]
        first = 0
        for ref in refs[:count]:
            all_ref[first : first + ref.shape[0], :width] = ref[...]
            first += ref.shape[0]
        all_ref[:, width : 2 * width] = dk_ref[:rows, :].astype(bf16)
        all_ref[:, 2 * width :] = dv_ref[:rows, :].astype(bf16)
        for k in range(number):
            send_ref[aligned(s_ref[0] ^ k, tokens), :] = all_ref[k * tokens : (k + 1) * tokens, :]

    return call(
        body,
        "head_grads",
        [shape(rows, 3 * width, dtype=bf16)] * 2,
        [*d_queries, d_key, d_value],
        scalars=group.reshape(1),
    )


def lane_copy(value):
    return jnp.broadcast_to(value, (value.shape[0], LANES))


def attention_norm(received, weights, inputs, vectors, f, number):
    tokens, model = inputs.shape
    shard = weights[0].shape[0]
    width = received.shape[1]

    def body(f_ref, p_ref, *refs):
        w_refs = refs[:4]
        x_ref, v_ref = refs[4:6]
        normed_ref, rounded_ref, unit_ref, inverse_ref, all_ref, matrix = refs[6:]
        for k in range(4):
            matrix[aligned(f_ref[0] ^ k, shard), :] = w_refs[k][...]
        for j in range(number):
            all_ref[:, j * width : (j + 1) * width] = p_ref[j * tokens : (j + 1) * tokens, :]
        value = x_ref[...] + v_ref[0:1, :] + matmul(all_ref[...], matrix[...])
        average = jnp.mean(value, axis=-1, keepdims=True)
        centered = value - average
        inverse = lax.rsqrt(jnp.mean(centered * centered, axis=-1, keepdims=True) + epsilon)
        unit = centered * inverse
        normed = unit * v_ref[1:2, :] + v_ref[2:3, :]
        normed_ref[...] = normed
        rounded_ref[...] = normed.astype(bf16)
        unit_ref[...] = unit
        inverse_ref[...] = lane_copy(inverse)

    return call(
        body,
        "attention_norm",
        [
            shape(tokens, model),
            shape(tokens, model, dtype=bf16),
            shape(tokens, model),
            shape(tokens, LANES),
            shape(tokens, model, dtype=bf16),
        ],
        [received, *weights, inputs, vectors],
        scalars=f.reshape(1),
        scratch=[pltpu.VMEM((model, model), bf16)],
    )


def feed_specs(shard, model):
    tile = 2 * shard

    def block(t, s):
        return s[0] ^ (2 * (t // 2))

    specs = [
        pl.BlockSpec((shard, tile), lambda t, s, k=k: (8 * k + block(t, s), t % 2)) for k in range(4)
    ]
    specs.append(pl.BlockSpec((tile, model), lambda t, s: (4 * block(t, s) + 2 + t % 2, 0)))
    return specs, lambda t, s: 2 * block(t, s) + t % 2


def feed_forward(own, sibling, matrix, bias, f):
    tokens, model = own.shape
    shard = model // 4
    tile = 2 * shard

    def body(f_ref, a_ref, b_ref, *refs):
        w_refs, r_ref, bias_ref = refs[:4], refs[4], refs[5]
        act_ref, slope_ref, own_ref, other_ref, x_all = refs[6:]

        @pl.when(pl.program_id(0) == 0)
        def _():
            x_all[:tokens, :] = a_ref[...]
            x_all[tokens:, :] = b_ref[...]
            own_ref[...] = jnp.zeros_like(own_ref)
            other_ref[...] = jnp.zeros_like(other_ref)

        value = bias_ref[...]
        for k in range(4):
            value = value + matmul(x_all[:, k * shard : (k + 1) * shard], w_refs[k][...])
        below = 0.5 + 0.5 * lax.erf(value * 0.7071067811865476)
        density = 0.3989422804014327 * jnp.exp(-0.5 * value * value)
        activated = (value * below).astype(bf16)
        act_ref[...] = activated
        slope_ref[...] = (below + value * density).astype(bf16)
        own_ref[...] += matmul(activated[:tokens], r_ref[...])
        other_ref[...] += matmul(activated[tokens:], r_ref[...])

    specs, column = feed_specs(shard, model)
    wide = shape(2 * tokens, 4 * tile, dtype=bf16)
    whole = pl.BlockSpec((tokens, model), lambda t, s: (0, 0))
    return call(
        body,
        "feed_forward",
        [wide, wide, shape(tokens, model), shape(tokens, model)],
        [own, sibling, *[matrix] * 5, bias],
        scalars=f.reshape(1),
        limit=2 * vmem_limit,
        scratch=[pltpu.VMEM((2 * tokens, model), bf16)],
        grid=(4,),
        in_specs=[whole, whole, *specs, pl.BlockSpec((1, tile), lambda t, s: (0, column(t, s)))],
        out_specs=[pl.BlockSpec((2 * tokens, tile), lambda t, s: (0, t))] * 2 + [whole, whole],
    )


def second_norm(normed, own, received, vectors, cotangent):
    tokens, model = normed.shape
    tile = 64

    def body(n_ref, p_ref, r_ref, v_ref, c_ref, out_ref, d_ref, rounded_ref, sums_ref):
        value = n_ref[...] + p_ref[...] + r_ref[...] + v_ref[0:1, :]
        average = jnp.mean(value, axis=-1, keepdims=True)
        centered = value - average
        inverse = lax.rsqrt(jnp.mean(centered * centered, axis=-1, keepdims=True) + epsilon)
        unit = centered * inverse
        out_ref[...] = unit * v_ref[1:2, :] + v_ref[2:3, :]
        dy = c_ref[...]
        dz = dy * v_ref[1:2, :]
        mean_dz = jnp.mean(dz, axis=-1, keepdims=True)
        mean_dzz = jnp.mean(dz * unit, axis=-1, keepdims=True)
        result = inverse * (dz - mean_dz - unit * mean_dzz)
        d_ref[...] = result
        rounded = result.astype(bf16)
        rounded_ref[...] = rounded

        @pl.when(pl.program_id(0) == 0)
        def _():
            sums_ref[...] = jnp.zeros_like(sums_ref)

        sums_ref[0:1, :] += jnp.sum(dy * unit, axis=0, keepdims=True)
        sums_ref[1:2, :] += jnp.sum(dy, axis=0, keepdims=True)
        sums_ref[2:3, :] += jnp.sum(rounded.astype(f32), axis=0, keepdims=True)

    rows = pl.BlockSpec((tile, model), lambda i: (i, 0))
    fixed = pl.BlockSpec((8, model), lambda i: (0, 0))
    return call(
        body,
        "second_norm",
        [shape(tokens, model), shape(tokens, model), shape(tokens, model, dtype=bf16), shape(8, model)],
        [normed, own, received, vectors, cotangent],
        grid=(tokens // tile,),
        in_specs=[rows, rows, rows, fixed, rows],
        out_specs=[rows, rows, rows, fixed],
    )


def feed_back(own, sibling, slope, matrix, f):
    tokens, model = own.shape
    shard = model // 4
    tile = 2 * shard

    def body(f_ref, a_ref, b_ref, slope_ref, *refs):
        w_refs, r_ref = refs[:4], refs[4]
        de_ref, sums_ref, own_ref, other_ref, d_all = refs[5:]

        @pl.when(pl.program_id(0) == 0)
        def _():
            d_all[:tokens, :] = a_ref[...]
            d_all[tokens:, :] = b_ref[...]
            own_ref[...] = jnp.zeros_like(own_ref)
            other_ref[...] = jnp.zeros_like(other_ref)

        value = right_transposed(d_all[...], r_ref[...])
        rounded = (value * slope_ref[...].astype(f32)).astype(bf16)
        de_ref[...] = rounded
        sums_ref[...] = jnp.sum(rounded.astype(f32), axis=0, keepdims=True)
        for k in range(4):
            cut = slice(k * shard, (k + 1) * shard)
            own_ref[:, cut] += right_transposed(rounded[:tokens], w_refs[k][...])
            other_ref[:, cut] += right_transposed(rounded[tokens:], w_refs[k][...])

    specs, _ = feed_specs(shard, model)
    whole = pl.BlockSpec((tokens, model), lambda t, s: (0, 0))
    wide = pl.BlockSpec((2 * tokens, tile), lambda t, s: (0, t))
    return call(
        body,
        "feed_back",
        [
            shape(2 * tokens, 4 * tile, dtype=bf16),
            shape(1, 4 * tile),
            shape(tokens, model),
            shape(tokens, model),
        ],
        [own, sibling, slope, *[matrix] * 5],
        scalars=f.reshape(1),
        limit=2 * vmem_limit,
        scratch=[pltpu.VMEM((2 * tokens, model), bf16)],
        grid=(4,),
        in_specs=[whole, whole, wide, *specs],
        out_specs=[wide, pl.BlockSpec((1, tile), lambda t, s: (0, t)), whole, whole],
    )


def first_norm_back(d_second, own, received, unit, inverse, vectors, weights, f, number):
    tokens, model = d_second.shape
    shard = weights[0].shape[0]
    width = model // number

    def body(f_ref, d_ref, p_ref, r_ref, u_ref, i_ref, v_ref, *refs):
        w_refs = refs[:4]
        first_ref, rounded_ref, sums_ref, out_ref, matrix = refs[4:]
        for k in range(4):
            matrix[aligned(f_ref[0] ^ k, shard), :] = w_refs[k][...]
        dy = d_ref[...] + p_ref[...] + r_ref[...]
        unit_value = u_ref[...]
        dz = dy * v_ref[1:2, :]
        mean_dz = jnp.mean(dz, axis=-1, keepdims=True)
        mean_dzz = jnp.mean(dz * unit_value, axis=-1, keepdims=True)
        result = i_ref[:, 0:1] * (dz - mean_dz - unit_value * mean_dzz)
        first_ref[...] = result
        rounded = result.astype(bf16)
        rounded_ref[...] = rounded
        sums_ref[...] = jnp.zeros_like(sums_ref)
        sums_ref[0:1, :] = jnp.sum(dy * unit_value, axis=0, keepdims=True)
        sums_ref[1:2, :] = jnp.sum(dy, axis=0, keepdims=True)
        sums_ref[2:3, :] = jnp.sum(rounded.astype(f32), axis=0, keepdims=True)
        d_attended = right_transposed(rounded, matrix[...]).astype(bf16)
        for j in range(number):
            out_ref[j * tokens : (j + 1) * tokens, :] = d_attended[:, j * width : (j + 1) * width]

    return call(
        body,
        "first_norm_back",
        [
            shape(tokens, model),
            shape(tokens, model, dtype=bf16),
            shape(8, model),
            shape(number * tokens, width, dtype=bf16),
        ],
        [d_second, own, received, unit, inverse, vectors, *weights],
        scalars=f.reshape(1),
        scratch=[pltpu.VMEM((model, model), bf16)],
    )


def input_gradient(d_first, received, matrix, number):
    tokens, model = d_first.shape
    width = received.shape[1] // 3

    def body(d_ref, m_ref, r_ref, out_ref, ordered):
        for j in range(number):
            for k in range(3):
                ordered[:, k * model + j * width : k * model + (j + 1) * width] = r_ref[
                    j * tokens : (j + 1) * tokens, k * width : (k + 1) * width
                ]
        out_ref[...] = d_ref[...] + right_transposed(ordered[...], m_ref[...])

    return call(
        body,
        "input_gradient",
        shape(tokens, model),
        [d_first, matrix, received],
        scratch=[pltpu.VMEM((tokens, 3 * model), bf16)],
    )


def cast_projections(matrices, deps):
    rows, model = matrices[0].shape

    def body(q_ref, k_ref, v_ref, out_ref):
        out_ref[:, :model] = (q_ref[...] * query_scale).astype(bf16)
        out_ref[:, model : 2 * model] = k_ref[...].astype(bf16)
        out_ref[:, 2 * model :] = v_ref[...].astype(bf16)

    whole = pl.BlockSpec((rows, model), lambda: (0, 0))
    return call(
        body,
        "cast_projections",
        shape(rows, 3 * model, dtype=bf16),
        [*matrices],
        deps=deps,
        grid=(),
        in_specs=[whole] * 3,
        out_specs=pl.BlockSpec((rows, 3 * model), lambda: (0, 0)),
    )


def padded(vectors):
    return jnp.concatenate((jnp.stack(vectors), jnp.zeros((8 - len(vectors), vectors[0].shape[0]), f32)))


def per_device(
    hidden_in,
    starts,
    w_query,
    w_key,
    w_value,
    w_output,
    w_expand,
    w_reduce,
    bias_query,
    bias_value,
    bias_output,
    bias_expand,
    bias_reduce,
    attention_gain,
    attention_shift,
    feedforward_gain,
    feedforward_shift,
    cotangent,
):
    Order.last = ()
    tokens, model = hidden_in.shape[1:]
    head_size = model // HEADS
    ctx_size = lax.axis_size("ctx")
    length = tokens * ctx_size
    near = min(ctx_size, HEADS)
    copies = ctx_size // near
    heads = HEADS // near
    width = heads * head_size
    shard = w_query.shape[0]
    ff_block = w_reduce.shape[0]
    documents = starts.shape[1]
    c = lax.axis_index("ctx").astype(jnp.int32)
    f = lax.axis_index("fsdp").astype(jnp.int32)
    group = c & (near - 1)

    inputs = hidden_in[0]
    feed_matrix = lax.all_gather(cast_feed(w_expand, w_reduce), "fsdp", axis=0, tiled=True)
    blocks = gather_ctx(cast_all(inputs))

    own_columns = jnp.concatenate(
        [
            lax.dynamic_slice_in_dim(m, group * width, width, 1) * scale
            for m, scale in ((w_query, query_scale), (w_key, 1.0), (w_value, 1.0))
        ],
        axis=1,
    ).astype(bf16)

    def gather_rows(own):
        across = swap(own, "fsdp", 2)
        return [own, swap(own, "fsdp", 1), across, swap(across, "fsdp", 1)]

    projection_parts = gather_rows(own_columns)

    output_parts = gather_rows(cast_all(w_output, [blocks[1], blocks[2], blocks[4]]))

    all_projection = lax.all_gather(
        cast_projections((w_query, w_key, w_value), ()), "fsdp", axis=0, tiled=True
    )

    order = c ^ lax.iota(jnp.int32, ctx_size)
    positions = (order[:, None] * tokens + lax.iota(jnp.int32, tokens)[None, :]).reshape(-1)
    docs = jnp.sum((starts[0][None, :] <= positions[:, None]).astype(jnp.int32), axis=1) - 1
    lane = lax.iota(jnp.int32, LANES - head_size)[None, :]
    same = docs[:, None] == lane
    query_docs = jnp.where((lane < documents) & ~same, masked_value, 0.0).astype(f32)
    key_docs = jnp.where(same | ((lane >= documents) & (lane < documents + 3)), 1.0, 0.0).astype(f32)
    own_bias = jnp.concatenate(
        (
            lax.dynamic_slice_in_dim(bias_query * query_scale, group * width, width, 0),
            jnp.zeros((width,), f32),
            lax.dynamic_slice_in_dim(bias_value, group * width, width, 0),
        )
    ).reshape(1, -1)
    attention_vectors = padded((bias_output, attention_gain, attention_shift))
    feed_vectors = padded((bias_reduce, feedforward_gain, feedforward_shift))

    queries, keys, values, keys_t, stream = project(
        blocks,
        0,
        projection_parts,
        own_bias,
        query_docs,
        key_docs,
        f,
        heads,
        head_size,
        length,
        None,
        (),
    )

    out, wide, back = attend(
        queries, keys, values, group, near, tokens, head_size, documents, output_parts[1:]
    )
    received = exchange(out, near)
    normed, normed_r, first_unit, first_inverse, attended_r = attention_norm(
        received, output_parts, inputs, attention_vectors, f, near
    )

    sibling_normed = swap(normed_r, "fsdp", 1)
    activated_r, slope, partial, other = feed_forward(
        normed_r, sibling_normed, feed_matrix, bias_expand.reshape(1, -1), f
    )
    layer_out, d_second, d_reduced_r, second_sums = second_norm(
        normed, partial, swap(other, "fsdp", 1), feed_vectors, cotangent[0]
    )
    sibling_reduced = swap(d_reduced_r, "fsdp", 1)

    d_expanded_r, bias_expand_sum, partial, other = feed_back(
        d_reduced_r, sibling_reduced, slope, feed_matrix, f
    )
    other = swap(other, "fsdp", 1)

    expand_send = expand_gradients(normed_r, sibling_normed, d_expanded_r, f, (2, 3), 1, shard)
    expand_received = swap(expand_send, "fsdp", 2)
    d_first, d_attention_r, first_sums, d_attended = first_norm_back(
        d_second,
        partial,
        other,
        first_unit,
        first_inverse,
        attention_vectors,
        output_parts,
        f,
        near,
    )
    douts = exchange(d_attended, near)
    output_keep, output_send = output_gradient(
        attended_r, d_attention_r, first_sums, second_sums, bias_expand_sum, f, shard
    )
    output_received = swap(output_send, "fsdp", 1)
    low = c & 1
    reduce_keep = reduce_gradient(activated_r, d_reduced_r, sibling_reduced, low)
    expand_keep = expand_gradients(normed_r, sibling_normed, d_expanded_r, f, (0, 1), 0, shard)
    reduce_send = reduce_gradient(activated_r, d_reduced_r, sibling_reduced, 1 - low, [douts])
    reduce_received = swap(reduce_send, "ctx", 1)

    rest = (2 * shard, 2 * shard + 16)
    d_query, d_key, d_value = attend_back(
        back, douts, wide, keys, values, keys_t, head_size, tokens, group
    )
    output_keep, output_send = add_parts(
        output_keep, output_received, [[(0, shard), rest], [(shard, 2 * shard), rest]]
    )
    output_received = swap(output_send, "fsdp", 2)
    count = ctx_size
    while count > near:
        count //= 2
        received = [
            swap(d[count * tokens :].astype(bf16), "ctx", count).astype(f32) for d in (d_key, d_value)
        ]
        d_key = d_key[: count * tokens] + received[0]
        d_value = d_value[: count * tokens] + received[1]
    d_all, d_send = head_grads([d_query], d_key, d_value, tokens, near, group)
    d_mine = exchange(d_send, near)

    send, keep = projection_gradients(stream, d_all, f, shard)
    received = swap(send, "fsdp", 1)
    (expand_send,) = add_parts(expand_keep, expand_received, [[(2 * shard, 4 * shard)]])
    expand_other = swap(expand_send, "fsdp", 1)
    send, keep = add_parts(keep, received, [[(0, shard), rest], [(shard, 2 * shard), rest]])
    received = swap(send, "fsdp", 2)
    cut = ff_block // 2
    reduce_keep, reduce_send = add_parts(
        reduce_keep, reduce_received, [[(0, cut)], [(cut, 2 * cut)]]
    )
    reduce_received = swap(reduce_send, "fsdp", 2)
    groups = ctx_groups()
    expander = CtxSum(
        groups,
        ([expand_keep, expand_received], 0, 2 * shard),
        ([expand_other], 0, 2 * shard),
        ([output_keep, output_received], 0, shard + 16),
    )
    mine = sum_all([keep, received])
    count = ctx_size
    while count > near:
        count //= 2
        mine = sum_all([mine, swap(mine, "ctx", count)])
    projections = lax.all_gather(mine, "ctx", axis=0, tiled=True)
    expander.step([d_mine])
    reducer = CtxSum(groups[1:], ([reduce_keep, reduce_received], 0, cut))
    input_grad = input_gradient(d_first, d_mine, all_projection, near)
    reducer.step()
    reducer.step()
    expander.step()
    reduced = lax.all_gather(sum_all(reducer.finish()), "ctx", axis=0, tiled=True)
    expander.step()
    expanded = lax.all_gather(sum_all(expander.finish()), "ctx", axis=0, tiled=True)
    grad_query, grad_key, grad_value, grad_bias_query, grad_bias_value = place_projections(
        projections[: near * (shard + 16)], f, near, width, shard
    )
    grad_w_reduce = place_rows(reduced, ctx_size)
    grad_w_expand, grad_w_output, *small = place_expand(expanded, f, shard, ctx_size)
    (
        grad_bias_query,
        grad_bias_value,
        grad_att_gain,
        grad_att_shift,
        grad_bias_output,
        grad_ff_gain,
        grad_ff_shift,
        grad_bias_reduce,
        grad_bias_expand,
    ) = [v.reshape(-1) for v in (grad_bias_query, grad_bias_value, *small)]

    return (
        layer_out[None],
        input_grad[None],
        grad_query,
        grad_key,
        grad_value,
        grad_w_output,
        grad_w_expand,
        grad_w_reduce,
        grad_bias_query,
        grad_bias_value,
        grad_bias_output,
        grad_bias_expand,
        grad_bias_reduce,
        grad_att_gain,
        grad_att_shift,
        grad_ff_gain,
        grad_ff_shift,
    )


def solution(mesh):
    rows = P("fsdp", None)
    activations = P("fsdp", "ctx", None)
    return jax.shard_map(
        per_device,
        mesh=mesh,
        in_specs=(activations,) + (rows,) * 7 + (P(),) * 9 + (activations,),
        out_specs=(activations, activations) + (rows,) * 6 + (P("fsdp"),) * 9,
        check_vma=False,
    )
```

time: 633 us -> 488 us (0.77); the launches traced: 625 us -> 487 us
  starting transfers between devices: 115 us -> 47.7 us
  Pallas kernels: 185 us -> 120 us
  local copies, waits for them, and re-layouts: 36.4 us -> 67.8 us
  matrix products: 19.1 us -> 0 us
  other arithmetic: 20.7 us -> 1.94 us
    ppermute x93 -> x30, starting transfers between devices: 115 us -> 32.8 us  [swap(): return lax.ppermute(array, axis, [(i, i ^ mask) for i in range(size)])]
    pallas_call x39 -> x35, Pallas kernels: 185 us -> 120 us  [call(): pl.pallas_call(ordered, out_shape=out_shape, grid_spec=pltpu.PrefetchScal...]
    ppermute x93 -> x30, waiting for transfers between devices: 233 us -> 169 us  [swap(): return lax.ppermute(array, axis, [(i, i ^ mask) for i in range(size)])]
    unnamed x245 -> x189, local copies, waits for them, and re-layouts: 12.4 us -> 65.9 us
    all_gather x1 -> x5, waiting for transfers between devices: 0.02 us -> 51.9 us  [the longest x1 51.8 us: per_device(): lax.all_gather(sum_all(expander.finish()), 'ctx', axis=0, tiled=True)]
    dot_general x14 -> x0, matrix products: 19.1 us -> none  [left_transposed(): lax.dot_general(left, right, (((0,), (0,)), ((), ())), preferred_element_...]
    all_to_all x0 -> x3, starting transfers between devices: none -> 14.5 us  [exchange(): return lax.all_to_all(array, 'ctx', 0, 0, tiled=True)]
    concatenate x15 -> x0, other arithmetic: 13.7 us -> none  [the longest x3 3.12 us: expand_units(): jnp.concatenate([expand_unit(row_block, k ^ flip) for k in range(2)], axi...]
  transfers between devices with their start and end apart: 94 -> 38, of which waited for: 30 -> 18; matrix products, arithmetic and copies ran while one was open for 10% -> 1% of each run, Pallas kernels for 25% -> 24%
where the time goes in v2:
time: 488 us; the launch traced here: 487 us
  waiting for transfers between devices  235 us (48%)
  Pallas kernels  120 us (25%)
  local copies, waits for them, and re-layouts  67.8 us (14%)
  starting transfers between devices  47.7 us (10%)
  between operations  14.5 us (3%)
    ppermute x30, waiting for transfers between devices, swap(): return lax.ppermute(array, axis, [(i, i ^ mask) for i in range(size)])  169 us
    pallas_call x35, Pallas kernels, call(): pl.pallas_call(ordered, out_shape=out_shape, grid_spec=pltpu.PrefetchScal...  120 us
    unnamed x189, local copies, waits for them, and re-layouts  65.9 us
    all_gather x1, waiting for transfers between devices, per_device(): lax.all_gather(sum_all(expander.finish()), 'ctx', axis=0, tiled=True)  51.8 us
    ppermute x30, starting transfers between devices, swap(): return lax.ppermute(array, axis, [(i, i ^ mask) for i in range(size)])  32.8 us
    all_to_all x3, starting transfers between devices, exchange(): return lax.all_to_all(array, 'ctx', 0, 0, tiled=True)  14.5 us
    all_to_all x3, waiting for transfers between devices, exchange(): return lax.all_to_all(array, 'ctx', 0, 0, tiled=True)  13.7 us
  transfers between devices with their start and end apart: 38, of which 18 were waited for; matrix products, arithmetic and copies ran while one was open for 1% of the time, Pallas kernels for 24%

profile of v2, /device:TPU:0, one launch (start us, length us, event | category | flops | bytes accessed | tf_op | source)
XLA Modules:
  0.0 486.6 jit_solution(6005069978917462695)
XLA Ops:
  7.2 2.2 copy-done.34
  9.4 2.2 copy-done.35
  12.5 2.0 copy-done
  15.8 2.2 copy-done.1
  18.0 4.1 collective-permute-start.3
  25.2 20.2 %collective-permute-done.3.refs_4_.refs_5_ = bf16[256,1024]{1,0:T(8,128)(2,1)S(1)} collective-permute-done((bf16[256,1024]{1,0:T(8,128)(2,1)S(1)}, bf16[256,1024]{1,0:T(8,128)(2,1)S(1)}, u32[]{:S(2)}, u32[]{:S(2)}) %collective-permute-start.3) | collective-permute-done | bytes 524320 | tf_op jit(solution)/shard_map/ppermute | solution.py:34
  53.5 8.6 %collective-permute-done.8.refs_11_ = bf16[256,384]{1,0:T(8,128)(2,1)S(1)} collective-permute-done((bf16[256,384]{1,0:T(8,128)(2,1)S(1)}, bf16[256,384]{1,0:T(8,128)(2,1)S(1)}, u32[]{:S(2)}, u32[]{:S(2)}) %collective-permute-start.8) | collective-permute-done | bytes 196640 | tf_op jit(solution)/shard_map/ppermute | solution.py:34
  67.0 16.5 %collective-permute-done.11.refs_6_.refs_4_.refs_9_ = bf16[256,1024]{1,0:T(8,128)(2,1)S(1)} collective-permute-done((bf16[256,1024]{1,0:T(8,128)(2,1)S(1)}, bf16[256,1024]{1,0:T(8,128)(2,1)S(1)}, u32[]{:S(2)}, u32[]{:S(2)}) %collective-permute-start.11) | collective-permute-done | bytes 524320 | tf_op jit(solution)/shard_map/ppermute | solution.py:34
  85.2 3.3 collective-permute-done.6.refs_8_
  88.5 7.2 %project.1 = (bf16[2,2048,128]{2,1,0:T(8,128)(2,1)S(1)}, bf16[2,2048,128]{2,1,0:T(8,128)(2,1)S(1)}, bf16[2,2048,128]{2,1,0:T(8,128)(2,1)S(1)}, bf16[128,2048]{1,0:T(8,128)(2,1)S(1)}, bf16[2048,1024]{1,0:T(8,128)(2,1)S(1)}) custom-call(s32[1]{0:T(128)} %bitcast.refs_0_, bf16[256,1024]{1,0:T(8,128)(2,1)S(1)} %cast_all.2.refs_1_, ...), custom_call_target="tpu_custom_call" | custom-call | flops 1 | bytes 1 | tf_op jit(solution)/shard_map/project/pallas_call | solution.py:64
  95.8 2.0 copy-done.36
  97.9 15.4 %attend.1 = (bf16[2048,128]{1,0:T(8,128)(2,1)}, f32[2048,128]{1,0:T(8,128)S(1)}, bf16[2,2048,128]{2,1,0:T(8,128)(2,1)S(1)}) custom-call(s32[1]{0:T(128)} %bitcast.1.refs_0_, bf16[2,2048,128]{2,1,0:T(8,128)(2,1)S(1)} %get-tuple-element.85.refs_1_.refs_4_, bf16[2,2048,128]{2,1,0:T(8,128)(2,1)S(1)} %get-tuple-element.86.refs_2_.refs_4_, ...), custom_call_target="tpu_custom_call" | custom-call | flops 1 | bytes 1 | tf_op jit(solution)/shard_map/attend/pallas_call | solution.py:64
  115.2 4.3 all-to-all-start
  119.7 13.7 %all-to-all-done = bf16[8,256,128]{2,1,0:T(8,128)(2,1)S(1)} async-done(((bf16[8,256,128]{2,1,0:T(8,128)(2,1)}), bf16[8,256,128]{2,1,0:T(8,128)(2,1)S(1)}, u32[]{:S(2)}, u32[]{:S(2)}) %all-to-all-start) | async-done | bytes 524320 | tf_op jit(solution)/shard_map/all_to_all | solution.py:100
  141.3 10.5 %feed_forward.1 = (bf16[512,2048]{1,0:T(8,128)(2,1)}, bf16[512,2048]{1,0:T(8,128)(2,1)}, f32[256,1024]{1,0:T(8,128)}, f32[256,1024]{1,0:T(8,128)}) custom-call(s32[1]{0:T(128)} %bitcast.refs_0_, bf16[256,1024]{1,0:T(8,128)(2,1)} %copy-done.19, bf16[256,1024]{1,0:T(8,128)(2,1)} %copy-done.22, ...), custom_call_target="tpu_custom_call" | custom-call | flops 1 | bytes 1 | tf_op jit(solution)/shard_map/feed_forward/pallas_call | solution.py:64
  152.2 2.6 collective-permute-done.14.refs_2_
  157.6 2.5 second_norm.1
  162.9 9.8 %feed_back.1 = (bf16[512,2048]{1,0:T(8,128)(2,1)}, f32[1,2048]{1,0:T(1,128)}, f32[256,1024]{1,0:T(8,128)}, f32[256,1024]{1,0:T(8,128)}) custom-call(s32[1]{0:T(128)} %bitcast.refs_0_, bf16[256,1024]{1,0:T(8,128)(2,1)} %copy-done.15, bf16[256,1024]{1,0:T(8,128)(2,1)} %copy-done.17, bf16[512,2048]{1,0:T(8,128)(2,1)} %get-tuple-element.97.refs_3_, ...), custom_call_target="tpu_custom_call" | custom-call | flops 1 | bytes 1 | tf_op jit(solution)/shard_map/feed_back/pallas_call | solution.py:64
  174.7 2.3 expand_gradients.2.refs_11_
  181.0 5.7 %all-to-all-start.1 = ((bf16[8,256,128]{2,1,0:T(8,128)(2,1)}), bf16[8,256,128]{2,1,0:T(8,128)(2,1)}, u32[]{:S(2)}, u32[]{:S(2)}) async-start(bf16[8,256,128]{2,1,0:T(8,128)(2,1)} %bitcast.43), calls=%async_computation.1 | async-start | bytes 1048576 | tf_op jit(solution)/shard_map/all_to_all | solution.py:100
  190.0 2.5 output_gradient.1
  203.7 2.3 expand_gradients.3.refs_4_.refs_0_.refs_1_
  207.6 2.6 reduce_gradient.3.refs_7_
  211.7 25.5 %attend_back.1 = (bf16[2048,128]{1,0:T(8,128)(2,1)S(1)}, f32[2048,128]{1,0:T(8,128)S(1)}, f32[2048,128]{1,0:T(8,128)S(1)}) custom-call(s32[1]{0:T(128)} %bitcast.1.refs_0_, bf16[2,2048,128]{2,1,0:T(8,128)(2,1)S(1)} %copy-done.71, bf16[2048,128]{1,0:T(8,128)(2,1)} %bitcast.16.refs_5_.refs_2_, f32[2048,128]{1,0:T(8,128)S(1)} %copy-done.69, ...), custom_call_target="tpu_custom_call" | custom-call | flops 1 | bytes 1 | tf_op jit(solution)/shard_map/attend_back/pallas_call | solution.py:64
  242.6 4.6 all-to-all-start.2
  248.6 2.2 copy-done.37
  250.8 3.3 projection_gradients.1
  254.3 2.0 add_parts.5.refs_2_
  258.3 9.1 %collective-permute-done.23.refs_1_ = bf16[1024,1024]{1,0:T(8,128)(2,1)} collective-permute-done((bf16[1024,1024]{1,0:T(8,128)(2,1)}, bf16[1024,1024]{1,0:T(8,128)(2,1)}, u32[]{:S(2)}, u32[]{:S(2)}) %collective-permute-start.23) | collective-permute-done | bytes 2097184 | tf_op jit(solution)/shard_map/ppermute | solution.py:34
  267.4 2.1 add_parts.7
  272.6 2.1 collective-permute-start.20
  274.8 13.7 %collective-permute-done.20.refs_5_ = bf16[272,1024]{1,0:T(8,128)(2,1)} collective-permute-done((bf16[272,1024]{1,0:T(8,128)(2,1)}, bf16[272,1024]{1,0:T(8,128)(2,1)}, u32[]{:S(2)}, u32[]{:S(2)}) %collective-permute-start.20) | collective-permute-done | bytes 557088 | tf_op jit(solution)/shard_map/ppermute | solution.py:34
  289.6 4.1 sum_split.5
  293.7 2.5 collective-permute-start.24
  296.1 2.8 copy-done.12
  300.2 4.3 input_gradient.1.refs_3_
  304.4 6.3 %collective-permute-done.25.refs_2_ = bf16[512,1024]{1,0:T(8,128)(2,1)} collective-permute-done((bf16[512,1024]{1,0:T(8,128)(2,1)}, bf16[512,1024]{1,0:T(8,128)(2,1)}, u32[]{:S(2)}, u32[]{:S(2)}) %collective-permute-start.25) | collective-permute-done | bytes 1048608 | tf_op jit(solution)/shard_map/ppermute | solution.py:34
  314.4 19.7 %collective-permute-done.26.refs_2_ = bf16[256,1024]{1,0:T(8,128)(2,1)S(1)} collective-permute-done((bf16[256,1024]{1,0:T(8,128)(2,1)S(1)}, bf16[256,1024]{1,0:T(8,128)(2,1)S(1)}, u32[]{:S(2)}, u32[]{:S(2)}) %collective-permute-start.26) | collective-permute-done | bytes 524320 | tf_op jit(solution)/shard_map/ppermute | solution.py:34
  334.5 5.1 %collective-permute-start.28 = (bf16[128,1024]{1,0:T(8,128)(2,1)S(1)}, bf16[128,1024]{1,0:T(8,128)(2,1)S(1)}, u32[]{:S(2)}, u32[]{:S(2)}) collective-permute-start(bf16[128,1024]{1,0:T(8,128)(2,1)S(1)} %get-tuple-element.136), channel_id=1, source_target_pairs={{0,16},{4,20},{8,24},{12,28},{16,0},{20,4},{24,8},{28,12},{1,17},{... | collective-permute-start | bytes 786440 | tf_op jit(solution)/shard_map/ppermute | solution.py:34
  339.6 2.2 sum_split.8
  341.8 9.2 %collective-permute-done.28.refs_1_ = bf16[128,1024]{1,0:T(8,128)(2,1)S(1)} collective-permute-done((bf16[128,1024]{1,0:T(8,128)(2,1)S(1)}, bf16[128,1024]{1,0:T(8,128)(2,1)S(1)}, u32[]{:S(2)}, u32[]{:S(2)}) %collective-permute-start.28) | collective-permute-done | bytes 262176 | tf_op jit(solution)/shard_map/ppermute | solution.py:34
  352.6 23.5 %collective-permute-done.27.refs_2_ = bf16[352,1024]{1,0:T(8,128)(2,1)S(1)} collective-permute-done((bf16[352,1024]{1,0:T(8,128)(2,1)S(1)}, bf16[352,1024]{1,0:T(8,128)(2,1)S(1)}, u32[]{:S(2)}, u32[]{:S(2)}) %collective-permute-start.27) | collective-permute-done | bytes 720928 | tf_op jit(solution)/shard_map/ppermute | solution.py:34
  376.5 3.9 collective-permute-start.29
  380.5 30.9 %collective-permute-done.29.refs_1_ = bf16[176,1024]{1,0:T(8,128)(2,1)S(1)} collective-permute-done((bf16[176,1024]{1,0:T(8,128)(2,1)S(1)}, bf16[176,1024]{1,0:T(8,128)(2,1)S(1)}, u32[]{:S(2)}, u32[]{:S(2)}) %collective-permute-start.29) | collective-permute-done | bytes 360480 | tf_op jit(solution)/shard_map/ppermute | solution.py:34
  418.3 3.5 place_rows.1.refs_2_
  421.8 51.8 %all-gather.12.cloned.1.call-done.refs_1_ = bf16[1408,1024]{1,0:T(8,128)(2,1)} async-done(((bf16[176,1024]{1,0:T(8,128)(2,1)}), bf16[1408,1024]{1,0:T(8,128)(2,1)}) %all-gather.12.cloned.1.call-update) | async-done | bytes 2883600 | tf_op jit(solution)/shard_map/all_gather | solution.py:1149
  473.6 2.2 copy-done.10
  477.6 2.5 place_expand.1
  (275 shorter events, 88.5 us)
Async XLA Ops:
  7.2 133.3 %all-gather.6.cloned.1.call-start = ((), (), s32[]{:S(2)}) async-start(), calls=%async_computation.3 | async-start | bytes 20971520 | tf_op jit(solution)/shard_map/all_gather | solution.py:997
  14.6 281.6 %all-gather.8.cloned.1.call-start = ((), (), s32[]{:S(2)}) async-start(), calls=%async_computation.4 | async-start | bytes 7864320 | tf_op jit(solution)/shard_map/all_gather | solution.py:1016
  18.0 28.9 %copy-start.61 = (f32[256,1024]{1,0:T(8,128)S(1)}, f32[256,1024]{1,0:T(8,128)}, u32[]{:S(2)}) copy-start(f32[256,1024]{1,0:T(8,128)} %refs_0_.4) | copy-start | bytes 3145732
  18.0 29.7 %copy-start.58 = (f32[256,1024]{1,0:T(8,128)S(1)}, f32[256,1024]{1,0:T(8,128)}, u32[]{:S(2)}) copy-start(f32[256,1024]{1,0:T(8,128)} %refs_0_.5) | copy-start | bytes 3145732
  18.0 29.7 %copy-start.59 = (f32[256,1024]{1,0:T(8,128)S(1)}, f32[256,1024]{1,0:T(8,128)}, u32[]{:S(2)}) copy-start(f32[256,1024]{1,0:T(8,128)} %refs_2_.1) | copy-start | bytes 3145732
  18.0 29.7 %copy-start.60 = (f32[256,1024]{1,0:T(8,128)S(1)}, f32[256,1024]{1,0:T(8,128)}, u32[]{:S(2)}) copy-start(f32[256,1024]{1,0:T(8,128)} %refs_1_.3) | copy-start | bytes 3145732
  18.0 27.4 %collective-permute-start.3 = (bf16[256,1024]{1,0:T(8,128)(2,1)S(1)}, bf16[256,1024]{1,0:T(8,128)(2,1)S(1)}, u32[]{:S(2)}, u32[]{:S(2)}) collective-permute-start(bf16[256,1024]{1,0:T(8,128)(2,1)S(1)} %cast_all.2.refs_1_), channel_id=1, source_target_pairs={{0,16},{4,20},{8,24},{12,28},{16,0},{20,4},{24,8},{28,12},{1,17},{... | collective-permute-start | bytes 1572872 | tf_op jit(solution)/shard_map/ppermute | solution.py:34
  22.1 23.3 %collective-permute-start = (bf16[256,1024]{1,0:T(8,128)(2,1)S(1)}, bf16[256,1024]{1,0:T(8,128)(2,1)}, u32[]{:S(2)}, u32[]{:S(2)}) collective-permute-start(bf16[256,1024]{1,0:T(8,128)(2,1)S(1)} %cast_all.2.refs_1_), channel_id=1, source_target_pairs={{0,4},{4,0},{8,12},{12,8},{16,20},{20,16},{24,28},{28,24},{1,5},{5... | collective-permute-start | bytes 1572872 | tf_op jit(solution)/shard_map/ppermute | solution.py:34
  23.7 23.2 %collective-permute-start.1 = (bf16[256,1024]{1,0:T(8,128)(2,1)S(1)}, bf16[256,1024]{1,0:T(8,128)(2,1)S(1)}, u32[]{:S(2)}, u32[]{:S(2)}) collective-permute-start(bf16[256,1024]{1,0:T(8,128)(2,1)S(1)} %cast_all.2.refs_1_), channel_id=1, source_target_pairs={{0,8},{4,12},{8,0},{12,4},{16,24},{20,28},{24,16},{28,20},{1,9},{5... | collective-permute-start | bytes 1572872 | tf_op jit(solution)/shard_map/ppermute | solution.py:34
  50.1 12.0 %collective-permute-start.8 = (bf16[256,384]{1,0:T(8,128)(2,1)S(1)}, bf16[256,384]{1,0:T(8,128)(2,1)S(1)}, u32[]{:S(2)}, u32[]{:S(2)}) collective-permute-start(bf16[256,384]{1,0:T(8,128)(2,1)S(1)} %pad_maximum_fusion.refs_9_), channel_id=1, source_target_pairs={{0,2},{1,3},{2,0},{3,1},{4,6},{5,7},{6,4},{7,5},{8,10},{9,11},{10,... | collective-permute-start | bytes 589832 | tf_op jit(solution)/shard_map/ppermute | solution.py:34
  51.7 10.9 %collective-permute-start.7 = (bf16[256,384]{1,0:T(8,128)(2,1)S(1)}, bf16[256,384]{1,0:T(8,128)(2,1)S(1)}, u32[]{:S(2)}, u32[]{:S(2)}) collective-permute-start(bf16[256,384]{1,0:T(8,128)(2,1)S(1)} %pad_maximum_fusion.refs_9_), channel_id=1, source_target_pairs={{0,1},{1,0},{2,3},{3,2},{4,5},{5,4},{6,7},{7,6},{8,9},{9,8},{10,11... | collective-permute-start | bytes 589832 | tf_op jit(solution)/shard_map/ppermute | solution.py:34
  51.8 31.7 %collective-permute-start.11 = (bf16[256,1024]{1,0:T(8,128)(2,1)S(1)}, bf16[256,1024]{1,0:T(8,128)(2,1)S(1)}, u32[]{:S(2)}, u32[]{:S(2)}) collective-permute-start(bf16[256,1024]{1,0:T(8,128)(2,1)S(1)} %cast_all.3.refs_3_.refs_2_.refs_7_), channel_id=1, source_target_pairs={{0,2},{1,3},{2,0},{3,1},{4,6},{5,7},{6,4},{7,5},{8,10},{9,11},{10,... | collective-permute-start | bytes 1572872 | tf_op jit(solution)/shard_map/ppermute | solution.py:34
  52.3 14.2 %collective-permute-start.5 = (bf16[256,1024]{1,0:T(8,128)(2,1)S(1)}, bf16[256,1024]{1,0:T(8,128)(2,1)}, u32[]{:S(2)}, u32[]{:S(2)}) collective-permute-start(bf16[256,1024]{1,0:T(8,128)(2,1)S(1)} %collective-permute-done.3.refs_4_.refs_5_), channel_id=1, source_target_pairs={{0,8},{4,12},{8,0},{12,4},{16,24},{20,28},{24,16},{28,20},{1,9},{5... | collective-permute-start | bytes 1572872 | tf_op jit(solution)/shard_map/ppermute | solution.py:34
  62.1 1.8 collective-permute-start.9
  62.1 35.7 %collective-permute-start.10 = (bf16[256,1024]{1,0:T(8,128)(2,1)S(1)}, bf16[256,1024]{1,0:T(8,128)(2,1)S(1)}, u32[]{:S(2)}, u32[]{:S(2)}) collective-permute-start(bf16[256,1024]{1,0:T(8,128)(2,1)S(1)} %cast_all.3.refs_3_.refs_2_.refs_7_), channel_id=1, source_target_pairs={{0,1},{1,0},{2,3},{3,2},{4,5},{5,4},{6,7},{7,6},{8,9},{9,8},{10,11... | collective-permute-start | bytes 1572872 | tf_op jit(solution)/shard_map/ppermute | solution.py:34
  63.3 21.9 %collective-permute-start.4 = (bf16[256,1024]{1,0:T(8,128)(2,1)S(1)}, bf16[256,1024]{1,0:T(8,128)(2,1)}, u32[]{:S(2)}, u32[]{:S(2)}) collective-permute-start(bf16[256,1024]{1,0:T(8,128)(2,1)S(1)} %collective-permute-done.3.refs_4_.refs_5_), channel_id=1, source_target_pairs={{0,4},{4,0},{8,12},{12,8},{16,20},{20,16},{24,28},{28,24},{1,5},{5... | collective-permute-start | bytes 1572872 | tf_op jit(solution)/shard_map/ppermute | solution.py:34
  64.6 20.6 %collective-permute-start.2 = (bf16[256,1024]{1,0:T(8,128)(2,1)}, bf16[256,1024]{1,0:T(8,128)(2,1)}, u32[]{:S(2)}, u32[]{:S(2)}) collective-permute-start(bf16[256,1024]{1,0:T(8,128)(2,1)} %collective-permute-done.refs_2_), channel_id=1, source_target_pairs={{0,8},{4,12},{8,0},{12,4},{16,24},{20,28},{24,16},{28,20},{1,9},{5... | collective-permute-start | bytes 1572872 | tf_op jit(solution)/shard_map/ppermute | solution.py:34
  66.5 22.0 %collective-permute-start.6 = (bf16[256,1024]{1,0:T(8,128)(2,1)}, bf16[256,1024]{1,0:T(8,128)(2,1)}, u32[]{:S(2)}, u32[]{:S(2)}) collective-permute-start(bf16[256,1024]{1,0:T(8,128)(2,1)} %collective-permute-done.5.refs_7_), channel_id=1, source_target_pairs={{0,4},{4,0},{8,12},{12,8},{16,20},{20,16},{24,28},{28,24},{1,5},{5... | collective-permute-start | bytes 1572872 | tf_op jit(solution)/shard_map/ppermute | solution.py:34
  83.5 14.3 %collective-permute-start.12 = (bf16[256,1024]{1,0:T(8,128)(2,1)S(1)}, bf16[256,1024]{1,0:T(8,128)(2,1)S(1)}, u32[]{:S(2)}, u32[]{:S(2)}) collective-permute-start(bf16[256,1024]{1,0:T(8,128)(2,1)S(1)} %collective-permute-done.11.refs_6_.refs_4_.refs_9_), channel_id=1, source_target_pairs={{0,1},{1,0},{2,3},{3,2},{4,5},{5,4},{6,7},{7,6},{8,9},{9,8},{10,11... | collective-permute-start | bytes 1572872 | tf_op jit(solution)/shard_map/ppermute | solution.py:34
  97.8 35.6 %copy-start.25 = (bf16[256,1024]{1,0:T(8,128)(2,1)}, bf16[256,1024]{1,0:T(8,128)(2,1)S(1)}, u32[]{:S(2)}) copy-start(bf16[256,1024]{1,0:T(8,128)(2,1)S(1)} %collective-permute-done.10.refs_5_.refs_3_.refs_8_) | copy-start | bytes 1572868
  97.8 35.6 %copy-start.27 = (bf16[256,1024]{1,0:T(8,128)(2,1)}, bf16[256,1024]{1,0:T(8,128)(2,1)S(1)}, u32[]{:S(2)}) copy-start(bf16[256,1024]{1,0:T(8,128)(2,1)S(1)} %collective-permute-done.12.refs_7_.refs_5_.refs_10_) | copy-start | bytes 1572868
  97.8 21.8 %copy-start.86 = (f32[1024]{0:T(1024)S(1)}, f32[1024]{0:T(1024)}, u32[]{:S(2)}) copy-start(f32[1024]{0:T(1024)} %param.34) | copy-start | bytes 12292
  97.8 21.8 %copy-start.87 = (f32[1024]{0:T(1024)S(1)}, f32[1024]{0:T(1024)}, u32[]{:S(2)}) copy-start(f32[1024]{0:T(1024)} %param.33) | copy-start | bytes 12292
  97.8 21.7 %copy-start.88 = (f32[1024]{0:T(1024)S(1)}, f32[1024]{0:T(1024)}, u32[]{:S(2)}) copy-start(f32[1024]{0:T(1024)} %param.30) | copy-start | bytes 12292
  115.2 18.2 %all-to-all-start = ((bf16[8,256,128]{2,1,0:T(8,128)(2,1)}), bf16[8,256,128]{2,1,0:T(8,128)(2,1)S(1)}, u32[]{:S(2)}, u32[]{:S(2)}) async-start(bf16[8,256,128]{2,1,0:T(8,128)(2,1)} %bitcast.4), calls=%async_computation | async-start | bytes 1048576 | tf_op jit(solution)/shard_map/all_to_all | solution.py:100
  138.6 1.9 collective-permute-start.13
  151.8 2.9 collective-permute-start.14
  160.1 2.0 collective-permute-start.15
  172.7 4.4 collective-permute-start.16
  181.0 25.0 %all-to-all-start.1 = ((bf16[8,256,128]{2,1,0:T(8,128)(2,1)}), bf16[8,256,128]{2,1,0:T(8,128)(2,1)}, u32[]{:S(2)}, u32[]{:S(2)}) async-start(bf16[8,256,128]{2,1,0:T(8,128)(2,1)} %bitcast.43), calls=%async_computation.1 | async-start | bytes 1048576 | tf_op jit(solution)/shard_map/all_to_all | solution.py:100
  193.6 43.6 %collective-permute-start.17 = (bf16[528,1024]{1,0:T(8,128)(2,1)}, bf16[528,1024]{1,0:T(8,128)(2,1)}, u32[]{:S(2)}, u32[]{:S(2)}) collective-permute-start(bf16[528,1024]{1,0:T(8,128)(2,1)} %get-tuple-element.117), channel_id=1, source_target_pairs={{0,1},{1,0},{2,3},{3,2},{4,5},{5,4},{6,7},{7,6},{8,9},{9,8},{10,11... | collective-permute-start | bytes 3244040 | tf_op jit(solution)/shard_map/ppermute | solution.py:34
  193.6 60.7 %collective-permute-start.18 = (bf16[1024,1024]{1,0:T(8,128)(2,1)}, bf16[1024,1024]{1,0:T(8,128)(2,1)}, u32[]{:S(2)}, u32[]{:S(2)}) collective-permute-start(bf16[1024,1024]{1,0:T(8,128)(2,1)} %copy-done.11), channel_id=1, source_target_pairs={{0,2},{1,3},{2,0},{3,1},{4,6},{5,7},{6,4},{7,5},{8,10},{9,11},{10,... | collective-permute-start | bytes 6291464 | tf_op jit(solution)/shard_map/ppermute | solution.py:34
  210.2 57.2 %collective-permute-start.23 = (bf16[1024,1024]{1,0:T(8,128)(2,1)}, bf16[1024,1024]{1,0:T(8,128)(2,1)}, u32[]{:S(2)}, u32[]{:S(2)}) collective-permute-start(bf16[1024,1024]{1,0:T(8,128)(2,1)} %reduce_gradient.3.refs_7_), channel_id=1, source_target_pairs={{0,4},{4,0},{8,12},{12,8},{16,20},{20,16},{24,28},{28,24},{1,5},{5... | collective-permute-start | bytes 6291464 | tf_op jit(solution)/shard_map/ppermute | solution.py:34
  211.7 25.5 %copy-start.31 = (bf16[528,1024]{1,0:T(8,128)(2,1)S(1)}, bf16[528,1024]{1,0:T(8,128)(2,1)}, u32[]{:S(2)}) copy-start(bf16[528,1024]{1,0:T(8,128)(2,1)} %copy-done.29) | copy-start | bytes 3244036
  242.6 45.9 %all-to-all-start.2 = ((bf16[8,256,384]{2,1,0:T(8,128)(2,1)}), bf16[8,256,384]{2,1,0:T(8,128)(2,1)}, u32[]{:S(2)}, u32[]{:S(2)}) async-start(bf16[8,256,384]{2,1,0:T(8,128)(2,1)} %bitcast.41), calls=%async_computation.2 | async-start | bytes 3145728 | tf_op jit(solution)/shard_map/all_to_all | solution.py:100
  247.2 165.0 %all-gather.10.cloned.1.call-start = ((), (), s32[]{:S(2)}) async-start(), calls=%async_computation.5 | async-start | bytes 1880064 | tf_op jit(solution)/shard_map/all_gather | solution.py:1140
  254.2 2.1 collective-permute-start.21
  256.4 14.1 %collective-permute-start.22 = (bf16[272,384]{1,0:T(8,128)(2,1)S(1)}, bf16[272,384]{1,0:T(8,128)(2,1)S(1)}, u32[]{:S(2)}, u32[]{:S(2)}) collective-permute-start(bf16[272,384]{1,0:T(8,128)(2,1)S(1)} %get-tuple-element.126.refs_2_), channel_id=1, source_target_pairs={{0,2},{1,3},{2,0},{3,1},{4,6},{5,7},{6,4},{7,5},{8,10},{9,11},{10,... | collective-permute-start | bytes 626696 | tf_op jit(solution)/shard_map/ppermute | solution.py:34
  272.2 143.3 %all-gather.14.cloned.1.call-start = ((), (), s32[]{:S(2)}) async-start(), calls=%async_computation.7 | async-start | bytes 2359296 | tf_op jit(solution)/shard_map/all_gather | solution.py:1147
  272.5 16.0 %collective-permute-start.19 = (bf16[512,1024]{1,0:T(8,128)(2,1)S(1)}, bf16[512,1024]{1,0:T(8,128)(2,1)}, u32[]{:S(2)}, u32[]{:S(2)}) collective-permute-start(bf16[512,1024]{1,0:T(8,128)(2,1)S(1)} %add_parts.5.refs_2_), channel_id=1, source_target_pairs={{0,1},{1,0},{2,3},{3,2},{4,5},{5,4},{6,7},{7,6},{8,9},{9,8},{10,11... | collective-permute-start | bytes 3145736 | tf_op jit(solution)/shard_map/ppermute | solution.py:34
  272.6 15.9 %collective-permute-start.20 = (bf16[272,1024]{1,0:T(8,128)(2,1)}, bf16[272,1024]{1,0:T(8,128)(2,1)}, u32[]{:S(2)}, u32[]{:S(2)}) collective-permute-start(bf16[272,1024]{1,0:T(8,128)(2,1)} %copy-done.85), channel_id=1, source_target_pairs={{0,2},{1,3},{2,0},{3,1},{4,6},{5,7},{6,4},{7,5},{8,10},{9,11},{10,... | collective-permute-start | bytes 1671176 | tf_op jit(solution)/shard_map/ppermute | solution.py:34
  274.7 36.0 %collective-permute-start.25 = (bf16[512,1024]{1,0:T(8,128)(2,1)}, bf16[512,1024]{1,0:T(8,128)(2,1)}, u32[]{:S(2)}, u32[]{:S(2)}) collective-permute-start(bf16[512,1024]{1,0:T(8,128)(2,1)} %copy-done.84), channel_id=1, source_target_pairs={{0,2},{1,3},{2,0},{3,1},{4,6},{5,7},{6,4},{7,5},{8,10},{9,11},{10,... | collective-permute-start | bytes 3145736 | tf_op jit(solution)/shard_map/ppermute | solution.py:34
  293.7 45.9 %collective-permute-start.24 = (bf16[704,1024]{1,0:T(8,128)(2,1)}, bf16[704,1024]{1,0:T(8,128)(2,1)}, u32[]{:S(2)}, u32[]{:S(2)}) collective-permute-start(bf16[704,1024]{1,0:T(8,128)(2,1)} %get-tuple-element.129), channel_id=1, source_target_pairs={{0,4},{4,0},{8,12},{12,8},{16,20},{20,16},{24,28},{28,24},{1,5},{5... | collective-permute-start | bytes 4325384 | tf_op jit(solution)/shard_map/ppermute | solution.py:34
  313.8 20.4 %collective-permute-start.26 = (bf16[256,1024]{1,0:T(8,128)(2,1)S(1)}, bf16[256,1024]{1,0:T(8,128)(2,1)S(1)}, u32[]{:S(2)}, u32[]{:S(2)}) collective-permute-start(bf16[256,1024]{1,0:T(8,128)(2,1)S(1)} %get-tuple-element.132), channel_id=1, source_target_pairs={{0,8},{4,12},{8,0},{12,4},{16,24},{20,28},{24,16},{28,20},{1,9},{5... | collective-permute-start | bytes 1572872 | tf_op jit(solution)/shard_map/ppermute | solution.py:34
  334.5 16.5 %collective-permute-start.28 = (bf16[128,1024]{1,0:T(8,128)(2,1)S(1)}, bf16[128,1024]{1,0:T(8,128)(2,1)S(1)}, u32[]{:S(2)}, u32[]{:S(2)}) collective-permute-start(bf16[128,1024]{1,0:T(8,128)(2,1)S(1)} %get-tuple-element.136), channel_id=1, source_target_pairs={{0,16},{4,20},{8,24},{12,28},{16,0},{20,4},{24,8},{28,12},{1,17},{... | collective-permute-start | bytes 786440 | tf_op jit(solution)/shard_map/ppermute | solution.py:34
  351.8 121.8 %all-gather.12.cloned.1.call-start = ((), (), s32[]{:S(2)}) async-start(), calls=%async_computation.6 | async-start | bytes 3244032 | tf_op jit(solution)/shard_map/all_gather | solution.py:1149
  351.8 24.3 %collective-permute-start.27 = (bf16[352,1024]{1,0:T(8,128)(2,1)S(1)}, bf16[352,1024]{1,0:T(8,128)(2,1)S(1)}, u32[]{:S(2)}, u32[]{:S(2)}) collective-permute-start(bf16[352,1024]{1,0:T(8,128)(2,1)S(1)} %get-tuple-element.135), channel_id=1, source_target_pairs={{0,8},{4,12},{8,0},{12,4},{16,24},{20,28},{24,16},{28,20},{1,9},{5... | collective-permute-start | bytes 2162696 | tf_op jit(solution)/shard_map/ppermute | solution.py:34
  376.5 34.8 %collective-permute-start.29 = (bf16[176,1024]{1,0:T(8,128)(2,1)S(1)}, bf16[176,1024]{1,0:T(8,128)(2,1)S(1)}, u32[]{:S(2)}, u32[]{:S(2)}) collective-permute-start(bf16[176,1024]{1,0:T(8,128)(2,1)S(1)} %get-tuple-element.138), channel_id=1, source_target_pairs={{0,16},{4,20},{8,24},{12,28},{16,0},{20,4},{24,8},{28,12},{1,17},{... | collective-permute-start | bytes 1081352 | tf_op jit(solution)/shard_map/ppermute | solution.py:34
  (84 other events, 354.6 us)
Sparse Core Ops, SparseCore 0:
  14.7 124.0 all-gather.5
  140.3 46.8 all-gather.7
  272.3 60.9 all-gather.9
  351.9 61.0 all-gather.13
  415.6 57.9 all-gather.11

commit v3 on v2

--- a/solution.py
+++ b/solution.py
@@ -94,6 +94,15 @@
     return [blocks[i] for i in range(len(blocks))]
 
 
+def gather_small(own, number):
+    blocks = {0: own}
+    for index in range(2, number, 2):
+        blocks[index] = swap(own, "ctx", index)
+    for index in list(blocks):
+        blocks[index | 1] = swap(blocks[index], "ctx", 1)
+    return [blocks[i] for i in range(number)]
+
+
 def exchange(array, number):
     size = lax.axis_size("ctx")
     if number == size:
@@ -108,15 +117,23 @@
     return result
 
 
-def ctx_groups():
-    return [(bit, 2) for bit in range(lax.axis_size("ctx").bit_length() - 1)]
-
-
-def piece_of(index, size):
+def ctx_groups(together=1):
+    bits = lax.axis_size("ctx").bit_length() - 1
+    groups, first = [(0, 2)], 1
+    while first < bits:
+        count = min(together, bits - first)
+        groups.append((first, 1 << count))
+        first += count
+    return groups
+
+
+def piece_of(index, size, together=1):
     bits = size.bit_length() - 1
-    piece = 0
-    for bit in range(bits):
-        piece = piece | (((index >> bit) & 1) << (bits - 1 - bit))
+    piece, first, count = 0, 0, 1
+    while first < bits:
+        piece = (piece << count) | ((index >> first) & ((1 << count) - 1))
+        first += count
+        count = min(together, bits - first)
     return piece
 
 
@@ -187,51 +204,66 @@
         return self.segments[0][0]
 
 
-def place_rows(gathered, size):
-    rows, width = gathered.shape
-
-    def body(in_ref, out_ref):
-        out_ref[...] = in_ref[...].astype(f32)
-
-    return call(
-        body,
-        "place_rows",
-        shape(rows, width),
-        [gathered],
-        grid=(size,),
-        in_specs=[pl.BlockSpec((rows // size, width), lambda p: (piece_of(p, size), 0))],
-        out_specs=pl.BlockSpec((rows // size, width), lambda p: (p, 0)),
-    )
-
-
-def place_expand(gathered, f, shard, size):
-    rows, columns = gathered.shape
-    piece = rows // size
-
-    def body(f_ref, in_ref, expand_ref, output_ref, *refs):
+def stack_sums(first, second):
+    sizes = [first[0].shape[0], second[0].shape[0]]
+
+    def body(*refs):
+        for begin, refs_of in ((0, refs[: len(first)]), (sizes[0], refs[len(first) : -1])):
+            value = refs_of[0][...].astype(f32)
+            for ref in refs_of[1:]:
+                value = value + ref[...].astype(f32)
+            refs[-1][begin : begin + value.shape[0], :] = value.astype(bf16)
+
+    return call(
+        body, "stack_sums", shape(sum(sizes), first[0].shape[1], dtype=bf16), [*first, *second]
+    )
+
+
+def place_gradients(gathered, f, shard, rows, size):
+    piece = gathered.shape[0] // size
+    columns = gathered.shape[1]
+    below = piece - rows
+
+    def body(f_ref, in_ref, reduce_ref, expand_ref, output_ref, *refs):
         outs, ordered, small = refs[:-2], refs[-2], refs[-1]
-        for j in range(size):
-            at = piece_of(j, size) * piece
-            ordered[at : at + piece, :] = in_ref[j * piece : (j + 1) * piece, :]
-        for unit, k in enumerate((0, 2, 1, 3)):
-            expand_ref[:, aligned(f_ref[0] ^ k, columns)] = ordered[
-                unit * shard : (unit + 1) * shard, :
-            ].astype(f32)
-        output_ref[...] = ordered[4 * shard : 5 * shard, :].astype(f32)
-        small[...] = ordered[5 * shard : 5 * shard + 16, :].astype(f32)
-        for k in range(6):
-            outs[k][...] = small[k : k + 1, aligned(f_ref[0], shard)]
-        outs[6][...] = small[pl.ds(8 + f_ref[0], 1), :]
-
-    return call(
-        body,
-        "place_expand",
-        [shape(shard, 4 * columns), shape(shard, columns)]
+        at = pl.program_id(0)
+        reduce_ref[...] = in_ref[0, :rows, :].astype(f32)
+        ordered[aligned(piece_of(at, size, 2), below), :] = in_ref[0, rows:, :]
+
+        @pl.when(at == size - 1)
+        def _():
+            for unit, k in enumerate((0, 2, 1, 3)):
+                expand_ref[:, aligned(f_ref[0] ^ k, columns)] = ordered[
+                    unit * shard : (unit + 1) * shard, :
+                ].astype(f32)
+            output_ref[...] = ordered[4 * shard : 5 * shard, :].astype(f32)
+            small[...] = ordered[5 * shard : 5 * shard + 16, :].astype(f32)
+            for k in range(6):
+                outs[k][...] = small[k : k + 1, aligned(f_ref[0], shard)]
+            outs[6][...] = small[pl.ds(8 + f_ref[0], 1), :]
+
+    def whole(*sizes):
+        return pl.BlockSpec(sizes, lambda p, s: (0, 0))
+
+    return call(
+        body,
+        "place_gradients",
+        [shape(size * rows, columns), shape(shard, 4 * columns), shape(shard, columns)]
         + [shape(1, shard)] * 6
         + [shape(1, columns)],
-        [gathered],
+        [gathered.reshape(size, piece, columns)],
         scalars=f.reshape(1),
-        scratch=[pltpu.VMEM((rows, columns), bf16), pltpu.VMEM((16, columns), f32)],
+        scratch=[pltpu.VMEM((size * below, columns), bf16), pltpu.VMEM((16, columns), f32)],
+        limit=2 * vmem_limit,
+        grid=(size,),
+        in_specs=[pl.BlockSpec((1, piece, columns), lambda j, s: (j, 0, 0))],
+        out_specs=[
+            pl.BlockSpec((rows, columns), lambda j, s: (piece_of(j, size), 0)),
+            whole(shard, 4 * columns),
+            whole(shard, columns),
+        ]
+        + [whole(1, shard)] * 6
+        + [whole(1, columns)],
     )
 
 
@@ -307,7 +339,7 @@
     )
 
 
-def expand_gradients(own, sibling, d_expanded, f, row_blocks, flip, shard):
+def expand_gradients(own, sibling, d_expanded, f, row_blocks, flip, shard, deps=()):
     tokens, model = own.shape
     columns = d_expanded.shape[1] // 2
 
@@ -324,6 +356,7 @@
         "expand_gradients",
         shape(4 * shard, columns, dtype=bf16),
         [own, sibling, d_expanded],
+        deps=deps,
         scalars=f.reshape(1),
         grid=(4,),
         in_specs=[left, left, pl.BlockSpec((2 * tokens, columns), lambda i, s: (0, (i % 2) ^ flip))],
@@ -447,28 +480,40 @@
     )
 
 
-def place_projections(gathered, f, count, width, shard):
-    rows = gathered.shape[0] // count
-
-    def body(f_ref, in_ref, *refs):
-        outs, sums = refs[:-1], refs[-1]
-        for j in range(count):
-            where = slice(j * width, (j + 1) * width)
+def place_projections(pieces, scalars, rows, width, shard):
+    count = len(pieces)
+    if width % LANES:
+        order = jnp.arange(count) ^ scalars[0]
+        ordered = jnp.take(jnp.stack(pieces), order, axis=0)
+        weights = jnp.transpose(ordered[:, :rows], (1, 0, 2)).astype(f32)
+        biases = ordered[:, rows].astype(f32)
+        return [
+            weights[:, :, k * width : (k + 1) * width].reshape(rows, count * width)
+            for k in range(3)
+        ] + [
+            lax.dynamic_slice_in_dim(
+                biases[:, k * width : (k + 1) * width].reshape(1, -1), scalars[1] * shard, shard, 1
+            )
+            for k in (0, 2)
+        ]
+
+    def body(s_ref, *refs):
+        outs, sums = refs[count:-1], refs[-1]
+        for i in range(count):
+            where = aligned(s_ref[0] ^ i, width)
             for k in range(3):
                 cut = slice(k * width, (k + 1) * width)
-                outs[k][:, where] = in_ref[j * rows : j * rows + shard, cut].astype(f32)
-                sums[k : k + 1, where] = in_ref[j * rows + shard : (j + 1) * rows, cut].astype(f32)[
-                    0:1, :
-                ]
+                outs[k][:, where] = refs[i][:rows, cut].astype(f32)
+                sums[k : k + 1, where] = refs[i][rows : rows + 16, cut].astype(f32)[0:1, :]
         for k, row in ((3, 0), (4, 2)):
-            outs[k][...] = sums[row : row + 1, aligned(f_ref[0], shard)]
+            outs[k][...] = sums[row : row + 1, aligned(s_ref[1], shard)]
 
     return call(
         body,
         "place_projections",
-        [shape(shard, count * width)] * 3 + [shape(1, shard)] * 2,
-        [gathered],
-        scalars=f.reshape(1),
+        [shape(rows, count * width)] * 3 + [shape(1, shard)] * 2,
+        pieces,
+        scalars=scalars,
         scratch=[pltpu.VMEM((8, count * width), f32)],
     )
 
@@ -548,23 +593,33 @@
 def attend(queries, keys, values, group, number, tokens, head_size, docs, deps):
     heads, length, _ = keys.shape
     width = heads * head_size
-    tile = 256 if length <= 4096 else 128
-    per = tokens // tile
+    tile = 2 * tokens if length <= 4096 else 128
+    per, span = max(1, tokens // tile), max(1, tile // tokens)
     rows = number * tokens
+    chunk = min(length, 1024)
 
     def body(s_ref, q_ref, k_ref, v_ref, out_ref, wide_ref, back_ref):
         lane = lax.broadcasted_iota(jnp.int32, (tile, LANES), 1)
         for h in range(heads):
             query = q_ref[h]
-            scores = right_transposed(query, k_ref[h])
-            largest = jnp.max(scores, axis=1, keepdims=True)
-            weights = jnp.exp(scores - largest).astype(bf16)
-            summed = matmul(weights, v_ref[h])
+            largest = summed = None
+            for first in range(0, length, chunk):
+                scores = right_transposed(query, k_ref[h, first : first + chunk, :])
+                before = largest
+                largest = jnp.max(scores, axis=1, keepdims=True)
+                if before is not None:
+                    largest = jnp.maximum(before, largest)
+                    summed = summed * jnp.exp(before - largest)
+                weights = jnp.exp(scores - largest).astype(bf16)
+                part = matmul(weights, v_ref[h, first : first + chunk, :])
+                summed = part if before is None else summed + part
             total = summed[:, head_size : head_size + 1]
             cut = slice(h * head_size, (h + 1) * head_size)
             attended = summed[:, :head_size] / total
             wide_ref[:, cut] = attended
-            out_ref[:, cut] = attended.astype(bf16)
+            for b in range(span):
+                where = aligned((b ^ s_ref[0]) & (span - 1), tile // span)
+                out_ref[where, cut] = attended[b * tokens : (b + 1) * tokens].astype(bf16)
             parts = three_parts(-(largest + jnp.log(total)))
             back = query.astype(f32)
             for k in range(3):
@@ -581,6 +636,7 @@
         ],
         [queries, keys, values],
         deps=deps,
+        limit=40 * 1024 * 1024,
         scalars=group.reshape(1),
         grid=(rows // tile,),
         in_specs=[
@@ -589,7 +645,7 @@
             pl.BlockSpec((heads, length, LANES), lambda i, s: (0, 0, 0)),
         ],
         out_specs=[
-            pl.BlockSpec((tile, width), lambda i, s: (((i // per) ^ s[0]) * per + i % per, 0)),
+            pl.BlockSpec((tile, width), lambda i, s: (((i // per) ^ (s[0] // span)) * per + i % per, 0)),
             pl.BlockSpec((tile, width), lambda i, s: (i, 0)),
             pl.BlockSpec((heads, tile, LANES), lambda i, s: (0, i, 0)),
         ],
@@ -600,8 +656,8 @@
     heads, length, _ = keys.shape
     rows = attended.shape[0]
     width = heads * head_size
-    tile = 256 if length <= 4096 else 128
-    per = tokens // tile
+    tile = 2 * tokens if length <= 4096 else 128
+    per, span = max(1, tokens // tile), max(1, tile // tokens)
 
     def body(s_ref, q_ref, d_ref, a_ref, k_ref, v_ref, kt_ref, dq_ref, dk_ref, dv_ref):
         @pl.when(pl.program_id(0) == 0)
@@ -612,7 +668,13 @@
         lane = lax.broadcasted_iota(jnp.int32, (tile, LANES - head_size), 1)
         for h in range(heads):
             cut = slice(h * head_size, (h + 1) * head_size)
-            dout = d_ref[:, cut].astype(f32)
+            dout = jnp.concatenate(
+                [
+                    d_ref[aligned((b ^ s_ref[0]) & (span - 1), tile // span), cut]
+                    for b in range(span)
+                ],
+                axis=0,
+            ).astype(f32)
             parts = three_parts(-jnp.sum(dout * a_ref[:, cut], axis=1, keepdims=True))
             extra = jnp.zeros((tile, LANES - head_size), f32)
             for k in range(3):
@@ -631,7 +693,7 @@
     resident = pl.BlockSpec((heads, length, LANES), lambda i, s: (0, 0, 0))
 
     def dout_map(i, s):
-        return (((i // per) ^ s[0]) * per + i % per, 0)
+        return (((i // per) ^ (s[0] // span)) * per + i % per, 0)
 
     in_specs = [
         pl.BlockSpec((heads, tile, LANES), lambda i, s: (0, i, 0)),
@@ -648,7 +710,7 @@
         [shape(rows, width, dtype=bf16), shape(length, width), shape(length, width)],
         operands,
         scalars=group.reshape(1),
-        limit=vmem_limit if length <= 4096 else 2 * vmem_limit,
+        limit=40 * 1024 * 1024 if length <= 4096 else 2 * vmem_limit,
         grid=(rows // tile,),
         in_specs=in_specs,
         out_specs=[pl.BlockSpec((tile, width), lambda i, s: (i, 0)), whole, whole],
@@ -773,7 +835,7 @@
         [wide, wide, shape(tokens, model), shape(tokens, model)],
         [own, sibling, *[matrix] * 5, bias],
         scalars=f.reshape(1),
-        limit=2 * vmem_limit,
+        limit=50 * 1024 * 1024,
         scratch=[pltpu.VMEM((2 * tokens, model), bf16)],
         grid=(4,),
         in_specs=[whole, whole, *specs, pl.BlockSpec((1, tile), lambda t, s: (0, column(t, s)))],
@@ -861,7 +923,7 @@
         ],
         [own, sibling, slope, *[matrix] * 5],
         scalars=f.reshape(1),
-        limit=2 * vmem_limit,
+        limit=50 * 1024 * 1024,
         scratch=[pltpu.VMEM((2 * tokens, model), bf16)],
         grid=(4,),
         in_specs=[whole, whole, wide, *specs],
@@ -1090,8 +1152,6 @@
     )
     output_received = swap(output_send, "fsdp", 1)
     low = c & 1
-    reduce_keep = reduce_gradient(activated_r, d_reduced_r, sibling_reduced, low)
-    expand_keep = expand_gradients(normed_r, sibling_normed, d_expanded_r, f, (0, 1), 0, shard)
     reduce_send = reduce_gradient(activated_r, d_reduced_r, sibling_reduced, 1 - low, [douts])
     reduce_received = swap(reduce_send, "ctx", 1)
 
@@ -1103,6 +1163,11 @@
         output_keep, output_received, [[(0, shard), rest], [(shard, 2 * shard), rest]]
     )
     output_received = swap(output_send, "fsdp", 2)
+    expand_keep = expand_gradients(
+        normed_r, sibling_normed, d_expanded_r, f, (0, 1), 0, shard
+    )
+    (expand_send,) = add_parts(expand_keep, expand_received, [[(2 * shard, 4 * shard)]])
+    expand_other = swap(expand_send, "fsdp", 1)
     count = ctx_size
     while count > near:
         count //= 2
@@ -1116,42 +1181,39 @@
 
     send, keep = projection_gradients(stream, d_all, f, shard)
     received = swap(send, "fsdp", 1)
-    (expand_send,) = add_parts(expand_keep, expand_received, [[(2 * shard, 4 * shard)]])
-    expand_other = swap(expand_send, "fsdp", 1)
+    cut = ff_block // 2
+    reduce_keep = reduce_gradient(activated_r, d_reduced_r, sibling_reduced, low)
+    reduce_keep, reduce_send = add_parts(
+        reduce_keep, reduce_received, [[(0, cut)], [(cut, 2 * cut)]]
+    )
+    reduce_received = swap(reduce_send, "fsdp", 2)
     send, keep = add_parts(keep, received, [[(0, shard), rest], [(shard, 2 * shard), rest]])
     received = swap(send, "fsdp", 2)
-    cut = ff_block // 2
-    reduce_keep, reduce_send = add_parts(
-        reduce_keep, reduce_received, [[(0, cut)], [(cut, 2 * cut)]]
-    )
-    reduce_received = swap(reduce_send, "fsdp", 2)
-    groups = ctx_groups()
     expander = CtxSum(
-        groups,
+        ctx_groups(2),
         ([expand_keep, expand_received], 0, 2 * shard),
         ([expand_other], 0, 2 * shard),
         ([output_keep, output_received], 0, shard + 16),
     )
+    expander.step()
     mine = sum_all([keep, received])
     count = ctx_size
     while count > near:
         count //= 2
         mine = sum_all([mine, swap(mine, "ctx", count)])
-    projections = lax.all_gather(mine, "ctx", axis=0, tiled=True)
-    expander.step([d_mine])
-    reducer = CtxSum(groups[1:], ([reduce_keep, reduce_received], 0, cut))
+    reducer = CtxSum(ctx_groups()[1:], ([reduce_keep, reduce_received], 0, cut))
+    reducer.step([d_mine])
+    expander.step()
+    reducer.step()
     input_grad = input_gradient(d_first, d_mine, all_projection, near)
-    reducer.step()
-    reducer.step()
-    expander.step()
-    reduced = lax.all_gather(sum_all(reducer.finish()), "ctx", axis=0, tiled=True)
-    expander.step()
-    expanded = lax.all_gather(sum_all(expander.finish()), "ctx", axis=0, tiled=True)
+    reduced, expanded = reducer.finish(), expander.finish()
+    gathered = lax.all_gather(stack_sums(reduced, expanded), "ctx", axis=0, tiled=True)
     grad_query, grad_key, grad_value, grad_bias_query, grad_bias_value = place_projections(
-        projections[: near * (shard + 16)], f, near, width, shard
-    )
-    grad_w_reduce = place_rows(reduced, ctx_size)
-    grad_w_expand, grad_w_output, *small = place_expand(expanded, f, shard, ctx_size)
+        gather_small(mine, near), jnp.stack((group, f)), shard, width, shard
+    )
+    grad_w_reduce, grad_w_expand, grad_w_output, *small = place_gradients(
+        gathered, f, shard, reduced[0].shape[0], ctx_size
+    )
     (
         grad_bias_query,
         grad_bias_value,

time: 488 us -> 461 us (0.945)
  local copies, waits for them, and re-layouts: 67.8 us -> 48.4 us
  waiting for transfers between devices: 235 us -> 217 us
  starting transfers between devices: 47.7 us -> 54.8 us
    ppermute x30 -> x38, waiting for transfers between devices: 169 us -> 130 us  [swap(): return lax.ppermute(array, axis, [(i, i ^ mask) for i in range(size)])]
    unnamed x189 -> x165, local copies, waits for them, and re-layouts: 65.9 us -> 46.4 us
    ppermute x30 -> x38, starting transfers between devices: 32.8 us -> 41.1 us  [swap(): return lax.ppermute(array, axis, [(i, i ^ mask) for i in range(size)])]
    all_gather x1, waiting for transfers between devices: 0.01 us -> 7.84 us  [per_device(): lax.all_gather(cast_feed(w_expand, w_reduce), 'fsdp', axis=0, tiled=True)]
    all_to_all x3, waiting for transfers between devices: 13.7 us -> 21.5 us  [exchange(): return lax.all_to_all(array, 'ctx', 0, 0, tiled=True)]
    all_gather x3 -> x1, waiting for transfers between devices: 51.9 us -> 57.5 us  [per_device(): lax.all_gather(stack_sums(reduced, expanded), 'ctx', axis=0, tiled=True)]
    pallas_call x35 -> x32, Pallas kernels: 120 us -> 122 us  [call(): pl.pallas_call(ordered, out_shape=out_shape, grid_spec=pltpu.PrefetchScal...]
  transfers between devices with their start and end apart: 38 -> 44, of which waited for: 18 -> 21; matrix products, arithmetic and copies ran while one was open for 1% -> 1% of each run, Pallas kernels for 24% -> 24%
where the time goes in v3:
time: 461 us; the launch traced here: 459 us
  waiting for transfers between devices  217 us (47%)
  Pallas kernels  122 us (26%)
  starting transfers between devices  54.8 us (12%)
  local copies, waits for them, and re-layouts  48.4 us (10%)
  between operations  14.5 us (3%)
    ppermute x38, waiting for transfers between devices, swap(): return lax.ppermute(array, axis, [(i, i ^ mask) for i in range(size)])  130 us
    pallas_call x32, Pallas kernels, call(): pl.pallas_call(ordered, out_shape=out_shape, grid_spec=pltpu.PrefetchScal...  122 us
    all_gather x1, waiting for transfers between devices, per_device(): lax.all_gather(stack_sums(reduced, expanded), 'ctx', axis=0, tiled=True)  57.5 us
    unnamed x165, local copies, waits for them, and re-layouts  46.4 us
    ppermute x38, starting transfers between devices, swap(): return lax.ppermute(array, axis, [(i, i ^ mask) for i in range(size)])  41.1 us
    all_to_all x3, waiting for transfers between devices, exchange(): return lax.all_to_all(array, 'ctx', 0, 0, tiled=True)  21.5 us
    all_to_all x3, starting transfers between devices, exchange(): return lax.all_to_all(array, 'ctx', 0, 0, tiled=True)  13.3 us
  transfers between devices with their start and end apart: 44, of which 21 were waited for; matrix products, arithmetic and copies ran while one was open for 1% of the time, Pallas kernels for 24%

profile of v3, /device:TPU:0, one launch (start us, length us, event | category | flops | bytes accessed | tf_op | source)
XLA Modules:
  0.0 459.4 jit_solution(16375765964025386661)
XLA Ops:
  15.8 2.2 copy-done.1
  18.0 4.1 collective-permute-start.3
  29.0 16.4 %collective-permute-done.3.refs_4_.refs_5_ = bf16[256,1024]{1,0:T(8,128)(2,1)S(1)} collective-permute-done((bf16[256,1024]{1,0:T(8,128)(2,1)S(1)}, bf16[256,1024]{1,0:T(8,128)(2,1)S(1)}, u32[]{:S(2)}, u32[]{:S(2)}) %collective-permute-start.3) | collective-permute-done | bytes 524320 | tf_op jit(solution)/shard_map/ppermute | solution.py:34
  55.9 8.0 %collective-permute-done.5.refs_7_ = bf16[256,1024]{1,0:T(8,128)(2,1)} collective-permute-done((bf16[256,1024]{1,0:T(8,128)(2,1)S(1)}, bf16[256,1024]{1,0:T(8,128)(2,1)}, u32[]{:S(2)}, u32[]{:S(2)}) %collective-permute-start.5) | collective-permute-done | bytes 524320 | tf_op jit(solution)/shard_map/ppermute | solution.py:34
  65.2 7.9 %collective-permute-done.11.refs_6_.refs_4_.refs_9_ = bf16[256,1024]{1,0:T(8,128)(2,1)S(1)} collective-permute-done((bf16[256,1024]{1,0:T(8,128)(2,1)S(1)}, bf16[256,1024]{1,0:T(8,128)(2,1)S(1)}, u32[]{:S(2)}, u32[]{:S(2)}) %collective-permute-start.11) | collective-permute-done | bytes 524320 | tf_op jit(solution)/shard_map/ppermute | solution.py:34
  74.8 3.3 collective-permute-done.6.refs_8_
  78.1 7.4 %project.1 = (bf16[2,2048,128]{2,1,0:T(8,128)(2,1)S(1)}, bf16[2,2048,128]{2,1,0:T(8,128)(2,1)S(1)}, bf16[2,2048,128]{2,1,0:T(8,128)(2,1)S(1)}, bf16[128,2048]{1,0:T(8,128)(2,1)S(1)}, bf16[2048,1024]{1,0:T(8,128)(2,1)S(1)}) custom-call(s32[1]{0:T(128)} %bitcast.refs_0_, bf16[256,1024]{1,0:T(8,128)(2,1)S(1)} %cast_all.2.refs_1_, ...), custom_call_target="tpu_custom_call" | custom-call | flops 1 | bytes 1 | tf_op jit(solution)/shard_map/project/pallas_call | solution.py:64
  88.5 12.8 %attend.1 = (bf16[2048,128]{1,0:T(8,128)(2,1)}, f32[2048,128]{1,0:T(8,128)S(1)}, bf16[2,2048,128]{2,1,0:T(8,128)(2,1)S(1)}) custom-call(s32[1]{0:T(128)} %bitcast.1.refs_0_, bf16[2,2048,128]{2,1,0:T(8,128)(2,1)S(1)} %get-tuple-element.86.refs_1_.refs_4_, bf16[2,2048,128]{2,1,0:T(8,128)(2,1)S(1)} %get-tuple-element.87.refs_2_.refs_4_, ...), custom_call_target="tpu_custom_call" | custom-call | flops 1 | bytes 1 | tf_op jit(solution)/shard_map/attend/pallas_call | solution.py:64
  103.2 4.4 all-to-all-start
  107.8 13.8 %all-to-all-done = bf16[8,256,128]{2,1,0:T(8,128)(2,1)S(1)} async-done(((bf16[8,256,128]{2,1,0:T(8,128)(2,1)}), bf16[8,256,128]{2,1,0:T(8,128)(2,1)S(1)}, u32[]{:S(2)}, u32[]{:S(2)}) %all-to-all-start) | async-done | bytes 524320 | tf_op jit(solution)/shard_map/all_to_all | solution.py:109
  128.6 7.8 %all-gather.4.cloned.1.call-done.refs_3_.refs_4_.refs_5_.refs_6_.refs_7_.refs_8_ = bf16[8192,1024]{1,0:T(8,128)(2,1)} async-done(((bf16[2048,1024]{1,0:T(8,128)(2,1)}), bf16[8192,1024]{1,0:T(8,128)(2,1)}) %all-gather.4.cloned.1.call-update) | async-done | bytes 16777232 | tf_op jit(solution)/shard_map/all_gather | solution.py:1059
  136.5 9.3 %feed_forward.1 = (bf16[512,2048]{1,0:T(8,128)(2,1)}, bf16[512,2048]{1,0:T(8,128)(2,1)}, f32[256,1024]{1,0:T(8,128)S(1)}, f32[256,1024]{1,0:T(8,128)S(1)}) custom-call(s32[1]{0:T(128)} %bitcast.refs_0_, bf16[256,1024]{1,0:T(8,128)(2,1)S(1)} %get-tuple-element.91.refs_1_, bf16[256,1024]{1,0:T(8,128)(2,1)S(1)} %collective-permute-done.13.refs_2_, ...), custom_call_target="tpu_custom_call" | custom-call | flops 1 | bytes 1 | tf_op jit(solution)/shard_map/feed_forward/pallas_call | solution.py:64
  146.0 3.6 collective-permute-done.14.refs_2_
  151.2 2.5 second_norm.1
  155.7 8.6 %feed_back.1 = (bf16[512,2048]{1,0:T(8,128)(2,1)}, f32[1,2048]{1,0:T(1,128)S(1)}, f32[256,1024]{1,0:T(8,128)S(1)}, f32[256,1024]{1,0:T(8,128)S(1)}) custom-call(s32[1]{0:T(128)} %bitcast.refs_0_, bf16[256,1024]{1,0:T(8,128)(2,1)S(1)} %get-tuple-element.97.refs_1_.refs_2_, bf16[256,1024]{1,0:T(8,128)(2,1)S(1)} %collective-permute-done.15.refs_2_.refs_3_, ...), custom_call_target="tpu_custom_call" | custom-call | flops 1 | bytes 1 | tf_op jit(solution)/shard_map/feed_back/pallas_call | solution.py:64
  166.1 3.3 expand_gradients.2.refs_11_
  175.2 4.5 all-to-all-start.1
  183.0 2.5 output_gradient.1
  186.6 7.7 %all-to-all-done.1 = bf16[8,256,128]{2,1,0:T(8,128)(2,1)} async-done(((bf16[8,256,128]{2,1,0:T(8,128)(2,1)}), bf16[8,256,128]{2,1,0:T(8,128)(2,1)}, u32[]{:S(2)}, u32[]{:S(2)}) %all-to-all-start.1) | async-done | bytes 524320 | tf_op jit(solution)/shard_map/all_to_all | solution.py:109
  195.6 2.7 reduce_gradient.2.refs_7_
  199.8 23.1 %attend_back.1 = (bf16[2048,128]{1,0:T(8,128)(2,1)S(1)}, f32[2048,128]{1,0:T(8,128)S(1)}, f32[2048,128]{1,0:T(8,128)S(1)}) custom-call(s32[1]{0:T(128)} %bitcast.1.refs_0_, bf16[2,2048,128]{2,1,0:T(8,128)(2,1)S(1)} %copy-done.58, bf16[2048,128]{1,0:T(8,128)(2,1)} %bitcast.16.refs_5_.refs_2_, f32[2048,128]{1,0:T(8,128)S(1)} %copy-done.56, ...), custom_call_target="tpu_custom_call" | custom-call | flops 1 | bytes 1 | tf_op jit(solution)/shard_map/attend_back/pallas_call | solution.py:64
  224.9 2.3 expand_gradients.3.refs_0_.refs_2_.refs_1_
  232.4 4.3 all-to-all-start.2
  241.2 3.3 projection_gradients.1
  246.4 9.4 %collective-permute-done.19.refs_1_ = bf16[1024,1024]{1,0:T(8,128)(2,1)} collective-permute-done((bf16[1024,1024]{1,0:T(8,128)(2,1)}, bf16[1024,1024]{1,0:T(8,128)(2,1)}, u32[]{:S(2)}, u32[]{:S(2)}) %collective-permute-start.19) | collective-permute-done | bytes 2097184 | tf_op jit(solution)/shard_map/ppermute | solution.py:34
  255.8 2.8 add_parts.6
  261.8 4.2 sum_split.4
  266.0 2.5 collective-permute-start.26
  270.1 13.2 %collective-permute-done.22.refs_1_ = bf16[272,384]{1,0:T(8,128)(2,1)S(1)} collective-permute-done((bf16[272,384]{1,0:T(8,128)(2,1)}, bf16[272,384]{1,0:T(8,128)(2,1)S(1)}, u32[]{:S(2)}, u32[]{:S(2)}) %collective-permute-start.22) | collective-permute-done | bytes 208928 | tf_op jit(solution)/shard_map/ppermute | solution.py:34
  284.3 2.6 sum_split.5
  286.9 11.2 %collective-permute-done.26.refs_2_ = bf16[704,1024]{1,0:T(8,128)(2,1)} collective-permute-done((bf16[704,1024]{1,0:T(8,128)(2,1)}, bf16[704,1024]{1,0:T(8,128)(2,1)}, u32[]{:S(2)}, u32[]{:S(2)}) %collective-permute-start.26) | collective-permute-done | bytes 1441824 | tf_op jit(solution)/shard_map/ppermute | solution.py:34
  298.1 3.2 sum_split.6
  302.3 3.6 collective-permute-start.36
  310.4 2.8 copy-done.7
  313.2 4.3 input_gradient.1.refs_6_
  317.4 19.0 %collective-permute-done.36.refs_4_ = bf16[176,1024]{1,0:T(8,128)(2,1)S(1)} collective-permute-done((bf16[176,1024]{1,0:T(8,128)(2,1)}, bf16[176,1024]{1,0:T(8,128)(2,1)S(1)}, u32[]{:S(2)}, u32[]{:S(2)}) %collective-permute-start.36) | collective-permute-done | bytes 360480 | tf_op jit(solution)/shard_map/ppermute | solution.py:34
  336.5 12.4 %collective-permute-done.34.refs_1_ = bf16[128,1024]{1,0:T(8,128)(2,1)S(1)} collective-permute-done((bf16[128,1024]{1,0:T(8,128)(2,1)}, bf16[128,1024]{1,0:T(8,128)(2,1)S(1)}, u32[]{:S(2)}, u32[]{:S(2)}) %collective-permute-start.34) | collective-permute-done | bytes 262176 | tf_op jit(solution)/shard_map/ppermute | solution.py:34
  351.3 2.9 collective-permute-start.30
  355.6 2.5 collective-permute-start.27
  358.1 2.8 collective-permute-done.28.refs_3_
  360.9 2.5 collective-permute-start.29
  363.4 12.1 %collective-permute-done.30.refs_5_ = bf16[272,384]{1,0:T(8,128)(2,1)S(1)} collective-permute-done((bf16[272,384]{1,0:T(8,128)(2,1)S(1)}, bf16[272,384]{1,0:T(8,128)(2,1)S(1)}, u32[]{:S(2)}, u32[]{:S(2)}) %collective-permute-start.30) | collective-permute-done | bytes 208928 | tf_op jit(solution)/shard_map/ppermute | solution.py:34
  375.5 2.6 collective-permute-start.31
  378.1 3.7 collective-permute-done.31.refs_6_
  381.8 2.2 collective-permute-done.33.refs_8_
  384.0 2.3 place_projections.1
  386.4 57.5 %all-gather.8.cloned.1.call-done = bf16[2432,1024]{1,0:T(8,128)(2,1)} async-done(((bf16[304,1024]{1,0:T(8,128)(2,1)}), bf16[2432,1024]{1,0:T(8,128)(2,1)}) %all-gather.8.cloned.1.call-update) | async-done | bytes 4980752 | tf_op jit(solution)/shard_map/all_gather | solution.py:1210
  443.9 9.0 %place_gradients.1 = (f32[1024,1024]{1,0:T(8,128)}, f32[256,4096]{1,0:T(8,128)}, f32[256,1024]{1,0:T(8,128)}, f32[1,256]{1,0:T(1,128)}, f32[1,256]{1,0:T(1,128)}...) custom-call(s32[1]{0:T(128)} %bitcast.refs_0_, ...), custom_call_target="tpu_custom_call" | custom-call | flops 1 | bytes 1 | tf_op jit(solution)/shard_map/place_gradients/pallas_call | solution.py:64
  (259 shorter events, 87.8 us)
Async XLA Ops:
  7.2 129.3 %all-gather.4.cloned.1.call-start = ((), (), s32[]{:S(2)}) async-start(), calls=%async_computation.3 | async-start | bytes 20971520 | tf_op jit(solution)/shard_map/all_gather | solution.py:1059
  14.6 295.8 %all-gather.6.cloned.1.call-start = ((), (), s32[]{:S(2)}) async-start(), calls=%async_computation.4 | async-start | bytes 7864320 | tf_op jit(solution)/shard_map/all_gather | solution.py:1078
  18.0 27.4 %collective-permute-start.3 = (bf16[256,1024]{1,0:T(8,128)(2,1)S(1)}, bf16[256,1024]{1,0:T(8,128)(2,1)S(1)}, u32[]{:S(2)}, u32[]{:S(2)}) collective-permute-start(bf16[256,1024]{1,0:T(8,128)(2,1)S(1)} %cast_all.2.refs_1_), channel_id=1, source_target_pairs={{0,16},{4,20},{8,24},{12,28},{16,0},{20,4},{24,8},{28,12},{1,17},{... | collective-permute-start | bytes 1572872 | tf_op jit(solution)/shard_map/ppermute | solution.py:34
  22.1 23.3 %collective-permute-start = (bf16[256,1024]{1,0:T(8,128)(2,1)S(1)}, bf16[256,1024]{1,0:T(8,128)(2,1)}, u32[]{:S(2)}, u32[]{:S(2)}) collective-permute-start(bf16[256,1024]{1,0:T(8,128)(2,1)S(1)} %cast_all.2.refs_1_), channel_id=1, source_target_pairs={{0,4},{4,0},{8,12},{12,8},{16,20},{20,16},{24,28},{28,24},{1,5},{5... | collective-permute-start | bytes 1572872 | tf_op jit(solution)/shard_map/ppermute | solution.py:34
  23.6 23.2 %collective-permute-start.1 = (bf16[256,1024]{1,0:T(8,128)(2,1)S(1)}, bf16[256,1024]{1,0:T(8,128)(2,1)S(1)}, u32[]{:S(2)}, u32[]{:S(2)}) collective-permute-start(bf16[256,1024]{1,0:T(8,128)(2,1)S(1)} %cast_all.2.refs_1_), channel_id=1, source_target_pairs={{0,8},{4,12},{8,0},{12,4},{16,24},{20,28},{24,16},{28,20},{1,9},{5... | collective-permute-start | bytes 1572872 | tf_op jit(solution)/shard_map/ppermute | solution.py:34
  27.4 23.5 %collective-permute-start.8 = (bf16[256,384]{1,0:T(8,128)(2,1)S(1)}, bf16[256,384]{1,0:T(8,128)(2,1)S(1)}, u32[]{:S(2)}, u32[]{:S(2)}) collective-permute-start(bf16[256,384]{1,0:T(8,128)(2,1)S(1)} %pad_maximum_fusion.refs_9_), channel_id=1, source_target_pairs={{0,2},{1,3},{2,0},{3,1},{4,6},{5,7},{6,4},{7,5},{8,10},{9,11},{10,... | collective-permute-start | bytes 589832 | tf_op jit(solution)/shard_map/ppermute | solution.py:34
  28.9 23.9 %collective-permute-start.7 = (bf16[256,384]{1,0:T(8,128)(2,1)S(1)}, bf16[256,384]{1,0:T(8,128)(2,1)}, u32[]{:S(2)}, u32[]{:S(2)}) collective-permute-start(bf16[256,384]{1,0:T(8,128)(2,1)S(1)} %pad_maximum_fusion.refs_9_), channel_id=1, source_target_pairs={{0,1},{1,0},{2,3},{3,2},{4,5},{5,4},{6,7},{7,6},{8,9},{9,8},{10,11... | collective-permute-start | bytes 589832 | tf_op jit(solution)/shard_map/ppermute | solution.py:34
  48.1 25.0 %collective-permute-start.11 = (bf16[256,1024]{1,0:T(8,128)(2,1)S(1)}, bf16[256,1024]{1,0:T(8,128)(2,1)S(1)}, u32[]{:S(2)}, u32[]{:S(2)}) collective-permute-start(bf16[256,1024]{1,0:T(8,128)(2,1)S(1)} %cast_all.3.refs_3_.refs_2_.refs_7_), channel_id=1, source_target_pairs={{0,2},{1,3},{2,0},{3,1},{4,6},{5,7},{6,4},{7,5},{8,10},{9,11},{10,... | collective-permute-start | bytes 1572872 | tf_op jit(solution)/shard_map/ppermute | solution.py:34
  49.7 14.2 %collective-permute-start.5 = (bf16[256,1024]{1,0:T(8,128)(2,1)S(1)}, bf16[256,1024]{1,0:T(8,128)(2,1)}, u32[]{:S(2)}, u32[]{:S(2)}) collective-permute-start(bf16[256,1024]{1,0:T(8,128)(2,1)S(1)} %collective-permute-done.3.refs_4_.refs_5_), channel_id=1, source_target_pairs={{0,8},{4,12},{8,0},{12,4},{16,24},{20,28},{24,16},{28,20},{1,9},{5... | collective-permute-start | bytes 1572872 | tf_op jit(solution)/shard_map/ppermute | solution.py:34
  50.9 3.5 collective-permute-start.9
  52.3 36.0 %collective-permute-start.10 = (bf16[256,1024]{1,0:T(8,128)(2,1)S(1)}, bf16[256,1024]{1,0:T(8,128)(2,1)S(1)}, u32[]{:S(2)}, u32[]{:S(2)}) collective-permute-start(bf16[256,1024]{1,0:T(8,128)(2,1)S(1)} %cast_all.3.refs_3_.refs_2_.refs_7_), channel_id=1, source_target_pairs={{0,1},{1,0},{2,3},{3,2},{4,5},{5,4},{6,7},{7,6},{8,9},{9,8},{10,11... | collective-permute-start | bytes 1572872 | tf_op jit(solution)/shard_map/ppermute | solution.py:34
  52.8 21.9 %collective-permute-start.4 = (bf16[256,1024]{1,0:T(8,128)(2,1)S(1)}, bf16[256,1024]{1,0:T(8,128)(2,1)}, u32[]{:S(2)}, u32[]{:S(2)}) collective-permute-start(bf16[256,1024]{1,0:T(8,128)(2,1)S(1)} %collective-permute-done.3.refs_4_.refs_5_), channel_id=1, source_target_pairs={{0,4},{4,0},{8,12},{12,8},{16,20},{20,16},{24,28},{28,24},{1,5},{5... | collective-permute-start | bytes 1572872 | tf_op jit(solution)/shard_map/ppermute | solution.py:34
  55.1 19.7 %collective-permute-start.2 = (bf16[256,1024]{1,0:T(8,128)(2,1)}, bf16[256,1024]{1,0:T(8,128)(2,1)}, u32[]{:S(2)}, u32[]{:S(2)}) collective-permute-start(bf16[256,1024]{1,0:T(8,128)(2,1)} %collective-permute-done.refs_2_), channel_id=1, source_target_pairs={{0,8},{4,12},{8,0},{12,4},{16,24},{20,28},{24,16},{28,20},{1,9},{5... | collective-permute-start | bytes 1572872 | tf_op jit(solution)/shard_map/ppermute | solution.py:34
  63.9 14.2 %collective-permute-start.6 = (bf16[256,1024]{1,0:T(8,128)(2,1)}, bf16[256,1024]{1,0:T(8,128)(2,1)}, u32[]{:S(2)}, u32[]{:S(2)}) collective-permute-start(bf16[256,1024]{1,0:T(8,128)(2,1)} %collective-permute-done.5.refs_7_), channel_id=1, source_target_pairs={{0,4},{4,0},{8,12},{12,8},{16,20},{20,16},{24,28},{28,24},{1,5},{5... | collective-permute-start | bytes 1572872 | tf_op jit(solution)/shard_map/ppermute | solution.py:34
  73.1 15.3 %collective-permute-start.12 = (bf16[256,1024]{1,0:T(8,128)(2,1)S(1)}, bf16[256,1024]{1,0:T(8,128)(2,1)S(1)}, u32[]{:S(2)}, u32[]{:S(2)}) collective-permute-start(bf16[256,1024]{1,0:T(8,128)(2,1)S(1)} %collective-permute-done.11.refs_6_.refs_4_.refs_9_), channel_id=1, source_target_pairs={{0,1},{1,0},{2,3},{3,2},{4,5},{5,4},{6,7},{7,6},{8,9},{9,8},{10,11... | collective-permute-start | bytes 1572872 | tf_op jit(solution)/shard_map/ppermute | solution.py:34
  88.4 33.2 %copy-start.14 = (bf16[256,1024]{1,0:T(8,128)(2,1)}, bf16[256,1024]{1,0:T(8,128)(2,1)S(1)}, u32[]{:S(2)}) copy-start(bf16[256,1024]{1,0:T(8,128)(2,1)S(1)} %collective-permute-done.10.refs_5_.refs_3_.refs_8_) | copy-start | bytes 1572868
  103.2 18.4 %all-to-all-start = ((bf16[8,256,128]{2,1,0:T(8,128)(2,1)}), bf16[8,256,128]{2,1,0:T(8,128)(2,1)S(1)}, u32[]{:S(2)}, u32[]{:S(2)}) async-start(bf16[8,256,128]{2,1,0:T(8,128)(2,1)} %bitcast.4), calls=%async_computation | async-start | bytes 1048576 | tf_op jit(solution)/shard_map/all_to_all | solution.py:109
  126.7 37.7 %copy-start.10 = (bf16[256,1024]{1,0:T(8,128)(2,1)}, bf16[256,1024]{1,0:T(8,128)(2,1)S(1)}, u32[]{:S(2)}) copy-start(bf16[256,1024]{1,0:T(8,128)(2,1)S(1)} %get-tuple-element.91.refs_1_) | copy-start | bytes 1572868
  126.7 1.9 collective-permute-start.13
  128.6 35.7 %copy-start.12 = (bf16[256,1024]{1,0:T(8,128)(2,1)}, bf16[256,1024]{1,0:T(8,128)(2,1)S(1)}, u32[]{:S(2)}) copy-start(bf16[256,1024]{1,0:T(8,128)(2,1)S(1)} %collective-permute-done.13.refs_2_) | copy-start | bytes 1572868
  145.8 3.9 collective-permute-start.14
  153.7 1.9 collective-permute-start.15
  164.3 6.9 %collective-permute-start.16 = (f32[256,1024]{1,0:T(8,128)S(1)}, f32[256,1024]{1,0:T(8,128)S(1)}, u32[]{:S(2)}, u32[]{:S(2)}) collective-permute-start(f32[256,1024]{1,0:T(8,128)S(1)} %get-tuple-element.100), channel_id=1, source_target_pairs={{0,1},{1,0},{2,3},{3,2},{4,5},{5,4},{6,7},{7,6},{8,9},{9,8},{10,11... | collective-permute-start | bytes 3145736 | tf_op jit(solution)/shard_map/ppermute | solution.py:34
  169.4 57.8 %collective-permute-start.18 = (bf16[1024,1024]{1,0:T(8,128)(2,1)}, bf16[1024,1024]{1,0:T(8,128)(2,1)}, u32[]{:S(2)}, u32[]{:S(2)}) collective-permute-start(bf16[1024,1024]{1,0:T(8,128)(2,1)} %expand_gradients.2.refs_11_), channel_id=1, source_target_pairs={{0,2},{1,3},{2,0},{3,1},{4,6},{5,7},{6,4},{7,5},{8,10},{9,11},{10,... | collective-permute-start | bytes 6291464 | tf_op jit(solution)/shard_map/ppermute | solution.py:34
  175.2 19.1 %all-to-all-start.1 = ((bf16[8,256,128]{2,1,0:T(8,128)(2,1)}), bf16[8,256,128]{2,1,0:T(8,128)(2,1)}, u32[]{:S(2)}, u32[]{:S(2)}) async-start(bf16[8,256,128]{2,1,0:T(8,128)(2,1)} %bitcast.45), calls=%async_computation.1 | async-start | bytes 1048576 | tf_op jit(solution)/shard_map/all_to_all | solution.py:109
  186.6 36.3 %collective-permute-start.17 = (bf16[528,1024]{1,0:T(8,128)(2,1)}, bf16[528,1024]{1,0:T(8,128)(2,1)}, u32[]{:S(2)}, u32[]{:S(2)}) collective-permute-start(bf16[528,1024]{1,0:T(8,128)(2,1)} %get-tuple-element.118), channel_id=1, source_target_pairs={{0,1},{1,0},{2,3},{3,2},{4,5},{5,4},{6,7},{7,6},{8,9},{9,8},{10,11... | collective-permute-start | bytes 3244040 | tf_op jit(solution)/shard_map/ppermute | solution.py:34
  198.3 57.5 %collective-permute-start.19 = (bf16[1024,1024]{1,0:T(8,128)(2,1)}, bf16[1024,1024]{1,0:T(8,128)(2,1)}, u32[]{:S(2)}, u32[]{:S(2)}) collective-permute-start(bf16[1024,1024]{1,0:T(8,128)(2,1)} %reduce_gradient.2.refs_7_), channel_id=1, source_target_pairs={{0,4},{4,0},{8,12},{12,8},{16,20},{20,16},{24,28},{28,24},{1,5},{5... | collective-permute-start | bytes 6291464 | tf_op jit(solution)/shard_map/ppermute | solution.py:34
  232.4 51.9 %all-to-all-start.2 = ((bf16[8,256,384]{2,1,0:T(8,128)(2,1)}), bf16[8,256,384]{2,1,0:T(8,128)(2,1)}, u32[]{:S(2)}, u32[]{:S(2)}) async-start(bf16[8,256,384]{2,1,0:T(8,128)(2,1)} %bitcast.43), calls=%async_computation.2 | async-start | bytes 3145728 | tf_op jit(solution)/shard_map/all_to_all | solution.py:109
  236.7 207.2 %all-gather.8.cloned.1.call-start = ((), (), s32[]{:S(2)}) async-start(), calls=%async_computation.5 | async-start | bytes 5603328 | tf_op jit(solution)/shard_map/all_gather | solution.py:1210
  237.0 24.7 %collective-permute-start.23 = (bf16[512,1024]{1,0:T(8,128)(2,1)}, bf16[512,1024]{1,0:T(8,128)(2,1)}, u32[]{:S(2)}, u32[]{:S(2)}) collective-permute-start(bf16[512,1024]{1,0:T(8,128)(2,1)} %copy-done.35), channel_id=1, source_target_pairs={{0,1},{1,0},{2,3},{3,2},{4,5},{5,4},{6,7},{7,6},{8,9},{9,8},{10,11... | collective-permute-start | bytes 3145736 | tf_op jit(solution)/shard_map/ppermute | solution.py:34
  237.1 24.6 %collective-permute-start.24 = (bf16[272,1024]{1,0:T(8,128)(2,1)}, bf16[272,1024]{1,0:T(8,128)(2,1)}, u32[]{:S(2)}, u32[]{:S(2)}) collective-permute-start(bf16[272,1024]{1,0:T(8,128)(2,1)} %copy-done.73), channel_id=1, source_target_pairs={{0,2},{1,3},{2,0},{3,1},{4,6},{5,7},{6,4},{7,5},{8,10},{9,11},{10,... | collective-permute-start | bytes 1671176 | tf_op jit(solution)/shard_map/ppermute | solution.py:34
  244.5 14.4 %collective-permute-start.21 = (bf16[528,384]{1,0:T(8,128)(2,1)S(1)}, bf16[528,384]{1,0:T(8,128)(2,1)}, u32[]{:S(2)}, u32[]{:S(2)}) collective-permute-start(bf16[528,384]{1,0:T(8,128)(2,1)S(1)} %get-tuple-element.123.refs_4_), channel_id=1, source_target_pairs={{0,1},{1,0},{2,3},{3,2},{4,5},{5,4},{6,7},{7,6},{8,9},{9,8},{10,11... | collective-permute-start | bytes 1216520 | tf_op jit(solution)/shard_map/ppermute | solution.py:34
  258.6 25.7 %collective-permute-start.20 = (bf16[512,1024]{1,0:T(8,128)(2,1)}, bf16[512,1024]{1,0:T(8,128)(2,1)}, u32[]{:S(2)}, u32[]{:S(2)}) collective-permute-start(bf16[512,1024]{1,0:T(8,128)(2,1)} %get-tuple-element.125), channel_id=1, source_target_pairs={{0,2},{1,3},{2,0},{3,1},{4,6},{5,7},{6,4},{7,5},{8,10},{9,11},{10,... | collective-permute-start | bytes 3145736 | tf_op jit(solution)/shard_map/ppermute | solution.py:34
  266.0 32.2 %collective-permute-start.26 = (bf16[704,1024]{1,0:T(8,128)(2,1)}, bf16[704,1024]{1,0:T(8,128)(2,1)}, u32[]{:S(2)}, u32[]{:S(2)}) collective-permute-start(bf16[704,1024]{1,0:T(8,128)(2,1)} %get-tuple-element.133), channel_id=1, source_target_pairs={{0,4},{4,0},{8,12},{12,8},{16,20},{20,16},{24,28},{28,24},{1,5},{5... | collective-permute-start | bytes 4325384 | tf_op jit(solution)/shard_map/ppermute | solution.py:34
  268.4 14.8 %collective-permute-start.22 = (bf16[272,384]{1,0:T(8,128)(2,1)}, bf16[272,384]{1,0:T(8,128)(2,1)S(1)}, u32[]{:S(2)}, u32[]{:S(2)}) collective-permute-start(bf16[272,384]{1,0:T(8,128)(2,1)} %get-tuple-element.128.refs_6_), channel_id=1, source_target_pairs={{0,2},{1,3},{2,0},{3,1},{4,6},{5,7},{6,4},{7,5},{8,10},{9,11},{10,... | collective-permute-start | bytes 626696 | tf_op jit(solution)/shard_map/ppermute | solution.py:34
  286.9 19.5 %collective-permute-start.25 = (bf16[256,1024]{1,0:T(8,128)(2,1)}, bf16[256,1024]{1,0:T(8,128)(2,1)}, u32[]{:S(2)}, u32[]{:S(2)}) collective-permute-start(bf16[256,1024]{1,0:T(8,128)(2,1)} %get-tuple-element.132), channel_id=1, source_target_pairs={{0,8},{4,12},{8,0},{12,4},{16,24},{20,28},{24,16},{28,20},{1,9},{5... | collective-permute-start | bytes 1572872 | tf_op jit(solution)/shard_map/ppermute | solution.py:34
  302.1 15.4 %collective-permute-start.35 = (bf16[176,1024]{1,0:T(8,128)(2,1)}, bf16[176,1024]{1,0:T(8,128)(2,1)S(1)}, u32[]{:S(2)}, u32[]{:S(2)}) collective-permute-start(bf16[176,1024]{1,0:T(8,128)(2,1)} %get-tuple-element.137), channel_id=1, source_target_pairs={{0,8},{4,12},{8,0},{12,4},{16,24},{20,28},{24,16},{28,20},{1,9},{5... | collective-permute-start | bytes 1081352 | tf_op jit(solution)/shard_map/ppermute | solution.py:34
  302.3 34.2 %collective-permute-start.36 = (bf16[176,1024]{1,0:T(8,128)(2,1)}, bf16[176,1024]{1,0:T(8,128)(2,1)S(1)}, u32[]{:S(2)}, u32[]{:S(2)}) collective-permute-start(bf16[176,1024]{1,0:T(8,128)(2,1)} %get-tuple-element.138), channel_id=1, source_target_pairs={{0,16},{4,20},{8,24},{12,28},{16,0},{20,4},{24,8},{28,12},{1,17},{... | collective-permute-start | bytes 1081352 | tf_op jit(solution)/shard_map/ppermute | solution.py:34
  305.9 30.6 %collective-permute-start.37 = (bf16[176,1024]{1,0:T(8,128)(2,1)}, bf16[176,1024]{1,0:T(8,128)(2,1)S(1)}, u32[]{:S(2)}, u32[]{:S(2)}) collective-permute-start(bf16[176,1024]{1,0:T(8,128)(2,1)} %get-tuple-element.139), channel_id=1, source_target_pairs={{0,24},{4,28},{8,16},{12,20},{16,8},{20,12},{24,0},{28,4},{1,25},{... | collective-permute-start | bytes 1081352 | tf_op jit(solution)/shard_map/ppermute | solution.py:34
  309.5 39.4 %collective-permute-start.34 = (bf16[128,1024]{1,0:T(8,128)(2,1)}, bf16[128,1024]{1,0:T(8,128)(2,1)S(1)}, u32[]{:S(2)}, u32[]{:S(2)}) collective-permute-start(bf16[128,1024]{1,0:T(8,128)(2,1)} %get-tuple-element.136), channel_id=1, source_target_pairs={{0,16},{4,20},{8,24},{12,28},{16,0},{20,4},{24,8},{28,12},{1,17},{... | collective-permute-start | bytes 786440 | tf_op jit(solution)/shard_map/ppermute | solution.py:34
  313.2 35.7 %copy-start.47 = (bf16[176,1024]{1,0:T(8,128)(2,1)S(1)}, bf16[176,1024]{1,0:T(8,128)(2,1)}, u32[]{:S(2)}) copy-start(bf16[176,1024]{1,0:T(8,128)(2,1)} %copy-done.45) | copy-start | bytes 1081348
  351.2 9.7 %collective-permute-start.28 = (bf16[272,384]{1,0:T(8,128)(2,1)S(1)}, bf16[272,384]{1,0:T(8,128)(2,1)S(1)}, u32[]{:S(2)}, u32[]{:S(2)}) collective-permute-start(bf16[272,384]{1,0:T(8,128)(2,1)S(1)} %sum_all.1.refs_3_.refs_1_), channel_id=1, source_target_pairs={{0,8},{4,12},{8,0},{12,4},{16,24},{20,28},{24,16},{28,20},{1,9},{5... | collective-permute-start | bytes 626696 | tf_op jit(solution)/shard_map/ppermute | solution.py:34
  351.3 24.2 %collective-permute-start.30 = (bf16[272,384]{1,0:T(8,128)(2,1)S(1)}, bf16[272,384]{1,0:T(8,128)(2,1)S(1)}, u32[]{:S(2)}, u32[]{:S(2)}) collective-permute-start(bf16[272,384]{1,0:T(8,128)(2,1)S(1)} %sum_all.1.refs_3_.refs_1_), channel_id=1, source_target_pairs={{0,16},{4,20},{8,24},{12,28},{16,0},{20,4},{24,8},{28,12},{1,17},{... | collective-permute-start | bytes 626696 | tf_op jit(solution)/shard_map/ppermute | solution.py:34
  354.2 23.8 %collective-permute-start.32 = (bf16[272,384]{1,0:T(8,128)(2,1)S(1)}, bf16[272,384]{1,0:T(8,128)(2,1)S(1)}, u32[]{:S(2)}, u32[]{:S(2)}) collective-permute-start(bf16[272,384]{1,0:T(8,128)(2,1)S(1)} %sum_all.1.refs_3_.refs_1_), channel_id=1, source_target_pairs={{0,24},{4,28},{8,16},{12,20},{16,8},{20,12},{24,0},{28,4},{1,25},{... | collective-permute-start | bytes 626696 | tf_op jit(solution)/shard_map/ppermute | solution.py:34
  355.6 22.5 %collective-permute-start.27 = (bf16[272,384]{1,0:T(8,128)(2,1)S(1)}, bf16[272,384]{1,0:T(8,128)(2,1)S(1)}, u32[]{:S(2)}, u32[]{:S(2)}) collective-permute-start(bf16[272,384]{1,0:T(8,128)(2,1)S(1)} %sum_all.1.refs_3_.refs_1_), channel_id=1, source_target_pairs={{0,4},{4,0},{8,12},{12,8},{16,20},{20,16},{24,28},{28,24},{1,5},{5... | collective-permute-start | bytes 626696 | tf_op jit(solution)/shard_map/ppermute | solution.py:34
  360.9 17.2 %collective-permute-start.29 = (bf16[272,384]{1,0:T(8,128)(2,1)S(1)}, bf16[272,384]{1,0:T(8,128)(2,1)S(1)}, u32[]{:S(2)}, u32[]{:S(2)}) collective-permute-start(bf16[272,384]{1,0:T(8,128)(2,1)S(1)} %collective-permute-done.28.refs_3_), channel_id=1, source_target_pairs={{0,4},{4,0},{8,12},{12,8},{16,20},{20,16},{24,28},{28,24},{1,5},{5... | collective-permute-start | bytes 626696 | tf_op jit(solution)/shard_map/ppermute | solution.py:34
  375.5 6.3 %collective-permute-start.31 = (bf16[272,384]{1,0:T(8,128)(2,1)S(1)}, bf16[272,384]{1,0:T(8,128)(2,1)S(1)}, u32[]{:S(2)}, u32[]{:S(2)}) collective-permute-start(bf16[272,384]{1,0:T(8,128)(2,1)S(1)} %collective-permute-done.30.refs_5_), channel_id=1, source_target_pairs={{0,4},{4,0},{8,12},{12,8},{16,20},{20,16},{24,28},{28,24},{1,5},{5... | collective-permute-start | bytes 626696 | tf_op jit(solution)/shard_map/ppermute | solution.py:34
  378.0 6.0 %collective-permute-start.33 = (bf16[272,384]{1,0:T(8,128)(2,1)S(1)}, bf16[272,384]{1,0:T(8,128)(2,1)S(1)}, u32[]{:S(2)}, u32[]{:S(2)}) collective-permute-start(bf16[272,384]{1,0:T(8,128)(2,1)S(1)} %collective-permute-done.32.refs_7_), channel_id=1, source_target_pairs={{0,4},{4,0},{8,12},{12,8},{16,20},{20,16},{24,28},{28,24},{1,5},{5... | collective-permute-start | bytes 626696 | tf_op jit(solution)/shard_map/ppermute | solution.py:34
  (78 other events, 552.4 us)
Sparse Core Ops, SparseCore 0:
  14.7 121.7 all-gather.3
  138.0 52.8 all-gather.5
  351.3 92.5 all-gather.7

commit v4 on v3

--- a/solution.py
+++ b/solution.py
@@ -219,12 +219,12 @@
     )
 
 
-def place_gradients(gathered, f, shard, rows, size):
+def place_gradients(gathered, vectors, f, shard, rows, size):
     piece = gathered.shape[0] // size
     columns = gathered.shape[1]
     below = piece - rows
 
-    def body(f_ref, in_ref, reduce_ref, expand_ref, output_ref, *refs):
+    def body(f_ref, in_ref, v_ref, reduce_ref, expand_ref, output_ref, *refs):
         outs, ordered, small = refs[:-2], refs[-2], refs[-1]
         at = pl.program_id(0)
         reduce_ref[...] = in_ref[0, :rows, :].astype(f32)
@@ -237,7 +237,7 @@
                     unit * shard : (unit + 1) * shard, :
                 ].astype(f32)
             output_ref[...] = ordered[4 * shard : 5 * shard, :].astype(f32)
-            small[...] = ordered[5 * shard : 5 * shard + 16, :].astype(f32)
+            small[...] = v_ref[...].astype(f32)
             for k in range(6):
                 outs[k][...] = small[k : k + 1, aligned(f_ref[0], shard)]
             outs[6][...] = small[pl.ds(8 + f_ref[0], 1), :]
@@ -251,12 +251,12 @@
         [shape(size * rows, columns), shape(shard, 4 * columns), shape(shard, columns)]
         + [shape(1, shard)] * 6
         + [shape(1, columns)],
-        [gathered.reshape(size, piece, columns)],
+        [gathered.reshape(size, piece, columns), vectors],
         scalars=f.reshape(1),
         scratch=[pltpu.VMEM((size * below, columns), bf16), pltpu.VMEM((16, columns), f32)],
         limit=2 * vmem_limit,
         grid=(size,),
-        in_specs=[pl.BlockSpec((1, piece, columns), lambda j, s: (j, 0, 0))],
+        in_specs=[pl.BlockSpec((1, piece, columns), lambda j, s: (j, 0, 0)), whole(16, columns)],
         out_specs=[
             pl.BlockSpec((rows, columns), lambda j, s: (piece_of(j, size), 0)),
             whole(shard, 4 * columns),
@@ -1193,7 +1193,7 @@
         ctx_groups(2),
         ([expand_keep, expand_received], 0, 2 * shard),
         ([expand_other], 0, 2 * shard),
-        ([output_keep, output_received], 0, shard + 16),
+        ([output_keep, output_received], 0, shard),
     )
     expander.step()
     mine = sum_all([keep, received])
@@ -1208,11 +1208,14 @@
     input_grad = input_gradient(d_first, d_mine, all_projection, near)
     reduced, expanded = reducer.finish(), expander.finish()
     gathered = lax.all_gather(stack_sums(reduced, expanded), "ctx", axis=0, tiled=True)
+    (vectors,) = add_parts(output_keep, output_received, [[(shard, shard + 16)]])
+    for bit, _ in ctx_groups():
+        vectors = sum_all([vectors, swap(vectors, "ctx", 1 << bit)])
     grad_query, grad_key, grad_value, grad_bias_query, grad_bias_value = place_projections(
         gather_small(mine, near), jnp.stack((group, f)), shard, width, shard
     )
     grad_w_reduce, grad_w_expand, grad_w_output, *small = place_gradients(
-        gathered, f, shard, reduced[0].shape[0], ctx_size
+        gathered, vectors, f, shard, reduced[0].shape[0], ctx_size
     )
     (
         grad_bias_query,

time: 461 us -> 452 us (0.980)
  waiting for transfers between devices: 217 us -> 191 us
  starting transfers between devices: 54.8 us -> 70.1 us
    all_gather x1, waiting for transfers between devices: 57.5 us -> 34.7 us  [per_device(): lax.all_gather(stack_sums(reduced, expanded), 'ctx', axis=0, tiled=True)]
    ppermute x38 -> x41, starting transfers between devices: 41.1 us -> 56.5 us  [swap(): return lax.ppermute(array, axis, [(i, i ^ mask) for i in range(size)])]
    ppermute x38 -> x41, waiting for transfers between devices: 130 us -> 127 us  [swap(): return lax.ppermute(array, axis, [(i, i ^ mask) for i in range(size)])]
    unnamed x165 -> x169, local copies, waits for them, and re-layouts: 46.4 us -> 47.4 us
    pallas_call x32 -> x36, Pallas kernels: 122 us -> 122 us  [call(): pl.pallas_call(ordered, out_shape=out_shape, grid_spec=pltpu.PrefetchScal...]
  transfers between devices with their start and end apart: 44 -> 47, of which waited for: 21 -> 22; matrix products, arithmetic and copies ran while one was open for 1% -> 1% of each run, Pallas kernels for 24% -> 25%
where the time goes in v4:
time: 452 us; the launch traced here: 450 us
  waiting for transfers between devices  191 us (42%)
  Pallas kernels  122 us (27%)
  starting transfers between devices  70.1 us (16%)
  local copies, waits for them, and re-layouts  49.4 us (11%)
  between operations  14.5 us (3%)
    ppermute x41, waiting for transfers between devices, swap(): return lax.ppermute(array, axis, [(i, i ^ mask) for i in range(size)])  127 us
    pallas_call x36, Pallas kernels, call(): pl.pallas_call(ordered, out_shape=out_shape, grid_spec=pltpu.PrefetchScal...  122 us
    ppermute x41, starting transfers between devices, swap(): return lax.ppermute(array, axis, [(i, i ^ mask) for i in range(size)])  56.5 us
    unnamed x169, local copies, waits for them, and re-layouts  47.4 us
    all_gather x1, waiting for transfers between devices, per_device(): lax.all_gather(stack_sums(reduced, expanded), 'ctx', axis=0, tiled=True)  34.7 us
    all_to_all x3, waiting for transfers between devices, exchange(): return lax.all_to_all(array, 'ctx', 0, 0, tiled=True)  21.5 us
    all_to_all x3, starting transfers between devices, exchange(): return lax.all_to_all(array, 'ctx', 0, 0, tiled=True)  13.2 us
  transfers between devices with their start and end apart: 47, of which 22 were waited for; matrix products, arithmetic and copies ran while one was open for 1% of the time, Pallas kernels for 25%

profile of v4, /device:TPU:0, one launch (start us, length us, event | category | flops | bytes accessed | tf_op | source)
XLA Modules:
  0.0 449.9 jit_solution(13429742364639310085)
XLA Ops:
  18.0 4.1 collective-permute-start.3
  29.0 16.4 %collective-permute-done.3.refs_4_.refs_5_ = bf16[256,1024]{1,0:T(8,128)(2,1)S(1)} collective-permute-done((bf16[256,1024]{1,0:T(8,128)(2,1)S(1)}, bf16[256,1024]{1,0:T(8,128)(2,1)S(1)}, u32[]{:S(2)}, u32[]{:S(2)}) %collective-permute-start.3) | collective-permute-done | bytes 524320 | tf_op jit(solution)/shard_map/ppermute | solution.py:34
  55.9 8.1 %collective-permute-done.5.refs_7_ = bf16[256,1024]{1,0:T(8,128)(2,1)} collective-permute-done((bf16[256,1024]{1,0:T(8,128)(2,1)S(1)}, bf16[256,1024]{1,0:T(8,128)(2,1)}, u32[]{:S(2)}, u32[]{:S(2)}) %collective-permute-start.5) | collective-permute-done | bytes 524320 | tf_op jit(solution)/shard_map/ppermute | solution.py:34
  65.2 7.9 %collective-permute-done.11.refs_6_.refs_4_.refs_9_ = bf16[256,1024]{1,0:T(8,128)(2,1)S(1)} collective-permute-done((bf16[256,1024]{1,0:T(8,128)(2,1)S(1)}, bf16[256,1024]{1,0:T(8,128)(2,1)S(1)}, u32[]{:S(2)}, u32[]{:S(2)}) %collective-permute-start.11) | collective-permute-done | bytes 524320 | tf_op jit(solution)/shard_map/ppermute | solution.py:34
  74.8 3.3 collective-permute-done.6.refs_8_
  78.1 7.4 %project.1 = (bf16[2,2048,128]{2,1,0:T(8,128)(2,1)S(1)}, bf16[2,2048,128]{2,1,0:T(8,128)(2,1)S(1)}, bf16[2,2048,128]{2,1,0:T(8,128)(2,1)S(1)}, bf16[128,2048]{1,0:T(8,128)(2,1)S(1)}, bf16[2048,1024]{1,0:T(8,128)(2,1)S(1)}) custom-call(s32[1]{0:T(128)} %bitcast.refs_0_, bf16[256,1024]{1,0:T(8,128)(2,1)S(1)} %cast_all.2.refs_1_, ...), custom_call_target="tpu_custom_call" | custom-call | flops 1 | bytes 1 | tf_op jit(solution)/shard_map/project/pallas_call | solution.py:64
  88.4 12.8 %attend.1 = (bf16[2048,128]{1,0:T(8,128)(2,1)}, f32[2048,128]{1,0:T(8,128)S(1)}, bf16[2,2048,128]{2,1,0:T(8,128)(2,1)S(1)}) custom-call(s32[1]{0:T(128)} %bitcast.1.refs_0_, bf16[2,2048,128]{2,1,0:T(8,128)(2,1)S(1)} %get-tuple-element.86.refs_1_.refs_4_, bf16[2,2048,128]{2,1,0:T(8,128)(2,1)S(1)} %get-tuple-element.87.refs_2_.refs_4_, ...), custom_call_target="tpu_custom_call" | custom-call | flops 1 | bytes 1 | tf_op jit(solution)/shard_map/attend/pallas_call | solution.py:64
  103.1 4.4 all-to-all-start
  107.8 13.8 %all-to-all-done = bf16[8,256,128]{2,1,0:T(8,128)(2,1)S(1)} async-done(((bf16[8,256,128]{2,1,0:T(8,128)(2,1)}), bf16[8,256,128]{2,1,0:T(8,128)(2,1)S(1)}, u32[]{:S(2)}, u32[]{:S(2)}) %all-to-all-start) | async-done | bytes 524320 | tf_op jit(solution)/shard_map/all_to_all | solution.py:109
  128.6 7.9 %all-gather.4.cloned.1.call-done.refs_3_.refs_4_.refs_5_.refs_6_.refs_7_.refs_8_ = bf16[8192,1024]{1,0:T(8,128)(2,1)} async-done(((bf16[2048,1024]{1,0:T(8,128)(2,1)}), bf16[8192,1024]{1,0:T(8,128)(2,1)}) %all-gather.4.cloned.1.call-update) | async-done | bytes 16777232 | tf_op jit(solution)/shard_map/all_gather | solution.py:1059
  136.5 9.3 %feed_forward.1 = (bf16[512,2048]{1,0:T(8,128)(2,1)}, bf16[512,2048]{1,0:T(8,128)(2,1)}, f32[256,1024]{1,0:T(8,128)S(1)}, f32[256,1024]{1,0:T(8,128)S(1)}) custom-call(s32[1]{0:T(128)} %bitcast.refs_0_, bf16[256,1024]{1,0:T(8,128)(2,1)S(1)} %get-tuple-element.91.refs_1_, bf16[256,1024]{1,0:T(8,128)(2,1)S(1)} %collective-permute-done.13.refs_2_, ...), custom_call_target="tpu_custom_call" | custom-call | flops 1 | bytes 1 | tf_op jit(solution)/shard_map/feed_forward/pallas_call | solution.py:64
  146.1 3.6 collective-permute-done.14.refs_2_
  151.2 2.5 second_norm.1
  155.7 8.6 %feed_back.1 = (bf16[512,2048]{1,0:T(8,128)(2,1)}, f32[1,2048]{1,0:T(1,128)S(1)}, f32[256,1024]{1,0:T(8,128)S(1)}, f32[256,1024]{1,0:T(8,128)S(1)}) custom-call(s32[1]{0:T(128)} %bitcast.refs_0_, bf16[256,1024]{1,0:T(8,128)(2,1)S(1)} %get-tuple-element.97.refs_1_.refs_2_, bf16[256,1024]{1,0:T(8,128)(2,1)S(1)} %collective-permute-done.15.refs_2_.refs_3_, ...), custom_call_target="tpu_custom_call" | custom-call | flops 1 | bytes 1 | tf_op jit(solution)/shard_map/feed_back/pallas_call | solution.py:64
  166.1 3.3 expand_gradients.2.refs_11_
  175.2 4.5 all-to-all-start.1
  183.0 2.5 output_gradient.1
  186.6 7.7 %all-to-all-done.1 = bf16[8,256,128]{2,1,0:T(8,128)(2,1)} async-done(((bf16[8,256,128]{2,1,0:T(8,128)(2,1)}), bf16[8,256,128]{2,1,0:T(8,128)(2,1)}, u32[]{:S(2)}, u32[]{:S(2)}) %all-to-all-start.1) | async-done | bytes 524320 | tf_op jit(solution)/shard_map/all_to_all | solution.py:109
  195.5 2.7 reduce_gradient.2.refs_7_
  199.7 23.1 %attend_back.1 = (bf16[2048,128]{1,0:T(8,128)(2,1)S(1)}, f32[2048,128]{1,0:T(8,128)S(1)}, f32[2048,128]{1,0:T(8,128)S(1)}) custom-call(s32[1]{0:T(128)} %bitcast.1.refs_0_, bf16[2,2048,128]{2,1,0:T(8,128)(2,1)S(1)} %copy-done.59, bf16[2048,128]{1,0:T(8,128)(2,1)} %bitcast.16.refs_5_.refs_2_, f32[2048,128]{1,0:T(8,128)S(1)} %copy-done.57, ...), custom_call_target="tpu_custom_call" | custom-call | flops 1 | bytes 1 | tf_op jit(solution)/shard_map/attend_back/pallas_call | solution.py:64
  224.9 2.3 expand_gradients.3.refs_0_.refs_2_.refs_1_
  232.3 4.3 all-to-all-start.2
  241.2 3.3 projection_gradients.1
  246.3 9.4 %collective-permute-done.19.refs_1_ = bf16[1024,1024]{1,0:T(8,128)(2,1)} collective-permute-done((bf16[1024,1024]{1,0:T(8,128)(2,1)}, bf16[1024,1024]{1,0:T(8,128)(2,1)}, u32[]{:S(2)}, u32[]{:S(2)}) %collective-permute-start.19) | collective-permute-done | bytes 2097184 | tf_op jit(solution)/shard_map/ppermute | solution.py:34
  255.7 2.8 add_parts.7
  262.8 4.0 sum_split.4
  266.8 2.5 collective-permute-start.26
  270.9 12.3 %collective-permute-done.22.refs_1_ = bf16[272,384]{1,0:T(8,128)(2,1)S(1)} collective-permute-done((bf16[272,384]{1,0:T(8,128)(2,1)}, bf16[272,384]{1,0:T(8,128)(2,1)S(1)}, u32[]{:S(2)}, u32[]{:S(2)}) %collective-permute-start.22) | collective-permute-done | bytes 208928 | tf_op jit(solution)/shard_map/ppermute | solution.py:34
  284.2 2.6 sum_split.5
  286.9 9.3 %collective-permute-done.26.refs_2_ = bf16[640,1024]{1,0:T(8,128)(2,1)} collective-permute-done((bf16[640,1024]{1,0:T(8,128)(2,1)}, bf16[640,1024]{1,0:T(8,128)(2,1)}, u32[]{:S(2)}, u32[]{:S(2)}) %collective-permute-start.26) | collective-permute-done | bytes 1310752 | tf_op jit(solution)/shard_map/ppermute | solution.py:34
  296.2 3.1 sum_split.6
  300.3 2.7 collective-permute-start.36
  307.3 2.8 copy-done.7
  310.1 4.2 input_gradient.1.refs_6_
  314.3 17.3 %collective-permute-done.36.refs_4_ = bf16[160,1024]{1,0:T(8,128)(2,1)S(1)} collective-permute-done((bf16[160,1024]{1,0:T(8,128)(2,1)}, bf16[160,1024]{1,0:T(8,128)(2,1)S(1)}, u32[]{:S(2)}, u32[]{:S(2)}) %collective-permute-start.36) | collective-permute-done | bytes 327712 | tf_op jit(solution)/shard_map/ppermute | solution.py:34
  331.7 11.2 %collective-permute-done.34.refs_1_ = bf16[128,1024]{1,0:T(8,128)(2,1)S(1)} collective-permute-done((bf16[128,1024]{1,0:T(8,128)(2,1)S(1)}, bf16[128,1024]{1,0:T(8,128)(2,1)S(1)}, u32[]{:S(2)}, u32[]{:S(2)}) %collective-permute-start.34) | collective-permute-done | bytes 262176 | tf_op jit(solution)/shard_map/ppermute | solution.py:34
  345.2 2.9 collective-permute-start.30
  349.6 2.5 collective-permute-start.27
  354.3 2.6 collective-permute-start.29
  356.9 13.3 %collective-permute-done.30.refs_5_ = bf16[272,384]{1,0:T(8,128)(2,1)S(1)} collective-permute-done((bf16[272,384]{1,0:T(8,128)(2,1)S(1)}, bf16[272,384]{1,0:T(8,128)(2,1)S(1)}, u32[]{:S(2)}, u32[]{:S(2)}) %collective-permute-start.30) | collective-permute-done | bytes 208928 | tf_op jit(solution)/shard_map/ppermute | solution.py:34
  370.2 2.6 collective-permute-start.31
  375.9 3.2 collective-permute-done.38.refs_1_
  379.1 10.1 %collective-permute-start.39 = (bf16[16,1024]{1,0:T(8,128)(2,1)S(1)}, bf16[16,1024]{1,0:T(8,128)(2,1)S(1)}, u32[]{:S(2)}, u32[]{:S(2)}) collective-permute-start(bf16[16,1024]{1,0:T(8,128)(2,1)S(1)} %sum_all.5.refs_0_.refs_2_), channel_id=1, source_target_pairs={{0,8},{4,12},{8,0},{12,4},{16,24},{20,28},{24,16},{28,20},{1,9},{5... | collective-permute-start | bytes 98312 | tf_op jit(solution)/shard_map/ppermute | solution.py:34
  391.3 3.4 collective-permute-start.40
  394.7 2.6 collective-permute-done.40.refs_1_
  397.4 2.3 place_projections.1
  399.7 34.7 %all-gather.8.cloned.1.call-done = bf16[2304,1024]{1,0:T(8,128)(2,1)} async-done(((bf16[288,1024]{1,0:T(8,128)(2,1)}), bf16[2304,1024]{1,0:T(8,128)(2,1)}) %all-gather.8.cloned.1.call-update) | async-done | bytes 4718608 | tf_op jit(solution)/shard_map/all_gather | solution.py:1210
  434.4 8.9 %place_gradients.1 = (f32[1024,1024]{1,0:T(8,128)}, f32[256,4096]{1,0:T(8,128)}, f32[256,1024]{1,0:T(8,128)}, f32[1,256]{1,0:T(1,128)}, f32[1,256]{1,0:T(1,128)}...) custom-call(s32[1]{0:T(128)} %bitcast.refs_0_, ...), custom_call_target="tpu_custom_call" | custom-call | flops 1 | bytes 1 | tf_op jit(solution)/shard_map/place_gradients/pallas_call | solution.py:64
  (273 shorter events, 98.2 us)
Async XLA Ops:
  7.2 129.3 %all-gather.4.cloned.1.call-start = ((), (), s32[]{:S(2)}) async-start(), calls=%async_computation.3 | async-start | bytes 20971520 | tf_op jit(solution)/shard_map/all_gather | solution.py:1059
  14.6 292.7 %all-gather.6.cloned.1.call-start = ((), (), s32[]{:S(2)}) async-start(), calls=%async_computation.4 | async-start | bytes 7864320 | tf_op jit(solution)/shard_map/all_gather | solution.py:1078
  18.0 27.4 %collective-permute-start.3 = (bf16[256,1024]{1,0:T(8,128)(2,1)S(1)}, bf16[256,1024]{1,0:T(8,128)(2,1)S(1)}, u32[]{:S(2)}, u32[]{:S(2)}) collective-permute-start(bf16[256,1024]{1,0:T(8,128)(2,1)S(1)} %cast_all.2.refs_1_), channel_id=1, source_target_pairs={{0,16},{4,20},{8,24},{12,28},{16,0},{20,4},{24,8},{28,12},{1,17},{... | collective-permute-start | bytes 1572872 | tf_op jit(solution)/shard_map/ppermute | solution.py:34
  22.1 23.3 %collective-permute-start = (bf16[256,1024]{1,0:T(8,128)(2,1)S(1)}, bf16[256,1024]{1,0:T(8,128)(2,1)}, u32[]{:S(2)}, u32[]{:S(2)}) collective-permute-start(bf16[256,1024]{1,0:T(8,128)(2,1)S(1)} %cast_all.2.refs_1_), channel_id=1, source_target_pairs={{0,4},{4,0},{8,12},{12,8},{16,20},{20,16},{24,28},{28,24},{1,5},{5... | collective-permute-start | bytes 1572872 | tf_op jit(solution)/shard_map/ppermute | solution.py:34
  23.6 23.2 %collective-permute-start.1 = (bf16[256,1024]{1,0:T(8,128)(2,1)S(1)}, bf16[256,1024]{1,0:T(8,128)(2,1)S(1)}, u32[]{:S(2)}, u32[]{:S(2)}) collective-permute-start(bf16[256,1024]{1,0:T(8,128)(2,1)S(1)} %cast_all.2.refs_1_), channel_id=1, source_target_pairs={{0,8},{4,12},{8,0},{12,4},{16,24},{20,28},{24,16},{28,20},{1,9},{5... | collective-permute-start | bytes 1572872 | tf_op jit(solution)/shard_map/ppermute | solution.py:34
  27.4 23.5 %collective-permute-start.8 = (bf16[256,384]{1,0:T(8,128)(2,1)S(1)}, bf16[256,384]{1,0:T(8,128)(2,1)S(1)}, u32[]{:S(2)}, u32[]{:S(2)}) collective-permute-start(bf16[256,384]{1,0:T(8,128)(2,1)S(1)} %pad_maximum_fusion.refs_9_), channel_id=1, source_target_pairs={{0,2},{1,3},{2,0},{3,1},{4,6},{5,7},{6,4},{7,5},{8,10},{9,11},{10,... | collective-permute-start | bytes 589832 | tf_op jit(solution)/shard_map/ppermute | solution.py:34
  28.9 23.9 %collective-permute-start.7 = (bf16[256,384]{1,0:T(8,128)(2,1)S(1)}, bf16[256,384]{1,0:T(8,128)(2,1)}, u32[]{:S(2)}, u32[]{:S(2)}) collective-permute-start(bf16[256,384]{1,0:T(8,128)(2,1)S(1)} %pad_maximum_fusion.refs_9_), channel_id=1, source_target_pairs={{0,1},{1,0},{2,3},{3,2},{4,5},{5,4},{6,7},{7,6},{8,9},{9,8},{10,11... | collective-permute-start | bytes 589832 | tf_op jit(solution)/shard_map/ppermute | solution.py:34
  48.1 25.0 %collective-permute-start.11 = (bf16[256,1024]{1,0:T(8,128)(2,1)S(1)}, bf16[256,1024]{1,0:T(8,128)(2,1)S(1)}, u32[]{:S(2)}, u32[]{:S(2)}) collective-permute-start(bf16[256,1024]{1,0:T(8,128)(2,1)S(1)} %cast_all.3.refs_3_.refs_2_.refs_7_), channel_id=1, source_target_pairs={{0,2},{1,3},{2,0},{3,1},{4,6},{5,7},{6,4},{7,5},{8,10},{9,11},{10,... | collective-permute-start | bytes 1572872 | tf_op jit(solution)/shard_map/ppermute | solution.py:34
  49.7 14.2 %collective-permute-start.5 = (bf16[256,1024]{1,0:T(8,128)(2,1)S(1)}, bf16[256,1024]{1,0:T(8,128)(2,1)}, u32[]{:S(2)}, u32[]{:S(2)}) collective-permute-start(bf16[256,1024]{1,0:T(8,128)(2,1)S(1)} %collective-permute-done.3.refs_4_.refs_5_), channel_id=1, source_target_pairs={{0,8},{4,12},{8,0},{12,4},{16,24},{20,28},{24,16},{28,20},{1,9},{5... | collective-permute-start | bytes 1572872 | tf_op jit(solution)/shard_map/ppermute | solution.py:34
  50.9 3.5 collective-permute-start.9
  52.3 36.0 %collective-permute-start.10 = (bf16[256,1024]{1,0:T(8,128)(2,1)S(1)}, bf16[256,1024]{1,0:T(8,128)(2,1)S(1)}, u32[]{:S(2)}, u32[]{:S(2)}) collective-permute-start(bf16[256,1024]{1,0:T(8,128)(2,1)S(1)} %cast_all.3.refs_3_.refs_2_.refs_7_), channel_id=1, source_target_pairs={{0,1},{1,0},{2,3},{3,2},{4,5},{5,4},{6,7},{7,6},{8,9},{9,8},{10,11... | collective-permute-start | bytes 1572872 | tf_op jit(solution)/shard_map/ppermute | solution.py:34
  52.8 22.0 %collective-permute-start.4 = (bf16[256,1024]{1,0:T(8,128)(2,1)S(1)}, bf16[256,1024]{1,0:T(8,128)(2,1)}, u32[]{:S(2)}, u32[]{:S(2)}) collective-permute-start(bf16[256,1024]{1,0:T(8,128)(2,1)S(1)} %collective-permute-done.3.refs_4_.refs_5_), channel_id=1, source_target_pairs={{0,4},{4,0},{8,12},{12,8},{16,20},{20,16},{24,28},{28,24},{1,5},{5... | collective-permute-start | bytes 1572872 | tf_op jit(solution)/shard_map/ppermute | solution.py:34
  55.1 19.7 %collective-permute-start.2 = (bf16[256,1024]{1,0:T(8,128)(2,1)}, bf16[256,1024]{1,0:T(8,128)(2,1)}, u32[]{:S(2)}, u32[]{:S(2)}) collective-permute-start(bf16[256,1024]{1,0:T(8,128)(2,1)} %collective-permute-done.refs_2_), channel_id=1, source_target_pairs={{0,8},{4,12},{8,0},{12,4},{16,24},{20,28},{24,16},{28,20},{1,9},{5... | collective-permute-start | bytes 1572872 | tf_op jit(solution)/shard_map/ppermute | solution.py:34
  63.9 14.1 %collective-permute-start.6 = (bf16[256,1024]{1,0:T(8,128)(2,1)}, bf16[256,1024]{1,0:T(8,128)(2,1)}, u32[]{:S(2)}, u32[]{:S(2)}) collective-permute-start(bf16[256,1024]{1,0:T(8,128)(2,1)} %collective-permute-done.5.refs_7_), channel_id=1, source_target_pairs={{0,4},{4,0},{8,12},{12,8},{16,20},{20,16},{24,28},{28,24},{1,5},{5... | collective-permute-start | bytes 1572872 | tf_op jit(solution)/shard_map/ppermute | solution.py:34
  73.1 15.2 %collective-permute-start.12 = (bf16[256,1024]{1,0:T(8,128)(2,1)S(1)}, bf16[256,1024]{1,0:T(8,128)(2,1)S(1)}, u32[]{:S(2)}, u32[]{:S(2)}) collective-permute-start(bf16[256,1024]{1,0:T(8,128)(2,1)S(1)} %collective-permute-done.11.refs_6_.refs_4_.refs_9_), channel_id=1, source_target_pairs={{0,1},{1,0},{2,3},{3,2},{4,5},{5,4},{6,7},{7,6},{8,9},{9,8},{10,11... | collective-permute-start | bytes 1572872 | tf_op jit(solution)/shard_map/ppermute | solution.py:34
  103.1 18.4 %all-to-all-start = ((bf16[8,256,128]{2,1,0:T(8,128)(2,1)}), bf16[8,256,128]{2,1,0:T(8,128)(2,1)S(1)}, u32[]{:S(2)}, u32[]{:S(2)}) async-start(bf16[8,256,128]{2,1,0:T(8,128)(2,1)} %bitcast.4), calls=%async_computation | async-start | bytes 1048576 | tf_op jit(solution)/shard_map/all_to_all | solution.py:109
  126.7 1.9 collective-permute-start.13
  145.8 3.8 collective-permute-start.14
  153.7 1.9 collective-permute-start.15
  164.3 6.9 %collective-permute-start.16 = (f32[256,1024]{1,0:T(8,128)S(1)}, f32[256,1024]{1,0:T(8,128)S(1)}, u32[]{:S(2)}, u32[]{:S(2)}) collective-permute-start(f32[256,1024]{1,0:T(8,128)S(1)} %get-tuple-element.100), channel_id=1, source_target_pairs={{0,1},{1,0},{2,3},{3,2},{4,5},{5,4},{6,7},{7,6},{8,9},{9,8},{10,11... | collective-permute-start | bytes 3145736 | tf_op jit(solution)/shard_map/ppermute | solution.py:34
  169.4 57.8 %collective-permute-start.18 = (bf16[1024,1024]{1,0:T(8,128)(2,1)}, bf16[1024,1024]{1,0:T(8,128)(2,1)}, u32[]{:S(2)}, u32[]{:S(2)}) collective-permute-start(bf16[1024,1024]{1,0:T(8,128)(2,1)} %expand_gradients.2.refs_11_), channel_id=1, source_target_pairs={{0,2},{1,3},{2,0},{3,1},{4,6},{5,7},{6,4},{7,5},{8,10},{9,11},{10,... | collective-permute-start | bytes 6291464 | tf_op jit(solution)/shard_map/ppermute | solution.py:34
  175.2 19.1 %all-to-all-start.1 = ((bf16[8,256,128]{2,1,0:T(8,128)(2,1)}), bf16[8,256,128]{2,1,0:T(8,128)(2,1)}, u32[]{:S(2)}, u32[]{:S(2)}) async-start(bf16[8,256,128]{2,1,0:T(8,128)(2,1)} %bitcast.45), calls=%async_computation.1 | async-start | bytes 1048576 | tf_op jit(solution)/shard_map/all_to_all | solution.py:109
  186.5 36.3 %collective-permute-start.17 = (bf16[528,1024]{1,0:T(8,128)(2,1)}, bf16[528,1024]{1,0:T(8,128)(2,1)}, u32[]{:S(2)}, u32[]{:S(2)}) collective-permute-start(bf16[528,1024]{1,0:T(8,128)(2,1)} %get-tuple-element.118), channel_id=1, source_target_pairs={{0,1},{1,0},{2,3},{3,2},{4,5},{5,4},{6,7},{7,6},{8,9},{9,8},{10,11... | collective-permute-start | bytes 3244040 | tf_op jit(solution)/shard_map/ppermute | solution.py:34
  198.2 57.5 %collective-permute-start.19 = (bf16[1024,1024]{1,0:T(8,128)(2,1)}, bf16[1024,1024]{1,0:T(8,128)(2,1)}, u32[]{:S(2)}, u32[]{:S(2)}) collective-permute-start(bf16[1024,1024]{1,0:T(8,128)(2,1)} %reduce_gradient.2.refs_7_), channel_id=1, source_target_pairs={{0,4},{4,0},{8,12},{12,8},{16,20},{20,16},{24,28},{28,24},{1,5},{5... | collective-permute-start | bytes 6291464 | tf_op jit(solution)/shard_map/ppermute | solution.py:34
  232.3 51.9 %all-to-all-start.2 = ((bf16[8,256,384]{2,1,0:T(8,128)(2,1)}), bf16[8,256,384]{2,1,0:T(8,128)(2,1)}, u32[]{:S(2)}, u32[]{:S(2)}) async-start(bf16[8,256,384]{2,1,0:T(8,128)(2,1)} %bitcast.43), calls=%async_computation.2 | async-start | bytes 3145728 | tf_op jit(solution)/shard_map/all_to_all | solution.py:109
  236.6 197.7 %all-gather.8.cloned.1.call-start = ((), (), s32[]{:S(2)}) async-start(), calls=%async_computation.5 | async-start | bytes 5308416 | tf_op jit(solution)/shard_map/all_gather | solution.py:1210
  237.0 24.7 %collective-permute-start.23 = (bf16[512,1024]{1,0:T(8,128)(2,1)}, bf16[512,1024]{1,0:T(8,128)(2,1)}, u32[]{:S(2)}, u32[]{:S(2)}) collective-permute-start(bf16[512,1024]{1,0:T(8,128)(2,1)} %copy-done.38), channel_id=1, source_target_pairs={{0,1},{1,0},{2,3},{3,2},{4,5},{5,4},{6,7},{7,6},{8,9},{9,8},{10,11... | collective-permute-start | bytes 3145736 | tf_op jit(solution)/shard_map/ppermute | solution.py:34
  237.0 24.6 %collective-permute-start.24 = (bf16[272,1024]{1,0:T(8,128)(2,1)}, bf16[272,1024]{1,0:T(8,128)(2,1)}, u32[]{:S(2)}, u32[]{:S(2)}) collective-permute-start(bf16[272,1024]{1,0:T(8,128)(2,1)} %copy-done.75), channel_id=1, source_target_pairs={{0,2},{1,3},{2,0},{3,1},{4,6},{5,7},{6,4},{7,5},{8,10},{9,11},{10,... | collective-permute-start | bytes 1671176 | tf_op jit(solution)/shard_map/ppermute | solution.py:34
  244.5 14.4 %collective-permute-start.21 = (bf16[528,384]{1,0:T(8,128)(2,1)S(1)}, bf16[528,384]{1,0:T(8,128)(2,1)}, u32[]{:S(2)}, u32[]{:S(2)}) collective-permute-start(bf16[528,384]{1,0:T(8,128)(2,1)S(1)} %get-tuple-element.123.refs_4_), channel_id=1, source_target_pairs={{0,1},{1,0},{2,3},{3,2},{4,5},{5,4},{6,7},{7,6},{8,9},{9,8},{10,11... | collective-permute-start | bytes 1216520 | tf_op jit(solution)/shard_map/ppermute | solution.py:34
  258.5 25.7 %collective-permute-start.20 = (bf16[512,1024]{1,0:T(8,128)(2,1)}, bf16[512,1024]{1,0:T(8,128)(2,1)}, u32[]{:S(2)}, u32[]{:S(2)}) collective-permute-start(bf16[512,1024]{1,0:T(8,128)(2,1)} %get-tuple-element.125), channel_id=1, source_target_pairs={{0,2},{1,3},{2,0},{3,1},{4,6},{5,7},{6,4},{7,5},{8,10},{9,11},{10,... | collective-permute-start | bytes 3145736 | tf_op jit(solution)/shard_map/ppermute | solution.py:34
  266.8 29.4 %collective-permute-start.26 = (bf16[640,1024]{1,0:T(8,128)(2,1)}, bf16[640,1024]{1,0:T(8,128)(2,1)}, u32[]{:S(2)}, u32[]{:S(2)}) collective-permute-start(bf16[640,1024]{1,0:T(8,128)(2,1)} %get-tuple-element.133), channel_id=1, source_target_pairs={{0,4},{4,0},{8,12},{12,8},{16,20},{20,16},{24,28},{28,24},{1,5},{5... | collective-permute-start | bytes 3932168 | tf_op jit(solution)/shard_map/ppermute | solution.py:34
  269.3 13.9 %collective-permute-start.22 = (bf16[272,384]{1,0:T(8,128)(2,1)}, bf16[272,384]{1,0:T(8,128)(2,1)S(1)}, u32[]{:S(2)}, u32[]{:S(2)}) collective-permute-start(bf16[272,384]{1,0:T(8,128)(2,1)} %get-tuple-element.128.refs_6_), channel_id=1, source_target_pairs={{0,2},{1,3},{2,0},{3,1},{4,6},{5,7},{6,4},{7,5},{8,10},{9,11},{10,... | collective-permute-start | bytes 626696 | tf_op jit(solution)/shard_map/ppermute | solution.py:34
  286.9 17.5 %collective-permute-start.25 = (bf16[256,1024]{1,0:T(8,128)(2,1)}, bf16[256,1024]{1,0:T(8,128)(2,1)}, u32[]{:S(2)}, u32[]{:S(2)}) collective-permute-start(bf16[256,1024]{1,0:T(8,128)(2,1)} %get-tuple-element.132), channel_id=1, source_target_pairs={{0,8},{4,12},{8,0},{12,4},{16,24},{20,28},{24,16},{28,20},{1,9},{5... | collective-permute-start | bytes 1572872 | tf_op jit(solution)/shard_map/ppermute | solution.py:34
  300.0 14.3 %collective-permute-start.35 = (bf16[160,1024]{1,0:T(8,128)(2,1)}, bf16[160,1024]{1,0:T(8,128)(2,1)S(1)}, u32[]{:S(2)}, u32[]{:S(2)}) collective-permute-start(bf16[160,1024]{1,0:T(8,128)(2,1)} %get-tuple-element.137), channel_id=1, source_target_pairs={{0,8},{4,12},{8,0},{12,4},{16,24},{20,28},{24,16},{28,20},{1,9},{5... | collective-permute-start | bytes 983048 | tf_op jit(solution)/shard_map/ppermute | solution.py:34
  300.3 31.4 %collective-permute-start.36 = (bf16[160,1024]{1,0:T(8,128)(2,1)}, bf16[160,1024]{1,0:T(8,128)(2,1)S(1)}, u32[]{:S(2)}, u32[]{:S(2)}) collective-permute-start(bf16[160,1024]{1,0:T(8,128)(2,1)} %get-tuple-element.138), channel_id=1, source_target_pairs={{0,16},{4,20},{8,24},{12,28},{16,0},{20,4},{24,8},{28,12},{1,17},{... | collective-permute-start | bytes 983048 | tf_op jit(solution)/shard_map/ppermute | solution.py:34
  303.0 28.7 %collective-permute-start.37 = (bf16[160,1024]{1,0:T(8,128)(2,1)}, bf16[160,1024]{1,0:T(8,128)(2,1)S(1)}, u32[]{:S(2)}, u32[]{:S(2)}) collective-permute-start(bf16[160,1024]{1,0:T(8,128)(2,1)} %get-tuple-element.139), channel_id=1, source_target_pairs={{0,24},{4,28},{8,16},{12,20},{16,8},{20,12},{24,0},{28,4},{1,25},{... | collective-permute-start | bytes 983048 | tf_op jit(solution)/shard_map/ppermute | solution.py:34
  306.7 36.2 %collective-permute-start.34 = (bf16[128,1024]{1,0:T(8,128)(2,1)S(1)}, bf16[128,1024]{1,0:T(8,128)(2,1)S(1)}, u32[]{:S(2)}, u32[]{:S(2)}) collective-permute-start(bf16[128,1024]{1,0:T(8,128)(2,1)S(1)} %get-tuple-element.136), channel_id=1, source_target_pairs={{0,16},{4,20},{8,24},{12,28},{16,0},{20,4},{24,8},{28,12},{1,17},{... | collective-permute-start | bytes 786440 | tf_op jit(solution)/shard_map/ppermute | solution.py:34
  314.3 58.5 %copy-start.12 = (bf16[272,1024]{1,0:T(8,128)(2,1)S(1)}, bf16[272,1024]{1,0:T(8,128)(2,1)}, u32[]{:S(2)}) copy-start(bf16[272,1024]{1,0:T(8,128)(2,1)} %copy-done.10) | copy-start | bytes 1671172
  345.1 9.2 %collective-permute-start.28 = (bf16[272,384]{1,0:T(8,128)(2,1)S(1)}, bf16[272,384]{1,0:T(8,128)(2,1)S(1)}, u32[]{:S(2)}, u32[]{:S(2)}) collective-permute-start(bf16[272,384]{1,0:T(8,128)(2,1)S(1)} %sum_all.4.refs_3_.refs_1_), channel_id=1, source_target_pairs={{0,8},{4,12},{8,0},{12,4},{16,24},{20,28},{24,16},{28,20},{1,9},{5... | collective-permute-start | bytes 626696 | tf_op jit(solution)/shard_map/ppermute | solution.py:34
  345.2 25.0 %collective-permute-start.30 = (bf16[272,384]{1,0:T(8,128)(2,1)S(1)}, bf16[272,384]{1,0:T(8,128)(2,1)S(1)}, u32[]{:S(2)}, u32[]{:S(2)}) collective-permute-start(bf16[272,384]{1,0:T(8,128)(2,1)S(1)} %sum_all.4.refs_3_.refs_1_), channel_id=1, source_target_pairs={{0,16},{4,20},{8,24},{12,28},{16,0},{20,4},{24,8},{28,12},{1,17},{... | collective-permute-start | bytes 626696 | tf_op jit(solution)/shard_map/ppermute | solution.py:34
  348.1 24.6 %collective-permute-start.32 = (bf16[272,384]{1,0:T(8,128)(2,1)S(1)}, bf16[272,384]{1,0:T(8,128)(2,1)S(1)}, u32[]{:S(2)}, u32[]{:S(2)}) collective-permute-start(bf16[272,384]{1,0:T(8,128)(2,1)S(1)} %sum_all.4.refs_3_.refs_1_), channel_id=1, source_target_pairs={{0,24},{4,28},{8,16},{12,20},{16,8},{20,12},{24,0},{28,4},{1,25},{... | collective-permute-start | bytes 626696 | tf_op jit(solution)/shard_map/ppermute | solution.py:34
  349.6 47.8 %collective-permute-start.27 = (bf16[272,384]{1,0:T(8,128)(2,1)S(1)}, bf16[272,384]{1,0:T(8,128)(2,1)S(1)}, u32[]{:S(2)}, u32[]{:S(2)}) collective-permute-start(bf16[272,384]{1,0:T(8,128)(2,1)S(1)} %sum_all.4.refs_3_.refs_1_), channel_id=1, source_target_pairs={{0,4},{4,0},{8,12},{12,8},{16,20},{20,16},{24,28},{28,24},{1,5},{5... | collective-permute-start | bytes 626696 | tf_op jit(solution)/shard_map/ppermute | solution.py:34
  354.3 43.0 %collective-permute-start.29 = (bf16[272,384]{1,0:T(8,128)(2,1)S(1)}, bf16[272,384]{1,0:T(8,128)(2,1)S(1)}, u32[]{:S(2)}, u32[]{:S(2)}) collective-permute-start(bf16[272,384]{1,0:T(8,128)(2,1)S(1)} %collective-permute-done.28.refs_3_), channel_id=1, source_target_pairs={{0,4},{4,0},{8,12},{12,8},{16,20},{20,16},{24,28},{28,24},{1,5},{5... | collective-permute-start | bytes 626696 | tf_op jit(solution)/shard_map/ppermute | solution.py:34
  370.2 27.2 %collective-permute-start.31 = (bf16[272,384]{1,0:T(8,128)(2,1)S(1)}, bf16[272,384]{1,0:T(8,128)(2,1)S(1)}, u32[]{:S(2)}, u32[]{:S(2)}) collective-permute-start(bf16[272,384]{1,0:T(8,128)(2,1)S(1)} %collective-permute-done.30.refs_5_), channel_id=1, source_target_pairs={{0,4},{4,0},{8,12},{12,8},{16,20},{20,16},{24,28},{28,24},{1,5},{5... | collective-permute-start | bytes 626696 | tf_op jit(solution)/shard_map/ppermute | solution.py:34
  372.8 24.6 %collective-permute-start.33 = (bf16[272,384]{1,0:T(8,128)(2,1)S(1)}, bf16[272,384]{1,0:T(8,128)(2,1)S(1)}, u32[]{:S(2)}, u32[]{:S(2)}) collective-permute-start(bf16[272,384]{1,0:T(8,128)(2,1)S(1)} %collective-permute-done.32.refs_7_), channel_id=1, source_target_pairs={{0,4},{4,0},{8,12},{12,8},{16,20},{20,16},{24,28},{28,24},{1,5},{5... | collective-permute-start | bytes 626696 | tf_op jit(solution)/shard_map/ppermute | solution.py:34
  373.9 5.3 %collective-permute-start.38 = (bf16[16,1024]{1,0:T(8,128)(2,1)S(1)}, bf16[16,1024]{1,0:T(8,128)(2,1)S(1)}, u32[]{:S(2)}, u32[]{:S(2)}) collective-permute-start(bf16[16,1024]{1,0:T(8,128)(2,1)S(1)} %add_parts.9.refs_0_.refs_2_), channel_id=1, source_target_pairs={{0,4},{4,0},{8,12},{12,8},{16,20},{20,16},{24,28},{28,24},{1,5},{5... | collective-permute-start | bytes 98312 | tf_op jit(solution)/shard_map/ppermute | solution.py:34
  379.1 12.1 %collective-permute-start.39 = (bf16[16,1024]{1,0:T(8,128)(2,1)S(1)}, bf16[16,1024]{1,0:T(8,128)(2,1)S(1)}, u32[]{:S(2)}, u32[]{:S(2)}) collective-permute-start(bf16[16,1024]{1,0:T(8,128)(2,1)S(1)} %sum_all.5.refs_0_.refs_2_), channel_id=1, source_target_pairs={{0,8},{4,12},{8,0},{12,4},{16,24},{20,28},{24,16},{28,20},{1,9},{5... | collective-permute-start | bytes 98312 | tf_op jit(solution)/shard_map/ppermute | solution.py:34
  391.3 6.0 %collective-permute-start.40 = (bf16[16,1024]{1,0:T(8,128)(2,1)S(1)}, bf16[16,1024]{1,0:T(8,128)(2,1)S(1)}, u32[]{:S(2)}, u32[]{:S(2)}) collective-permute-start(bf16[16,1024]{1,0:T(8,128)(2,1)S(1)} %sum_all.6.refs_0_.refs_2_), channel_id=1, source_target_pairs={{0,16},{4,20},{8,24},{12,28},{16,0},{20,4},{24,8},{28,12},{1,17},{... | collective-permute-start | bytes 98312 | tf_op jit(solution)/shard_map/ppermute | solution.py:34
  (83 other events, 725.9 us)
Sparse Core Ops, SparseCore 0:
  14.7 121.7 all-gather.3
  138.0 52.8 all-gather.5
  345.3 89.0 all-gather.7

commit v5 on v4

--- a/solution.py
+++ b/solution.py
@@ -1159,15 +1159,6 @@
     d_query, d_key, d_value = attend_back(
         back, douts, wide, keys, values, keys_t, head_size, tokens, group
     )
-    output_keep, output_send = add_parts(
-        output_keep, output_received, [[(0, shard), rest], [(shard, 2 * shard), rest]]
-    )
-    output_received = swap(output_send, "fsdp", 2)
-    expand_keep = expand_gradients(
-        normed_r, sibling_normed, d_expanded_r, f, (0, 1), 0, shard
-    )
-    (expand_send,) = add_parts(expand_keep, expand_received, [[(2 * shard, 4 * shard)]])
-    expand_other = swap(expand_send, "fsdp", 1)
     count = ctx_size
     while count > near:
         count //= 2
@@ -1178,6 +1169,15 @@
         d_value = d_value[: count * tokens] + received[1]
     d_all, d_send = head_grads([d_query], d_key, d_value, tokens, near, group)
     d_mine = exchange(d_send, near)
+    output_keep, output_send = add_parts(
+        output_keep, output_received, [[(0, shard), rest], [(shard, 2 * shard), rest]]
+    )
+    output_received = swap(output_send, "fsdp", 2)
+    expand_keep = expand_gradients(
+        normed_r, sibling_normed, d_expanded_r, f, (0, 1), 0, shard
+    )
+    (expand_send,) = add_parts(expand_keep, expand_received, [[(2 * shard, 4 * shard)]])
+    expand_other = swap(expand_send, "fsdp", 1)
 
     send, keep = projection_gradients(stream, d_all, f, shard)
     received = swap(send, "fsdp", 1)

time: 452 us -> 450 us (level)
  waiting for transfers between devices: 191 us -> 201 us
  starting transfers between devices: 70.1 us -> 63 us
    ppermute x41, waiting for transfers between devices: 127 us -> 139 us  [swap(): return lax.ppermute(array, axis, [(i, i ^ mask) for i in range(size)])]
    ppermute x41, starting transfers between devices: 56.5 us -> 49.1 us  [swap(): return lax.ppermute(array, axis, [(i, i ^ mask) for i in range(size)])]
    unnamed x169 -> x161, local copies, waits for them, and re-layouts: 47.4 us -> 42.9 us
  transfers between devices with their start and end apart: 47 -> 47, of which waited for: 22 -> 23; matrix products, arithmetic and copies ran while one was open for 1% -> 1% of each run, Pallas kernels for 25% -> 25%
where the time goes in v5:
time: 450 us; the launch traced here: 448 us
  waiting for transfers between devices  201 us (45%)
  Pallas kernels  122 us (27%)
  starting transfers between devices  63 us (14%)
  local copies, waits for them, and re-layouts  44.9 us (10%)
  between operations  14.6 us (3%)
    ppermute x41, waiting for transfers between devices, swap(): return lax.ppermute(array, axis, [(i, i ^ mask) for i in range(size)])  139 us
    pallas_call x36, Pallas kernels, call(): pl.pallas_call(ordered, out_shape=out_shape, grid_spec=pltpu.PrefetchScal...  122 us
    ppermute x41, starting transfers between devices, swap(): return lax.ppermute(array, axis, [(i, i ^ mask) for i in range(size)])  49.1 us
    unnamed x161, local copies, waits for them, and re-layouts  42.9 us
    all_gather x1, waiting for transfers between devices, per_device(): lax.all_gather(stack_sums(reduced, expanded), 'ctx', axis=0, tiled=True)  32.2 us
    all_to_all x3, waiting for transfers between devices, exchange(): return lax.all_to_all(array, 'ctx', 0, 0, tiled=True)  20 us
    all_to_all x3, starting transfers between devices, exchange(): return lax.all_to_all(array, 'ctx', 0, 0, tiled=True)  13.5 us
  transfers between devices with their start and end apart: 47, of which 23 were waited for; matrix products, arithmetic and copies ran while one was open for 1% of the time, Pallas kernels for 25%

profile of v5, /device:TPU:0, one launch (start us, length us, event | category | flops | bytes accessed | tf_op | source)
XLA Modules:
  0.0 448.3 jit_solution(17497761846134321891)
XLA Ops:
  7.2 2.2 copy-done.26
  9.4 2.2 copy-done.27
  15.8 2.2 copy-done.1
  18.0 4.1 collective-permute-start.3
  29.0 16.4 %collective-permute-done.3.refs_4_.refs_5_ = bf16[256,1024]{1,0:T(8,128)(2,1)S(1)} collective-permute-done((bf16[256,1024]{1,0:T(8,128)(2,1)S(1)}, bf16[256,1024]{1,0:T(8,128)(2,1)S(1)}, u32[]{:S(2)}, u32[]{:S(2)}) %collective-permute-start.3) | collective-permute-done | bytes 524320 | tf_op jit(solution)/shard_map/ppermute | solution.py:34
  54.0 9.4 %collective-permute-done.5.refs_7_ = bf16[256,1024]{1,0:T(8,128)(2,1)} collective-permute-done((bf16[256,1024]{1,0:T(8,128)(2,1)S(1)}, bf16[256,1024]{1,0:T(8,128)(2,1)}, u32[]{:S(2)}, u32[]{:S(2)}) %collective-permute-start.5) | collective-permute-done | bytes 524320 | tf_op jit(solution)/shard_map/ppermute | solution.py:34
  63.9 7.9 %collective-permute-done.11.refs_6_.refs_4_.refs_9_ = bf16[256,1024]{1,0:T(8,128)(2,1)S(1)} collective-permute-done((bf16[256,1024]{1,0:T(8,128)(2,1)S(1)}, bf16[256,1024]{1,0:T(8,128)(2,1)S(1)}, u32[]{:S(2)}, u32[]{:S(2)}) %collective-permute-start.11) | collective-permute-done | bytes 524320 | tf_op jit(solution)/shard_map/ppermute | solution.py:34
  73.5 3.3 collective-permute-done.6.refs_8_
  76.9 7.4 %project.1 = (bf16[2,2048,128]{2,1,0:T(8,128)(2,1)S(1)}, bf16[2,2048,128]{2,1,0:T(8,128)(2,1)S(1)}, bf16[2,2048,128]{2,1,0:T(8,128)(2,1)S(1)}, bf16[128,2048]{1,0:T(8,128)(2,1)S(1)}, bf16[2048,1024]{1,0:T(8,128)(2,1)S(1)}) custom-call(s32[1]{0:T(128)} %bitcast.refs_0_, bf16[256,1024]{1,0:T(8,128)(2,1)S(1)} %cast_all.2.refs_1_, ...), custom_call_target="tpu_custom_call" | custom-call | flops 1 | bytes 1 | tf_op jit(solution)/shard_map/project/pallas_call | solution.py:64
  87.2 12.8 %attend.1 = (bf16[2048,128]{1,0:T(8,128)(2,1)}, f32[2048,128]{1,0:T(8,128)S(1)}, bf16[2,2048,128]{2,1,0:T(8,128)(2,1)S(1)}) custom-call(s32[1]{0:T(128)} %bitcast.1.refs_0_, bf16[2,2048,128]{2,1,0:T(8,128)(2,1)S(1)} %get-tuple-element.86.refs_1_.refs_4_, bf16[2,2048,128]{2,1,0:T(8,128)(2,1)S(1)} %get-tuple-element.87.refs_2_.refs_4_, ...), custom_call_target="tpu_custom_call" | custom-call | flops 1 | bytes 1 | tf_op jit(solution)/shard_map/attend/pallas_call | solution.py:64
  101.9 4.7 %all-to-all-start = ((bf16[8,256,128]{2,1,0:T(8,128)(2,1)}), bf16[8,256,128]{2,1,0:T(8,128)(2,1)S(1)}, u32[]{:S(2)}, u32[]{:S(2)}) async-start(bf16[8,256,128]{2,1,0:T(8,128)(2,1)} %bitcast.4), calls=%async_computation | async-start | bytes 1048576 | tf_op jit(solution)/shard_map/all_to_all | solution.py:109
  106.8 13.8 %all-to-all-done = bf16[8,256,128]{2,1,0:T(8,128)(2,1)S(1)} async-done(((bf16[8,256,128]{2,1,0:T(8,128)(2,1)}), bf16[8,256,128]{2,1,0:T(8,128)(2,1)S(1)}, u32[]{:S(2)}, u32[]{:S(2)}) %all-to-all-start) | async-done | bytes 524320 | tf_op jit(solution)/shard_map/all_to_all | solution.py:109
  127.6 8.8 %all-gather.4.cloned.1.call-done.refs_3_.refs_4_.refs_5_.refs_6_.refs_7_.refs_8_ = bf16[8192,1024]{1,0:T(8,128)(2,1)} async-done(((bf16[2048,1024]{1,0:T(8,128)(2,1)}), bf16[8192,1024]{1,0:T(8,128)(2,1)}) %all-gather.4.cloned.1.call-update) | async-done | bytes 16777232 | tf_op jit(solution)/shard_map/all_gather | solution.py:1059
  136.5 9.3 %feed_forward.1 = (bf16[512,2048]{1,0:T(8,128)(2,1)}, bf16[512,2048]{1,0:T(8,128)(2,1)}, f32[256,1024]{1,0:T(8,128)S(1)}, f32[256,1024]{1,0:T(8,128)S(1)}) custom-call(s32[1]{0:T(128)} %bitcast.refs_0_, bf16[256,1024]{1,0:T(8,128)(2,1)S(1)} %get-tuple-element.91.refs_1_, bf16[256,1024]{1,0:T(8,128)(2,1)S(1)} %collective-permute-done.13.refs_2_, ...), custom_call_target="tpu_custom_call" | custom-call | flops 1 | bytes 1 | tf_op jit(solution)/shard_map/feed_forward/pallas_call | solution.py:64
  146.1 3.6 collective-permute-done.14.refs_2_
  151.2 2.5 second_norm.1
  155.7 8.8 %feed_back.1 = (bf16[512,2048]{1,0:T(8,128)(2,1)}, f32[1,2048]{1,0:T(1,128)S(1)}, f32[256,1024]{1,0:T(8,128)S(1)}, f32[256,1024]{1,0:T(8,128)S(1)}) custom-call(s32[1]{0:T(128)} %bitcast.refs_0_, bf16[256,1024]{1,0:T(8,128)(2,1)S(1)} %get-tuple-element.97.refs_1_.refs_2_, bf16[256,1024]{1,0:T(8,128)(2,1)S(1)} %collective-permute-done.15.refs_2_.refs_3_, ...), custom_call_target="tpu_custom_call" | custom-call | flops 1 | bytes 1 | tf_op jit(solution)/shard_map/feed_back/pallas_call | solution.py:64
  166.2 2.3 expand_gradients.2.refs_11_
  172.6 4.5 %all-to-all-start.1 = ((bf16[8,256,128]{2,1,0:T(8,128)(2,1)}), bf16[8,256,128]{2,1,0:T(8,128)(2,1)}, u32[]{:S(2)}, u32[]{:S(2)}) async-start(bf16[8,256,128]{2,1,0:T(8,128)(2,1)} %bitcast.45), calls=%async_computation.1 | async-start | bytes 1048576 | tf_op jit(solution)/shard_map/all_to_all | solution.py:109
  182.3 2.5 output_gradient.1
  185.9 6.3 %all-to-all-done.1 = bf16[8,256,128]{2,1,0:T(8,128)(2,1)} async-done(((bf16[8,256,128]{2,1,0:T(8,128)(2,1)}), bf16[8,256,128]{2,1,0:T(8,128)(2,1)}, u32[]{:S(2)}, u32[]{:S(2)}) %all-to-all-start.1) | async-done | bytes 524320 | tf_op jit(solution)/shard_map/all_to_all | solution.py:109
  194.4 2.7 reduce_gradient.2.refs_7_
  198.6 23.0 %attend_back.1 = (bf16[2048,128]{1,0:T(8,128)(2,1)S(1)}, f32[2048,128]{1,0:T(8,128)S(1)}, f32[2048,128]{1,0:T(8,128)S(1)}) custom-call(s32[1]{0:T(128)} %bitcast.1.refs_0_, bf16[2,2048,128]{2,1,0:T(8,128)(2,1)S(1)} %copy-done.58, bf16[2048,128]{1,0:T(8,128)(2,1)} %bitcast.16.refs_5_.refs_2_, f32[2048,128]{1,0:T(8,128)S(1)} %copy-done.56, ...), custom_call_target="tpu_custom_call" | custom-call | flops 1 | bytes 1 | tf_op jit(solution)/shard_map/attend_back/pallas_call | solution.py:64
  223.2 4.3 all-to-all-start.2
  231.4 2.3 expand_gradients.3.refs_0_.refs_2_.refs_1_
  233.8 3.0 add_parts.6.refs_3_
  238.9 3.4 projection_gradients.1
  244.0 14.6 %collective-permute-done.19.refs_1_ = bf16[1024,1024]{1,0:T(8,128)(2,1)} collective-permute-done((bf16[1024,1024]{1,0:T(8,128)(2,1)}, bf16[1024,1024]{1,0:T(8,128)(2,1)}, u32[]{:S(2)}, u32[]{:S(2)}) %collective-permute-start.19) | collective-permute-done | bytes 2097184 | tf_op jit(solution)/shard_map/ppermute | solution.py:34
  258.6 2.8 add_parts.7
  267.6 4.0 sum_split.4
  272.0 16.3 %collective-permute-done.22.refs_1_ = bf16[272,384]{1,0:T(8,128)(2,1)S(1)} collective-permute-done((bf16[272,384]{1,0:T(8,128)(2,1)}, bf16[272,384]{1,0:T(8,128)(2,1)S(1)}, u32[]{:S(2)}, u32[]{:S(2)}) %collective-permute-start.22) | collective-permute-done | bytes 208928 | tf_op jit(solution)/shard_map/ppermute | solution.py:34
  289.3 2.6 sum_split.5
  291.9 6.4 %collective-permute-done.26.refs_2_ = bf16[640,1024]{1,0:T(8,128)(2,1)} collective-permute-done((bf16[640,1024]{1,0:T(8,128)(2,1)}, bf16[640,1024]{1,0:T(8,128)(2,1)}, u32[]{:S(2)}, u32[]{:S(2)}) %collective-permute-start.26) | collective-permute-done | bytes 1310752 | tf_op jit(solution)/shard_map/ppermute | solution.py:34
  298.3 3.1 sum_split.6
  302.1 4.2 collective-permute-start.36
  310.6 2.8 copy-done.8
  313.4 4.3 input_gradient.1.refs_6_
  317.7 17.1 %collective-permute-done.36.refs_4_ = bf16[160,1024]{1,0:T(8,128)(2,1)S(1)} collective-permute-done((bf16[160,1024]{1,0:T(8,128)(2,1)}, bf16[160,1024]{1,0:T(8,128)(2,1)S(1)}, u32[]{:S(2)}, u32[]{:S(2)}) %collective-permute-start.36) | collective-permute-done | bytes 327712 | tf_op jit(solution)/shard_map/ppermute | solution.py:34
  334.8 8.7 %collective-permute-done.34.refs_1_ = bf16[128,1024]{1,0:T(8,128)(2,1)S(1)} collective-permute-done((bf16[128,1024]{1,0:T(8,128)(2,1)S(1)}, bf16[128,1024]{1,0:T(8,128)(2,1)S(1)}, u32[]{:S(2)}, u32[]{:S(2)}) %collective-permute-start.34) | collective-permute-done | bytes 262176 | tf_op jit(solution)/shard_map/ppermute | solution.py:34
  345.9 2.9 collective-permute-start.30
  352.9 16.9 %collective-permute-done.30.refs_5_ = bf16[272,384]{1,0:T(8,128)(2,1)S(1)} collective-permute-done((bf16[272,384]{1,0:T(8,128)(2,1)S(1)}, bf16[272,384]{1,0:T(8,128)(2,1)S(1)}, u32[]{:S(2)}, u32[]{:S(2)}) %collective-permute-start.30) | collective-permute-done | bytes 208928 | tf_op jit(solution)/shard_map/ppermute | solution.py:34
  374.0 4.2 collective-permute-done.38.refs_1_
  378.1 9.0 %collective-permute-start.39 = (bf16[16,1024]{1,0:T(8,128)(2,1)S(1)}, bf16[16,1024]{1,0:T(8,128)(2,1)S(1)}, u32[]{:S(2)}, u32[]{:S(2)}) collective-permute-start(bf16[16,1024]{1,0:T(8,128)(2,1)S(1)} %sum_all.5.refs_0_.refs_2_), channel_id=1, source_target_pairs={{0,8},{4,12},{8,0},{12,4},{16,24},{20,28},{24,16},{28,20},{1,9},{5... | collective-permute-start | bytes 98312 | tf_op jit(solution)/shard_map/ppermute | solution.py:34
  389.1 4.6 %collective-permute-start.40 = (bf16[16,1024]{1,0:T(8,128)(2,1)S(1)}, bf16[16,1024]{1,0:T(8,128)(2,1)S(1)}, u32[]{:S(2)}, u32[]{:S(2)}) collective-permute-start(bf16[16,1024]{1,0:T(8,128)(2,1)S(1)} %sum_all.6.refs_0_.refs_2_), channel_id=1, source_target_pairs={{0,16},{4,20},{8,24},{12,28},{16,0},{20,4},{24,8},{28,12},{1,17},{... | collective-permute-start | bytes 98312 | tf_op jit(solution)/shard_map/ppermute | solution.py:34
  393.7 4.5 collective-permute-done.40.refs_1_
  398.3 2.3 place_projections.1
  400.6 32.2 %all-gather.8.cloned.1.call-done = bf16[2304,1024]{1,0:T(8,128)(2,1)} async-done(((bf16[288,1024]{1,0:T(8,128)(2,1)}), bf16[2304,1024]{1,0:T(8,128)(2,1)}) %all-gather.8.cloned.1.call-update) | async-done | bytes 4718608 | tf_op jit(solution)/shard_map/all_gather | solution.py:1210
  432.8 8.9 %place_gradients.1 = (f32[1024,1024]{1,0:T(8,128)}, f32[256,4096]{1,0:T(8,128)}, f32[256,1024]{1,0:T(8,128)}, f32[1,256]{1,0:T(1,128)}, f32[1,256]{1,0:T(1,128)}...) custom-call(s32[1]{0:T(128)} %bitcast.refs_0_, ...), custom_call_target="tpu_custom_call" | custom-call | flops 1 | bytes 1 | tf_op jit(solution)/shard_map/place_gradients/pallas_call | solution.py:64
  (265 shorter events, 87.8 us)
Async XLA Ops:
  7.2 129.3 %all-gather.4.cloned.1.call-start = ((), (), s32[]{:S(2)}) async-start(), calls=%async_computation.3 | async-start | bytes 20971520 | tf_op jit(solution)/shard_map/all_gather | solution.py:1059
  14.6 296.0 %all-gather.6.cloned.1.call-start = ((), (), s32[]{:S(2)}) async-start(), calls=%async_computation.4 | async-start | bytes 7864320 | tf_op jit(solution)/shard_map/all_gather | solution.py:1078
  18.0 27.4 %collective-permute-start.3 = (bf16[256,1024]{1,0:T(8,128)(2,1)S(1)}, bf16[256,1024]{1,0:T(8,128)(2,1)S(1)}, u32[]{:S(2)}, u32[]{:S(2)}) collective-permute-start(bf16[256,1024]{1,0:T(8,128)(2,1)S(1)} %cast_all.2.refs_1_), channel_id=1, source_target_pairs={{0,16},{4,20},{8,24},{12,28},{16,0},{20,4},{24,8},{28,12},{1,17},{... | collective-permute-start | bytes 1572872 | tf_op jit(solution)/shard_map/ppermute | solution.py:34
  22.1 23.3 %collective-permute-start = (bf16[256,1024]{1,0:T(8,128)(2,1)S(1)}, bf16[256,1024]{1,0:T(8,128)(2,1)}, u32[]{:S(2)}, u32[]{:S(2)}) collective-permute-start(bf16[256,1024]{1,0:T(8,128)(2,1)S(1)} %cast_all.2.refs_1_), channel_id=1, source_target_pairs={{0,4},{4,0},{8,12},{12,8},{16,20},{20,16},{24,28},{28,24},{1,5},{5... | collective-permute-start | bytes 1572872 | tf_op jit(solution)/shard_map/ppermute | solution.py:34
  23.6 23.2 %collective-permute-start.1 = (bf16[256,1024]{1,0:T(8,128)(2,1)S(1)}, bf16[256,1024]{1,0:T(8,128)(2,1)S(1)}, u32[]{:S(2)}, u32[]{:S(2)}) collective-permute-start(bf16[256,1024]{1,0:T(8,128)(2,1)S(1)} %cast_all.2.refs_1_), channel_id=1, source_target_pairs={{0,8},{4,12},{8,0},{12,4},{16,24},{20,28},{24,16},{28,20},{1,9},{5... | collective-permute-start | bytes 1572872 | tf_op jit(solution)/shard_map/ppermute | solution.py:34
  27.3 22.3 %collective-permute-start.8 = (bf16[256,384]{1,0:T(8,128)(2,1)S(1)}, bf16[256,384]{1,0:T(8,128)(2,1)S(1)}, u32[]{:S(2)}, u32[]{:S(2)}) collective-permute-start(bf16[256,384]{1,0:T(8,128)(2,1)S(1)} %pad_maximum_fusion.refs_9_), channel_id=1, source_target_pairs={{0,2},{1,3},{2,0},{3,1},{4,6},{5,7},{6,4},{7,5},{8,10},{9,11},{10,... | collective-permute-start | bytes 589832 | tf_op jit(solution)/shard_map/ppermute | solution.py:34
  28.9 22.7 %collective-permute-start.7 = (bf16[256,384]{1,0:T(8,128)(2,1)S(1)}, bf16[256,384]{1,0:T(8,128)(2,1)}, u32[]{:S(2)}, u32[]{:S(2)}) collective-permute-start(bf16[256,384]{1,0:T(8,128)(2,1)S(1)} %pad_maximum_fusion.refs_9_), channel_id=1, source_target_pairs={{0,1},{1,0},{2,3},{3,2},{4,5},{5,4},{6,7},{7,6},{8,9},{9,8},{10,11... | collective-permute-start | bytes 589832 | tf_op jit(solution)/shard_map/ppermute | solution.py:34
  46.9 25.0 %collective-permute-start.11 = (bf16[256,1024]{1,0:T(8,128)(2,1)S(1)}, bf16[256,1024]{1,0:T(8,128)(2,1)S(1)}, u32[]{:S(2)}, u32[]{:S(2)}) collective-permute-start(bf16[256,1024]{1,0:T(8,128)(2,1)S(1)} %cast_all.3.refs_3_.refs_2_.refs_7_), channel_id=1, source_target_pairs={{0,2},{1,3},{2,0},{3,1},{4,6},{5,7},{6,4},{7,5},{8,10},{9,11},{10,... | collective-permute-start | bytes 1572872 | tf_op jit(solution)/shard_map/ppermute | solution.py:34
  48.5 14.9 %collective-permute-start.5 = (bf16[256,1024]{1,0:T(8,128)(2,1)S(1)}, bf16[256,1024]{1,0:T(8,128)(2,1)}, u32[]{:S(2)}, u32[]{:S(2)}) collective-permute-start(bf16[256,1024]{1,0:T(8,128)(2,1)S(1)} %collective-permute-done.3.refs_4_.refs_5_), channel_id=1, source_target_pairs={{0,8},{4,12},{8,0},{12,4},{16,24},{20,28},{24,16},{28,20},{1,9},{5... | collective-permute-start | bytes 1572872 | tf_op jit(solution)/shard_map/ppermute | solution.py:34
  49.6 3.5 collective-permute-start.9
  51.1 36.0 %collective-permute-start.10 = (bf16[256,1024]{1,0:T(8,128)(2,1)S(1)}, bf16[256,1024]{1,0:T(8,128)(2,1)S(1)}, u32[]{:S(2)}, u32[]{:S(2)}) collective-permute-start(bf16[256,1024]{1,0:T(8,128)(2,1)S(1)} %cast_all.3.refs_3_.refs_2_.refs_7_), channel_id=1, source_target_pairs={{0,1},{1,0},{2,3},{3,2},{4,5},{5,4},{6,7},{7,6},{8,9},{9,8},{10,11... | collective-permute-start | bytes 1572872 | tf_op jit(solution)/shard_map/ppermute | solution.py:34
  51.6 21.9 %collective-permute-start.4 = (bf16[256,1024]{1,0:T(8,128)(2,1)S(1)}, bf16[256,1024]{1,0:T(8,128)(2,1)}, u32[]{:S(2)}, u32[]{:S(2)}) collective-permute-start(bf16[256,1024]{1,0:T(8,128)(2,1)S(1)} %collective-permute-done.3.refs_4_.refs_5_), channel_id=1, source_target_pairs={{0,4},{4,0},{8,12},{12,8},{16,20},{20,16},{24,28},{28,24},{1,5},{5... | collective-permute-start | bytes 1572872 | tf_op jit(solution)/shard_map/ppermute | solution.py:34
  53.2 20.3 %collective-permute-start.2 = (bf16[256,1024]{1,0:T(8,128)(2,1)}, bf16[256,1024]{1,0:T(8,128)(2,1)}, u32[]{:S(2)}, u32[]{:S(2)}) collective-permute-start(bf16[256,1024]{1,0:T(8,128)(2,1)} %collective-permute-done.refs_2_), channel_id=1, source_target_pairs={{0,8},{4,12},{8,0},{12,4},{16,24},{20,28},{24,16},{28,20},{1,9},{5... | collective-permute-start | bytes 1572872 | tf_op jit(solution)/shard_map/ppermute | solution.py:34
  63.4 13.5 %collective-permute-start.6 = (bf16[256,1024]{1,0:T(8,128)(2,1)}, bf16[256,1024]{1,0:T(8,128)(2,1)}, u32[]{:S(2)}, u32[]{:S(2)}) collective-permute-start(bf16[256,1024]{1,0:T(8,128)(2,1)} %collective-permute-done.5.refs_7_), channel_id=1, source_target_pairs={{0,4},{4,0},{8,12},{12,8},{16,20},{20,16},{24,28},{28,24},{1,5},{5... | collective-permute-start | bytes 1572872 | tf_op jit(solution)/shard_map/ppermute | solution.py:34
  71.9 15.2 %collective-permute-start.12 = (bf16[256,1024]{1,0:T(8,128)(2,1)S(1)}, bf16[256,1024]{1,0:T(8,128)(2,1)S(1)}, u32[]{:S(2)}, u32[]{:S(2)}) collective-permute-start(bf16[256,1024]{1,0:T(8,128)(2,1)S(1)} %collective-permute-done.11.refs_6_.refs_4_.refs_9_), channel_id=1, source_target_pairs={{0,1},{1,0},{2,3},{3,2},{4,5},{5,4},{6,7},{7,6},{8,9},{9,8},{10,11... | collective-permute-start | bytes 1572872 | tf_op jit(solution)/shard_map/ppermute | solution.py:34
  101.9 18.7 %all-to-all-start = ((bf16[8,256,128]{2,1,0:T(8,128)(2,1)}), bf16[8,256,128]{2,1,0:T(8,128)(2,1)S(1)}, u32[]{:S(2)}, u32[]{:S(2)}) async-start(bf16[8,256,128]{2,1,0:T(8,128)(2,1)} %bitcast.4), calls=%async_computation | async-start | bytes 1048576 | tf_op jit(solution)/shard_map/all_to_all | solution.py:109
  125.7 1.9 collective-permute-start.13
  145.8 3.8 collective-permute-start.14
  153.7 1.9 collective-permute-start.15
  164.4 4.1 collective-permute-start.16
  172.6 19.5 %all-to-all-start.1 = ((bf16[8,256,128]{2,1,0:T(8,128)(2,1)}), bf16[8,256,128]{2,1,0:T(8,128)(2,1)}, u32[]{:S(2)}, u32[]{:S(2)}) async-start(bf16[8,256,128]{2,1,0:T(8,128)(2,1)} %bitcast.45), calls=%async_computation.1 | async-start | bytes 1048576 | tf_op jit(solution)/shard_map/all_to_all | solution.py:109
  177.1 56.7 %collective-permute-start.18 = (bf16[1024,1024]{1,0:T(8,128)(2,1)}, bf16[1024,1024]{1,0:T(8,128)(2,1)}, u32[]{:S(2)}, u32[]{:S(2)}) collective-permute-start(bf16[1024,1024]{1,0:T(8,128)(2,1)} %copy-done.7), channel_id=1, source_target_pairs={{0,2},{1,3},{2,0},{3,1},{4,6},{5,7},{6,4},{7,5},{8,10},{9,11},{10,... | collective-permute-start | bytes 6291464 | tf_op jit(solution)/shard_map/ppermute | solution.py:34
  197.1 61.5 %collective-permute-start.19 = (bf16[1024,1024]{1,0:T(8,128)(2,1)}, bf16[1024,1024]{1,0:T(8,128)(2,1)}, u32[]{:S(2)}, u32[]{:S(2)}) collective-permute-start(bf16[1024,1024]{1,0:T(8,128)(2,1)} %reduce_gradient.2.refs_7_), channel_id=1, source_target_pairs={{0,4},{4,0},{8,12},{12,8},{16,20},{20,16},{24,28},{28,24},{1,5},{5... | collective-permute-start | bytes 6291464 | tf_op jit(solution)/shard_map/ppermute | solution.py:34
  198.6 29.2 %collective-permute-start.17 = (bf16[528,1024]{1,0:T(8,128)(2,1)}, bf16[528,1024]{1,0:T(8,128)(2,1)}, u32[]{:S(2)}, u32[]{:S(2)}) collective-permute-start(bf16[528,1024]{1,0:T(8,128)(2,1)} %get-tuple-element.121), channel_id=1, source_target_pairs={{0,1},{1,0},{2,3},{3,2},{4,5},{5,4},{6,7},{7,6},{8,9},{9,8},{10,11... | collective-permute-start | bytes 3244040 | tf_op jit(solution)/shard_map/ppermute | solution.py:34
  223.2 66.1 %all-to-all-start.2 = ((bf16[8,256,384]{2,1,0:T(8,128)(2,1)}), bf16[8,256,384]{2,1,0:T(8,128)(2,1)}, u32[]{:S(2)}, u32[]{:S(2)}) async-start(bf16[8,256,384]{2,1,0:T(8,128)(2,1)} %bitcast.43), calls=%async_computation.2 | async-start | bytes 3145728 | tf_op jit(solution)/shard_map/all_to_all | solution.py:109
  227.5 205.3 %all-gather.8.cloned.1.call-start = ((), (), s32[]{:S(2)}) async-start(), calls=%async_computation.5 | async-start | bytes 5308416 | tf_op jit(solution)/shard_map/all_gather | solution.py:1210
  236.7 29.8 %collective-permute-start.23 = (bf16[512,1024]{1,0:T(8,128)(2,1)}, bf16[512,1024]{1,0:T(8,128)(2,1)}, u32[]{:S(2)}, u32[]{:S(2)}) collective-permute-start(bf16[512,1024]{1,0:T(8,128)(2,1)} %add_parts.6.refs_3_), channel_id=1, source_target_pairs={{0,1},{1,0},{2,3},{3,2},{4,5},{5,4},{6,7},{7,6},{8,9},{9,8},{10,11... | collective-permute-start | bytes 3145736 | tf_op jit(solution)/shard_map/ppermute | solution.py:34
  237.2 29.3 %collective-permute-start.24 = (bf16[272,1024]{1,0:T(8,128)(2,1)}, bf16[272,1024]{1,0:T(8,128)(2,1)}, u32[]{:S(2)}, u32[]{:S(2)}) collective-permute-start(bf16[272,1024]{1,0:T(8,128)(2,1)} %get-tuple-element.129), channel_id=1, source_target_pairs={{0,2},{1,3},{2,0},{3,1},{4,6},{5,7},{6,4},{7,5},{8,10},{9,11},{10,... | collective-permute-start | bytes 1671176 | tf_op jit(solution)/shard_map/ppermute | solution.py:34
  242.3 20.8 %collective-permute-start.21 = (bf16[528,384]{1,0:T(8,128)(2,1)S(1)}, bf16[528,384]{1,0:T(8,128)(2,1)}, u32[]{:S(2)}, u32[]{:S(2)}) collective-permute-start(bf16[528,384]{1,0:T(8,128)(2,1)S(1)} %get-tuple-element.123.refs_4_), channel_id=1, source_target_pairs={{0,1},{1,0},{2,3},{3,2},{4,5},{5,4},{6,7},{7,6},{8,9},{9,8},{10,11... | collective-permute-start | bytes 1216520 | tf_op jit(solution)/shard_map/ppermute | solution.py:34
  261.4 27.8 %collective-permute-start.20 = (bf16[512,1024]{1,0:T(8,128)(2,1)}, bf16[512,1024]{1,0:T(8,128)(2,1)}, u32[]{:S(2)}, u32[]{:S(2)}) collective-permute-start(bf16[512,1024]{1,0:T(8,128)(2,1)} %get-tuple-element.125), channel_id=1, source_target_pairs={{0,2},{1,3},{2,0},{3,1},{4,6},{5,7},{6,4},{7,5},{8,10},{9,11},{10,... | collective-permute-start | bytes 3145736 | tf_op jit(solution)/shard_map/ppermute | solution.py:34
  271.6 26.7 %collective-permute-start.26 = (bf16[640,1024]{1,0:T(8,128)(2,1)}, bf16[640,1024]{1,0:T(8,128)(2,1)}, u32[]{:S(2)}, u32[]{:S(2)}) collective-permute-start(bf16[640,1024]{1,0:T(8,128)(2,1)} %get-tuple-element.133), channel_id=1, source_target_pairs={{0,4},{4,0},{8,12},{12,8},{16,20},{20,16},{24,28},{28,24},{1,5},{5... | collective-permute-start | bytes 3932168 | tf_op jit(solution)/shard_map/ppermute | solution.py:34
  271.6 16.6 %collective-permute-start.22 = (bf16[272,384]{1,0:T(8,128)(2,1)}, bf16[272,384]{1,0:T(8,128)(2,1)S(1)}, u32[]{:S(2)}, u32[]{:S(2)}) collective-permute-start(bf16[272,384]{1,0:T(8,128)(2,1)} %get-tuple-element.128.refs_6_), channel_id=1, source_target_pairs={{0,2},{1,3},{2,0},{3,1},{4,6},{5,7},{6,4},{7,5},{8,10},{9,11},{10,... | collective-permute-start | bytes 626696 | tf_op jit(solution)/shard_map/ppermute | solution.py:34
  291.9 16.3 %collective-permute-start.25 = (bf16[256,1024]{1,0:T(8,128)(2,1)}, bf16[256,1024]{1,0:T(8,128)(2,1)}, u32[]{:S(2)}, u32[]{:S(2)}) collective-permute-start(bf16[256,1024]{1,0:T(8,128)(2,1)} %get-tuple-element.132), channel_id=1, source_target_pairs={{0,8},{4,12},{8,0},{12,4},{16,24},{20,28},{24,16},{28,20},{1,9},{5... | collective-permute-start | bytes 1572872 | tf_op jit(solution)/shard_map/ppermute | solution.py:34
  302.1 15.6 %collective-permute-start.35 = (bf16[160,1024]{1,0:T(8,128)(2,1)}, bf16[160,1024]{1,0:T(8,128)(2,1)S(1)}, u32[]{:S(2)}, u32[]{:S(2)}) collective-permute-start(bf16[160,1024]{1,0:T(8,128)(2,1)} %get-tuple-element.137), channel_id=1, source_target_pairs={{0,8},{4,12},{8,0},{12,4},{16,24},{20,28},{24,16},{28,20},{1,9},{5... | collective-permute-start | bytes 983048 | tf_op jit(solution)/shard_map/ppermute | solution.py:34
  302.1 32.7 %collective-permute-start.36 = (bf16[160,1024]{1,0:T(8,128)(2,1)}, bf16[160,1024]{1,0:T(8,128)(2,1)S(1)}, u32[]{:S(2)}, u32[]{:S(2)}) collective-permute-start(bf16[160,1024]{1,0:T(8,128)(2,1)} %get-tuple-element.138), channel_id=1, source_target_pairs={{0,16},{4,20},{8,24},{12,28},{16,0},{20,4},{24,8},{28,12},{1,17},{... | collective-permute-start | bytes 983048 | tf_op jit(solution)/shard_map/ppermute | solution.py:34
  306.3 28.5 %collective-permute-start.37 = (bf16[160,1024]{1,0:T(8,128)(2,1)}, bf16[160,1024]{1,0:T(8,128)(2,1)S(1)}, u32[]{:S(2)}, u32[]{:S(2)}) collective-permute-start(bf16[160,1024]{1,0:T(8,128)(2,1)} %get-tuple-element.139), channel_id=1, source_target_pairs={{0,24},{4,28},{8,16},{12,20},{16,8},{20,12},{24,0},{28,4},{1,25},{... | collective-permute-start | bytes 983048 | tf_op jit(solution)/shard_map/ppermute | solution.py:34
  310.5 33.0 %collective-permute-start.34 = (bf16[128,1024]{1,0:T(8,128)(2,1)S(1)}, bf16[128,1024]{1,0:T(8,128)(2,1)S(1)}, u32[]{:S(2)}, u32[]{:S(2)}) collective-permute-start(bf16[128,1024]{1,0:T(8,128)(2,1)S(1)} %get-tuple-element.136), channel_id=1, source_target_pairs={{0,16},{4,20},{8,24},{12,28},{16,0},{20,4},{24,8},{28,12},{1,17},{... | collective-permute-start | bytes 786440 | tf_op jit(solution)/shard_map/ppermute | solution.py:34
  317.7 54.1 %copy-start.13 = (bf16[272,1024]{1,0:T(8,128)(2,1)S(1)}, bf16[272,1024]{1,0:T(8,128)(2,1)}, u32[]{:S(2)}) copy-start(bf16[272,1024]{1,0:T(8,128)(2,1)} %copy-done.11) | copy-start | bytes 1671172
  345.8 6.5 %collective-permute-start.28 = (bf16[272,384]{1,0:T(8,128)(2,1)S(1)}, bf16[272,384]{1,0:T(8,128)(2,1)S(1)}, u32[]{:S(2)}, u32[]{:S(2)}) collective-permute-start(bf16[272,384]{1,0:T(8,128)(2,1)S(1)} %sum_all.4.refs_3_.refs_1_), channel_id=1, source_target_pairs={{0,8},{4,12},{8,0},{12,4},{16,24},{20,28},{24,16},{28,20},{1,9},{5... | collective-permute-start | bytes 626696 | tf_op jit(solution)/shard_map/ppermute | solution.py:34
  345.9 23.9 %collective-permute-start.30 = (bf16[272,384]{1,0:T(8,128)(2,1)S(1)}, bf16[272,384]{1,0:T(8,128)(2,1)S(1)}, u32[]{:S(2)}, u32[]{:S(2)}) collective-permute-start(bf16[272,384]{1,0:T(8,128)(2,1)S(1)} %sum_all.4.refs_3_.refs_1_), channel_id=1, source_target_pairs={{0,16},{4,20},{8,24},{12,28},{16,0},{20,4},{24,8},{28,12},{1,17},{... | collective-permute-start | bytes 626696 | tf_op jit(solution)/shard_map/ppermute | solution.py:34
  348.8 22.0 %collective-permute-start.32 = (bf16[272,384]{1,0:T(8,128)(2,1)S(1)}, bf16[272,384]{1,0:T(8,128)(2,1)S(1)}, u32[]{:S(2)}, u32[]{:S(2)}) collective-permute-start(bf16[272,384]{1,0:T(8,128)(2,1)S(1)} %sum_all.4.refs_3_.refs_1_), channel_id=1, source_target_pairs={{0,24},{4,28},{8,16},{12,20},{16,8},{20,12},{24,0},{28,4},{1,25},{... | collective-permute-start | bytes 626696 | tf_op jit(solution)/shard_map/ppermute | solution.py:34
  350.2 48.0 %collective-permute-start.27 = (bf16[272,384]{1,0:T(8,128)(2,1)S(1)}, bf16[272,384]{1,0:T(8,128)(2,1)S(1)}, u32[]{:S(2)}, u32[]{:S(2)}) collective-permute-start(bf16[272,384]{1,0:T(8,128)(2,1)S(1)} %sum_all.4.refs_3_.refs_1_), channel_id=1, source_target_pairs={{0,4},{4,0},{8,12},{12,8},{16,20},{20,16},{24,28},{28,24},{1,5},{5... | collective-permute-start | bytes 626696 | tf_op jit(solution)/shard_map/ppermute | solution.py:34
  352.3 46.0 %collective-permute-start.29 = (bf16[272,384]{1,0:T(8,128)(2,1)S(1)}, bf16[272,384]{1,0:T(8,128)(2,1)S(1)}, u32[]{:S(2)}, u32[]{:S(2)}) collective-permute-start(bf16[272,384]{1,0:T(8,128)(2,1)S(1)} %collective-permute-done.28.refs_3_), channel_id=1, source_target_pairs={{0,4},{4,0},{8,12},{12,8},{16,20},{20,16},{24,28},{28,24},{1,5},{5... | collective-permute-start | bytes 626696 | tf_op jit(solution)/shard_map/ppermute | solution.py:34
  369.7 28.5 %collective-permute-start.31 = (bf16[272,384]{1,0:T(8,128)(2,1)S(1)}, bf16[272,384]{1,0:T(8,128)(2,1)S(1)}, u32[]{:S(2)}, u32[]{:S(2)}) collective-permute-start(bf16[272,384]{1,0:T(8,128)(2,1)S(1)} %collective-permute-done.30.refs_5_), channel_id=1, source_target_pairs={{0,4},{4,0},{8,12},{12,8},{16,20},{20,16},{24,28},{28,24},{1,5},{5... | collective-permute-start | bytes 626696 | tf_op jit(solution)/shard_map/ppermute | solution.py:34
  370.8 27.4 %collective-permute-start.33 = (bf16[272,384]{1,0:T(8,128)(2,1)S(1)}, bf16[272,384]{1,0:T(8,128)(2,1)S(1)}, u32[]{:S(2)}, u32[]{:S(2)}) collective-permute-start(bf16[272,384]{1,0:T(8,128)(2,1)S(1)} %collective-permute-done.32.refs_7_), channel_id=1, source_target_pairs={{0,4},{4,0},{8,12},{12,8},{16,20},{20,16},{24,28},{28,24},{1,5},{5... | collective-permute-start | bytes 626696 | tf_op jit(solution)/shard_map/ppermute | solution.py:34
  372.8 5.3 %collective-permute-start.38 = (bf16[16,1024]{1,0:T(8,128)(2,1)S(1)}, bf16[16,1024]{1,0:T(8,128)(2,1)S(1)}, u32[]{:S(2)}, u32[]{:S(2)}) collective-permute-start(bf16[16,1024]{1,0:T(8,128)(2,1)S(1)} %add_parts.9.refs_0_.refs_2_), channel_id=1, source_target_pairs={{0,4},{4,0},{8,12},{12,8},{16,20},{20,16},{24,28},{28,24},{1,5},{5... | collective-permute-start | bytes 98312 | tf_op jit(solution)/shard_map/ppermute | solution.py:34
  378.1 10.9 %collective-permute-start.39 = (bf16[16,1024]{1,0:T(8,128)(2,1)S(1)}, bf16[16,1024]{1,0:T(8,128)(2,1)S(1)}, u32[]{:S(2)}, u32[]{:S(2)}) collective-permute-start(bf16[16,1024]{1,0:T(8,128)(2,1)S(1)} %sum_all.5.refs_0_.refs_2_), channel_id=1, source_target_pairs={{0,8},{4,12},{8,0},{12,4},{16,24},{20,28},{24,16},{28,20},{1,9},{5... | collective-permute-start | bytes 98312 | tf_op jit(solution)/shard_map/ppermute | solution.py:34
  389.1 9.1 %collective-permute-start.40 = (bf16[16,1024]{1,0:T(8,128)(2,1)S(1)}, bf16[16,1024]{1,0:T(8,128)(2,1)S(1)}, u32[]{:S(2)}, u32[]{:S(2)}) collective-permute-start(bf16[16,1024]{1,0:T(8,128)(2,1)S(1)} %sum_all.6.refs_0_.refs_2_), channel_id=1, source_target_pairs={{0,16},{4,20},{8,24},{12,28},{16,0},{20,4},{24,8},{28,12},{1,17},{... | collective-permute-start | bytes 98312 | tf_op jit(solution)/shard_map/ppermute | solution.py:34
  (79 other events, 641.2 us)
Sparse Core Ops, SparseCore 0:
  14.7 121.7 all-gather.3
  138.0 45.0 all-gather.5
  345.9 86.8 all-gather.7
